TPU v7x, 32 devices: a whole 2x2x4 slice. The times are simulated.
32 devices in a mesh: groups: 2 (over x), chan: 8 (over z, y), seq: 2 (over core).
Axes of the slice: x: 2, y: 2, z: 4, core: 2. Of those that a mesh axis runs over, the one named last changes fastest.
Arguments:
- tokens: bfloat16 [2048, 8192], P(('groups', 'seq'), 'chan'), parts along dimension 0, may hold values from -42 to 42
- norm_gain: float32 [8192], replicated, may hold values from 0.1 to 1.9
- in_weight: bfloat16 [3, 8192, 8192], P(None, None, 'chan'), may hold values from -0.0625 to 0.0625
- short_weight: float32 [3, 7, 8192], P(None, None, 'chan'), may hold values from -2 to 2
- log_decay: float32 [16, 8192], P(None, 'chan'), may hold values from -0.034 to 0
- residue: float32 [16, 8192], P(None, 'chan'), may hold values from -0.15625 to 0.15625
- skip: float32 [8192], P('chan'), may hold values from 0.1 to 1.9
- out_weight: bfloat16 [8192, 8192], P('chan'), may hold values from -0.09375 to 0.09375
Outputs:
- mixed: bfloat16 [2048, 8192], P(('groups', 'seq'), 'chan'), parts along dimension 0
There are 2 independent parts, one for each index of `groups`. A program takes and returns all parts, laid end to end along the dimension named above; an argument that names none is the same for every part. Nothing has to cross between parts.
All inputs are finite; a program needn't handle non-finite values.
Results may differ from a plain program's by a relative error of at most 0.0067.
Values may be sent and summed in bfloat16 or wider, within the bound.
No kernel may reach another device: no remote copies, remote signals or barrier semaphores. Data moves between devices by JAX's collectives and lax.ppermute only.
A program may use at most 448 MiB of HBM per device.

v0:
```python
import functools

import jax
import jax.numpy as jnp
from jax import lax
from jax.experimental import pallas as pl
from jax.experimental.pallas import tpu as pltpu
from jax.sharding import PartitionSpec as P

EPSILON = 1e-06
LANES = 128
KEEP = 8
VMEM_LIMIT = 48 * 1024 * 1024


def from_behind(block, axis, distance):
    count = lax.axis_size(axis)
    route = [(i - distance, i) for i in range(count) if i - distance >= 0]
    return lax.ppermute(block, axis, route)


def tree_sum(terms):
    while len(terms) > 1:
        pairs = [terms[i] + terms[i + 1] for i in range(0, len(terms) - 1, 2)]
        terms = pairs + terms[len(pairs) * 2 :]
    return terms[0]


def accumulate_kernel(depths, pairs, width, has_acc, has_sq, part_count, place_ref, *refs):
    def take(count):
        nonlocal refs
        taken, refs = refs[:count], refs[count:]
        return taken

    chunk_refs = take(len(depths) + sum(pairs))
    gain_refs, w_refs = take(len(depths)), take(len(depths))
    held_refs, held_sq_refs = take(int(has_acc)), take(int(has_sq))
    part_refs = take(part_count or 0)
    acc_ref, sq_ref = take(2)
    scaled_ref = refs[-1]
    feat, col = pl.program_id(0), pl.program_id(1)
    last = part_count is not None

    @pl.when((feat == 0) & (col == 0))
    def _():
        square = held_sq_refs[0][...] if has_sq else None
        start = at = 0
        for j, depth in enumerate(depths):
            x = chunk_refs[at][...]
            at += 1
            if pairs[j]:
                x = jnp.where(place_ref[len(depths)] == 1, x, chunk_refs[at][...])
                at += 1
            x = x.astype(jnp.float32)
            parts = [x[:, g : g + LANES] * x[:, g : g + LANES] for g in range(0, depth, LANES)]
            part = tree_sum(parts)
            square = part if square is None else square + part
            scaled_ref[:, start : start + depth] = (x * gain_refs[j][0]).astype(jnp.bfloat16)
            start += depth
        if last:
            total = jnp.sum(square, axis=1, keepdims=True)
            square = jnp.broadcast_to(lax.rsqrt(total / width + EPSILON), square.shape)
        sq_ref[...] = square

    start, part = 0, None
    for j, depth in enumerate(depths):
        one = jnp.dot(scaled_ref[:, start : start + depth], w_refs[j][0], preferred_element_type=jnp.float32)
        part = one if part is None else part + one
        start += depth
    acc_ref[0] = held_refs[0][0] + part if has_acc else part
    if last:
        rim_ref = refs[0]
        keep = rim_ref.shape[1]
        rows = acc_ref.shape[1]
        rim = acc_ref[0, rows - keep :, :]
        for ref in part_refs:
            rim = rim + ref[0]
        rim_ref[0] = (rim * sq_ref[rows - keep :, :1]).astype(jnp.bfloat16).astype(jnp.float32)


def accumulate(chunks, places, gain, in_weight, acc=None, square=None, parts=None, use_first=None):
    pairs = [isinstance(c, tuple) for c in chunks]
    arrays = [a for c in chunks for a in (c if isinstance(c, tuple) else (c,))]
    depths = [(c[0] if isinstance(c, tuple) else c).shape[1] for c in chunks]
    rows = arrays[0].shape[0]
    width, chans = in_weight.shape[1:]
    tile = min(512, chans)
    acc_spec = pl.BlockSpec((1, rows, tile), lambda i, c, p: (i, 0, c))
    sq_spec = pl.BlockSpec((rows, LANES), lambda i, c, p: (0, 0))
    in_specs = [pl.BlockSpec(a.shape, lambda i, c, p: (0, 0)) for a in arrays]
    in_specs += [pl.BlockSpec((1, 1, d), lambda i, c, p, j=j: (p[j], 0, 0)) for j, d in enumerate(depths)]
    in_specs += [pl.BlockSpec((1, d, tile), lambda i, c, p, j=j: (i, p[j], c)) for j, d in enumerate(depths)]
    out_specs = [acc_spec, sq_spec]
    out_shape = [
        jax.ShapeDtypeStruct((3, rows, chans), jnp.float32),
        jax.ShapeDtypeStruct((rows, LANES), jnp.float32),
    ]
    extra, aliases = [], {}
    before = 1 + len(arrays) + 2 * len(depths)
    for n, (held, spec) in enumerate(((acc, acc_spec), (square, sq_spec))):
        if held is not None:
            aliases[before + len(extra)] = n
            extra.append(held)
            in_specs.append(spec)
    if parts is not None:
        extra += parts
        in_specs += [pl.BlockSpec((1, KEEP, tile), lambda i, c, p: (i, rows // KEEP - 1, c))] * len(parts)
        out_specs.append(pl.BlockSpec((1, KEEP, tile), lambda i, c, p: (i, 0, c)))
        out_shape.append(jax.ShapeDtypeStruct((3, KEEP, chans), jnp.float32))
    scalars = list(places) + ([] if use_first is None else [use_first])
    part_count = None if parts is None else len(parts)
    return pl.pallas_call(
        functools.partial(
            accumulate_kernel, depths, pairs, width, acc is not None, square is not None, part_count
        ),
        grid_spec=pltpu.PrefetchScalarGridSpec(
            num_scalar_prefetch=1,
            grid=(3, chans // tile),
            in_specs=in_specs,
            out_specs=out_specs,
            scratch_shapes=[pltpu.VMEM((rows, sum(depths)), jnp.bfloat16)],
        ),
        out_shape=out_shape,
        input_output_aliases=aliases,
        compiler_params=pltpu.CompilerParams(vmem_limit_bytes=VMEM_LIMIT),
        cost_estimate=pl.CostEstimate(
            flops=rows * sum(depths) * chans,
            bytes_accessed=6 * sum(depths) * chans,
            transcendentals=0,
        ),
        name="accumulate",
    )(
        jnp.stack([jnp.asarray(n, jnp.int32) for n in scalars]),
        *arrays,
        *[gain.reshape(-1, 1, d) for d in depths],
        *[in_weight] * len(depths),
        *extra,
    )


def pieces_kernel(count, place_ref, gated_ref, w_ref, *refs):
    outs = refs[-count:]
    total = jnp.dot(gated_ref[...], w_ref[...], preferred_element_type=jnp.float32)
    for j in range(count):

        @pl.when(pl.program_id(0) == j)
        def _():
            outs[j][...] = total.astype(outs[j].dtype)


def pieces(out_weight, gated, wanted, *earlier):
    rows, chans = gated.shape
    count = len(wanted)
    out = pl.pallas_call(
        functools.partial(pieces_kernel, count),
        grid_spec=pltpu.PrefetchScalarGridSpec(
            num_scalar_prefetch=1,
            grid=(count,),
            in_specs=[
                pl.BlockSpec((rows, chans), lambda t, p: (0, 0)),
                pl.BlockSpec((chans, chans), lambda t, p: (0, p[t])),
            ]
            + [pl.BlockSpec(memory_space=pl.ANY)] * len(earlier),
            out_specs=[pl.BlockSpec((rows, chans), lambda t, p: (0, 0))] * count,
        ),
        out_shape=[jax.ShapeDtypeStruct((rows, chans), dtype) for place, dtype in wanted],
        compiler_params=pltpu.CompilerParams(vmem_limit_bytes=VMEM_LIMIT),
        cost_estimate=pl.CostEstimate(flops=count * 1000000, bytes_accessed=count * 100000, transcendentals=0),
        name="pieces",
    )(jnp.stack([place.astype(jnp.int32) for place, dtype in wanted]), gated, out_weight, *earlier)
    return list(out)


def finish_kernel(*refs):
    out_ref = refs[-1]
    count = (len(refs) - 1) // 2
    step, per_half = pl.program_id(0), pl.num_programs(0) // 2

    for h in range(2):

        @pl.when((step >= h * per_half) & (step < (h + 1) * per_half))
        def _():
            total = refs[h * count][...].astype(jnp.float32)
            for ref in refs[h * count + 1 : (h + 1) * count]:
                total = total + ref[...].astype(jnp.float32)
            out_ref[...] = total.astype(jnp.bfloat16)


def finish(upper, lower):
    rows, chans = upper[0].shape
    blk = min(128, rows)
    per_half = rows // blk
    spec = lambda h: pl.BlockSpec((blk, chans), lambda t: (jnp.clip(t - h * per_half, 0, per_half - 1), 0))
    return pl.pallas_call(
        finish_kernel,
        grid=(2 * per_half,),
        in_specs=[spec(0)] * len(upper) + [spec(1)] * len(lower),
        out_specs=pl.BlockSpec((blk, chans), lambda t: (t, 0)),
        out_shape=jax.ShapeDtypeStruct((2 * rows, chans), jnp.bfloat16),
        compiler_params=pltpu.CompilerParams(vmem_limit_bytes=VMEM_LIMIT),
        name="finish",
    )(*upper, *lower)


def along_line(block, pairs):
    return lax.ppermute(block, "chan", [(2 * a + y, 2 * b + y) for a, b in pairs for y in (0, 1)])


def after(block, *earlier):
    return lax.optimization_barrier((block,) + earlier)[0]


def across(block, *earlier):
    count = lax.axis_size("chan")
    if earlier:
        block = after(block, *earlier)
    return lax.ppermute(block, "chan", [(c, c ^ 1) for c in range(count)])


def total(*terms):
    return functools.reduce(lambda a, b: a + b, [t.astype(jnp.float32) for t in terms])


PAIRS = [(0, 1), (1, 0), (2, 3), (3, 2)]
MIDDLE = [(1, 2), (2, 1)]
OUTWARD = [(1, 0), (2, 3)]
INWARD = [(0, 1), (3, 2)]


def gather_and_project(tokens, gain, in_weight, params):
    me = lax.axis_index("chan")
    half = tokens.shape[1] // 2
    at_end = (me < 2) | (me >= 6)
    own_over = across(tokens)
    next_one = along_line(tokens, PAIRS)
    middle = along_line(tokens, MIDDLE)
    acc, square = accumulate([tokens], [me], gain, in_weight)
    next_over = across(next_one, own_over, square)
    second_out = along_line(after(middle, square), OUTWARD)
    second_mid = along_line(after(next_one, square), MIDDLE)
    square, *params = lax.optimization_barrier((square, *params))
    acc, square = accumulate([own_over, next_one], [me ^ 1, me ^ 2], gain, in_weight, acc, square)
    second = jnp.where(at_end, second_out, second_mid)
    second_over = across(second, next_over, square)
    third_out = along_line(after(second_mid, second_out, square), OUTWARD)
    rest_mid = along_line(after(own_over[:, half:], second_mid, square), MIDDLE)
    acc, square = accumulate([next_over, second], [me ^ 3, me ^ 4], gain, in_weight, acc, square)
    third_over = across(jnp.where(at_end, third_out[:, :half], middle[:, :half]), second_over, square)
    rest_out = along_line(after(second_over[:, half:], square), OUTWARD)
    third = (third_out, middle)
    more, square = accumulate(
        [second_over, third], [me ^ 5, me ^ 6], gain, in_weight, None, square, use_first=at_end
    )
    place = (me ^ 7) * 2
    rest, inv_rms, rim = accumulate(
        [third_over, (rest_out, rest_mid)],
        [place, place + 1],
        gain,
        in_weight,
        None,
        square,
        [acc, more],
        use_first=at_end,
    )
    return [acc, more, rest], inv_rms, rim, params


def project_and_reduce(upper, lower, out_weight, tokens):
    me = lax.axis_index("chan")
    half = tokens.shape[0] // 2
    send = lambda k: (me ^ (2 * k + 1), jnp.bfloat16)
    keep = lambda k: (me ^ (2 * k), jnp.float32)
    narrow = lambda a: a.astype(jnp.bfloat16)
    make = functools.partial(pieces, out_weight)
    both = (0, 1)

    third_send_0 = make(upper, [send(3)])[0]
    third_over = across(third_send_0)
    lower = lower(third_send_0)
    third_send_1 = make(lower, [send(3)])[0]
    rest_in = along_line(third_send_1, INWARD)
    rest_mid = along_line(third_send_1, MIDDLE)
    second_send_0, third_keep_0 = make(upper, [send(2), keep(3)], third_send_1)
    second_send_1, third_1 = make(lower, [send(2), (keep(3)[0], jnp.bfloat16)], second_send_0)
    third = [narrow(total(third_keep_0, third_over)), third_1]
    third_in = [along_line(third[h], INWARD) for h in both]
    second_send = [second_send_0, narrow(total(second_send_1, rest_in))]
    second_over = [across(second_send[h], third_over) for h in both]
    halves = (upper, lower)
    later = [make(halves[h], [keep(2), send(1)], (third_over, second_send[1])[h]) for h in both]
    second = [narrow(total(later[h][0], second_over[h], third_in[h])) for h in both]
    second_in = [along_line(second[h], INWARD) for h in both]
    second_mid = [along_line(second[h], MIDDLE) for h in both]
    next_over = [across(later[h][1], second_over[h]) for h in both]
    later = [make(halves[h], [keep(1), send(0)], third_over) for h in both]
    own_send = [later[0][1], narrow(total(later[1][1], rest_mid))]
    next_one = [narrow(total(later[h][0], next_over[h], second_mid[h])) for h in both]
    next_in = [along_line(next_one[h], PAIRS) for h in both]
    middle_in = [along_line(narrow(total(third[h], second_in[h])), MIDDLE) for h in both]
    own_over = [across(own_send[h], next_over[h]) for h in both]
    own_keep = [make(halves[h], [keep(0)], second_over[0])[0] for h in both]
    base = [total(own_keep[h], tokens[h * half : (h + 1) * half]) for h in both]
    return finish(*[[base[h], own_over[h], next_in[h], middle_in[h]] for h in both])


def convolve_kernel(part_count, *refs):
    part_refs, refs = refs[:part_count], refs[part_count:]
    rms_ref, rim_ref, taps_ref, decay_ref, q_ref, prod_ref, end_ref, win_ref, state_ref = refs
    step = pl.program_id(0)
    rows = q_ref.shape[0]
    tap_count, groups = taps_ref.shape[1:3]
    poles = decay_ref.shape[0]
    keep = rim_ref.shape[1]
    unroll = 8

    @pl.when(step == 0)
    def _():
        for g in range(groups):
            for i in range(3):
                win_ref[i, pl.ds(g, keep, stride=groups), :] = rim_ref[i, :, g * LANES : (g + 1) * LANES]
        state_ref[...] = jnp.zeros_like(state_ref)

    inv_rms = rms_ref[:, :1]
    for i in range(3):
        for g in range(groups):
            cols = tree_sum([ref[i, :, g * LANES : (g + 1) * LANES] for ref in part_refs]) * inv_rms
            cols = cols.astype(jnp.bfloat16).astype(jnp.float32)
            win_ref[i, pl.ds(keep * groups + g, rows, stride=groups), :] = cols
    decay = [jnp.exp(decay_ref[n]) for n in range(poles)]

    def row_of(i, t):
        return win_ref[i, pl.ds(pl.multiple_of(t * groups, groups), groups), :]

    def advance(blk, state):
        state = list(state)
        first = blk * unroll
        conv = []
        for i in range(3):
            taps = [taps_ref[i, j] for j in range(tap_count)]
            held = [row_of(i, first + keep - (tap_count - 1) + r) for r in range(unroll + tap_count - 1)]
            conv.append(
                [
                    functools.reduce(
                        lambda a, b: a + b, [taps[j] * held[r + tap_count - 1 - j] for j in range(tap_count)]
                    )
                    for r in range(unroll)
                ]
            )
        for r in range(unroll):
            q_ref[first + r] = conv[0][r]
            product = conv[1][r] * conv[2][r]
            prod_ref[first + r] = product
            for n in range(poles):
                state[n] = decay[n] * state[n] + product
        return tuple(state)

    state = lax.fori_loop(0, rows // unroll, advance, tuple(state_ref[n] for n in range(poles)))
    for n in range(poles):
        state_ref[n] = state[n]
    win_ref[:, : keep * groups] = win_ref[:, rows * groups :]

    @pl.when(step == pl.num_programs(0) - 1)
    def _():
        for n in range(poles):
            end_ref[n] = state[n]


def convolve(parts, inv_rms, rim, taps, log_decay):
    rows, chans = parts[0].shape[1:]
    groups = chans // LANES
    tap_count, poles = taps.shape[1], log_decay.shape[0]
    keep = rim.shape[1]
    blk = min(128, rows)
    whole = lambda *shape: pl.BlockSpec(shape, lambda t: (0,) * len(shape))
    row_spec = pl.BlockSpec((blk, groups, LANES), lambda t: (t, 0, 0))
    return pl.pallas_call(
        functools.partial(convolve_kernel, len(parts)),
        grid=(rows // blk,),
        in_specs=[pl.BlockSpec((3, blk, chans), lambda t: (0, t, 0))] * len(parts)
        + [
            pl.BlockSpec((blk, LANES), lambda t: (t, 0)),
            whole(3, keep, chans),
            whole(3, tap_count, groups, LANES),
            whole(poles, groups, LANES),
        ],
        out_specs=[row_spec, row_spec, whole(poles, groups, LANES)],
        out_shape=[
            jax.ShapeDtypeStruct((rows, groups, LANES), jnp.float32),
            jax.ShapeDtypeStruct((rows, groups, LANES), jnp.float32),
            jax.ShapeDtypeStruct((poles, groups, LANES), jnp.float32),
        ],
        scratch_shapes=[
            pltpu.VMEM((3, (keep + blk) * groups, LANES), jnp.float32),
            pltpu.VMEM((poles, groups, LANES), jnp.float32),
        ],
        compiler_params=pltpu.CompilerParams(vmem_limit_bytes=VMEM_LIMIT),
        cost_estimate=pl.CostEstimate(
            flops=110 * rows * groups * LANES, bytes_accessed=20 * rows * groups * LANES, transcendentals=0
        ),
        name="convolve",
    )(*parts, inv_rms, rim, taps, log_decay)


def respond_kernel(q_ref, prod_ref, enter_ref, decay_ref, res_ref, skip_ref, *refs):
    out_ref, end_ref, state_ref, row_ref = refs[-4:]
    step = pl.program_id(0)
    rows, groups = q_ref.shape[:2]
    poles = decay_ref.shape[0]
    unroll = 8

    @pl.when(step == 0)
    def _():
        state_ref[...] = enter_ref[...]

    decay = [jnp.exp(decay_ref[n]) for n in range(poles)]
    res = [res_ref[n] for n in range(poles)]
    skip = skip_ref[0]

    def recur(blk, state):
        state = list(state)
        for r in range(unroll):
            t = blk * unroll + r
            product = prod_ref[t]
            sums = [skip * product]
            for n in range(poles):
                state[n] = decay[n] * state[n] + product
                term = res[n] * state[n]
                if n < 3:
                    sums.append(term)
                else:
                    sums[n % 4] = sums[n % 4] + term
            row_ref[pl.ds(pl.multiple_of(t * groups, groups), groups), :] = q_ref[t] * tree_sum(sums)
        return tuple(state)

    state = lax.fori_loop(0, rows // unroll, recur, tuple(state_ref[n] for n in range(poles)))
    for n in range(poles):
        state_ref[n] = state[n]
        end_ref[n] = state[n]
    for g in range(groups):
        out_ref[:, g * LANES : (g + 1) * LANES] = row_ref[pl.ds(g, rows, stride=groups), :].astype(jnp.bfloat16)


def respond(query, product, enter, log_decay, residue, skip, start, rows, *earlier):
    groups = query.shape[1]
    poles = log_decay.shape[0]
    blk = min(128, rows)
    whole = lambda *shape: pl.BlockSpec(shape, lambda t: (0,) * len(shape))
    row_spec = pl.BlockSpec((blk, groups, LANES), lambda t: (t + start // blk, 0, 0))
    return pl.pallas_call(
        respond_kernel,
        grid=(rows // blk,),
        in_specs=[row_spec, row_spec]
        + [whole(poles, groups, LANES)] * 3
        + [whole(1, groups, LANES)]
        + [pl.BlockSpec(memory_space=pl.ANY)] * len(earlier),
        out_specs=[pl.BlockSpec((blk, groups * LANES), lambda t: (t, 0)), whole(poles, groups, LANES)],
        out_shape=[
            jax.ShapeDtypeStruct((rows, groups * LANES), jnp.bfloat16),
            jax.ShapeDtypeStruct((poles, groups, LANES), jnp.float32),
        ],
        scratch_shapes=[
            pltpu.VMEM((poles, groups, LANES), jnp.float32),
            pltpu.VMEM((blk * groups, LANES), jnp.float32),
        ],
        compiler_params=pltpu.CompilerParams(vmem_limit_bytes=VMEM_LIMIT),
        cost_estimate=pl.CostEstimate(
            flops=70 * rows * groups * LANES, bytes_accessed=80 * rows * groups * LANES, transcendentals=0
        ),
        name="respond",
    )(query, product, enter, log_decay, residue, skip, *earlier)


def per_device(tokens, norm_gain, in_weight, short_weight, log_decay, residue, skip, out_weight):
    rows, chans = tokens.shape
    groups = chans // LANES
    by_lane = lambda a: a.reshape(a.shape[:-1] + (groups, LANES))
    taps, log_decay, residue = by_lane(short_weight), by_lane(log_decay), by_lane(residue)
    skip = by_lane(skip[None, :])

    paired_line = lax.axis_size("chan") == 8
    if paired_line:
        params = (taps, log_decay, residue, skip)
        parts, inv_rms, rim, params = gather_and_project(tokens, norm_gain, in_weight, params)
        taps, log_decay, residue, skip = params
    else:
        gathered = lax.all_gather(tokens, "chan", axis=1, tiled=True)
        depth = min(1024, gathered.shape[1])
        chunks = [gathered[:, k : k + depth] for k in range(0, gathered.shape[1], depth)]
        acc = square = None
        for k, chunk in enumerate(chunks[:-1]):
            acc, square = accumulate([chunk], [k], norm_gain, in_weight, acc, square)
        acc, inv_rms, rim = accumulate(chunks[-1:], [len(chunks) - 1], norm_gain, in_weight, acc, square, [])
        parts = [acc]
    rim = from_behind(rim, "seq", 1)
    query, product, end = convolve(parts, inv_rms, rim, taps, log_decay)
    shard_decay = jnp.exp(rows * log_decay)
    state, passing = jnp.zeros_like(end), end
    for _ in range(lax.axis_size("seq") - 1):
        passing = from_behind(passing, "seq", 1)
        state = state + passing
        passing = passing * shard_decay
    filt = (log_decay, residue, skip)
    if paired_line:
        half = rows // 2
        upper, state = respond(query, product, state, *filt, 0, half)
        lower = lambda *earlier: respond(query, product, state, *filt, half, half, *earlier)[0]
        return project_and_reduce(upper, lower, out_weight, tokens)
    gated = respond(query, product, state, *filt, 0, rows)[0]
    partial = jnp.dot(gated, out_weight, preferred_element_type=jnp.float32)
    branch = lax.psum_scatter(partial.astype(jnp.bfloat16), "chan", scatter_dimension=1, tiled=True)
    return (tokens.astype(jnp.float32) + branch.astype(jnp.float32)).astype(jnp.bfloat16)


def solution(mesh):
    return jax.shard_map(
        per_device,
        mesh=mesh,
        in_specs=(
            P(("groups", "seq"), "chan"),
            P(),
            P(None, None, "chan"),
            P(None, None, "chan"),
            P(None, "chan"),
            P(None, "chan"),
            P("chan"),
            P("chan", None),
        ),
        out_specs=P(("groups", "seq"), "chan"),
        check_vma=False,
    )
```

profile of v0, /device:TPU:0, one launch (start us, length us, event | category | flops | bytes accessed | tf_op | source)
XLA Modules:
  0.0 230.2 jit_solution(3115290302156073858)
XLA Ops:
  0.0 3.0 %collective-permute-start = (bf16[512,1024]{1,0:T(8,128)(2,1)}, bf16[512,1024]{1,0:T(8,128)(2,1)}, u32[]{:S(2)}, u32[]{:S(2)}) collective-permute-start(bf16[512,1024]{1,0:T(8,128)(2,1)} %refs_0_.1), channel_id=1, source_target_pairs={{0,4},{2,6},{4,0},{6,2},{8,12},{10,14},{12,8},{14,10},{1,5},{3,7},... | collective-permute-start | bytes 3145736 | tf_op jit(solution)/shard_map/ppermute | solution.py:206
  7.4 8.9 %accumulate.5 = (f32[3,512,1024]{2,1,0:T(8,128)}, f32[512,128]{1,0:T(8,128)S(1)}) custom-call(s32[1]{0:T(128)} %bitcast.place_ref, bf16[512,1024]{1,0:T(8,128)(2,1)S(1)} %copy-done, f32[8,1,1024]{2,1,0:T(1,128)S(1)} %bitcast.18, bf16[3,8192,1024]{2,1,0:T(8,128)(2,1)} %refs_6_.3), custom_call_target="tpu_custom_call" | custom-call | flops 536870912 | bytes 6291456 | tf_op jit(solution)/shard_map/accumulate/pallas_call | solution.py:112
  16.2 10.3 %collective-permute-done.refs_1_ = bf16[512,1024]{1,0:T(8,128)(2,1)} collective-permute-done((bf16[512,1024]{1,0:T(8,128)(2,1)}, bf16[512,1024]{1,0:T(8,128)(2,1)}, u32[]{:S(2)}, u32[]{:S(2)}) %collective-permute-start) | collective-permute-done | bytes 1048608 | tf_op jit(solution)/shard_map/ppermute | solution.py:206
  32.5 14.8 %accumulate.6 = (f32[3,512,1024]{2,1,0:T(8,128)}, f32[512,128]{1,0:T(8,128)S(1)}) custom-call(s32[2]{0:T(128)S(1)} %pad_add_fusion.1.place_ref, bf16[512,1024]{1,0:T(8,128)(2,1)S(1)} %collective-permute-done.1.refs_0_, bf16[512,1024]{1,0:T(8,128)(2,1)} %collective-permute-done.refs_1_, ...), custom_call_target="tpu_custom_call", output_to_operand_aliasing={{0}: (7, {}), {1}: (8, {})} | custom-call | flops 1073741824 | bytes 12582912 | tf_op jit(solution)/shard_map/accumulate/pallas_call | solution.py:112
  47.3 7.5 %collective-permute-done.4 = bf16[512,1024]{1,0:T(8,128)(2,1)} collective-permute-done((bf16[512,1024]{1,0:T(8,128)(2,1)S(1)}, bf16[512,1024]{1,0:T(8,128)(2,1)}, u32[]{:S(2)}, u32[]{:S(2)}) %collective-permute-start.4) | collective-permute-done | bytes 1048608 | tf_op jit(solution)/shard_map/ppermute | solution.py:206
  60.7 14.8 %accumulate.7 = (f32[3,512,1024]{2,1,0:T(8,128)}, f32[512,128]{1,0:T(8,128)S(1)}) custom-call(s32[2]{0:T(128)S(1)} %pad_add_fusion.place_ref, bf16[512,1024]{1,0:T(8,128)(2,1)} %collective-permute-done.2.refs_0_, bf16[512,1024]{1,0:T(8,128)(2,1)S(1)} %broadcast_select_fusion.refs_1_, ...), custom_call_target="tpu_custom_call", output_to_operand_aliasing={{0}: (7, {}), {1}: (8, {})} | custom-call | flops 1073741824 | bytes 12582912 | tf_op jit(solution)/shard_map/accumulate/pallas_call | solution.py:112
  75.5 4.2 %collective-permute-done.6.refs_0_ = bf16[512,1024]{1,0:T(8,128)(2,1)} collective-permute-done((bf16[512,1024]{1,0:T(8,128)(2,1)S(1)}, bf16[512,1024]{1,0:T(8,128)(2,1)}, u32[]{:S(2)}, u32[]{:S(2)}) %collective-permute-start.6) | collective-permute-done | bytes 1048608 | tf_op jit(solution)/shard_map/ppermute | solution.py:217
  82.1 3.6 %collective-permute-done.7.refs_1_ = bf16[512,1024]{1,0:T(8,128)(2,1)} collective-permute-done((bf16[512,1024]{1,0:T(8,128)(2,1)}, bf16[512,1024]{1,0:T(8,128)(2,1)}, u32[]{:S(2)}, u32[]{:S(2)}) %collective-permute-start.7) | collective-permute-done | bytes 1048608 | tf_op jit(solution)/shard_map/ppermute | solution.py:206
  87.8 13.7 %accumulate.8 = (f32[3,512,1024]{2,1,0:T(8,128)}, f32[512,128]{1,0:T(8,128)S(1)}) custom-call(s32[3]{0:T(128)S(1)} %add_add_fusion.place_ref, bf16[512,1024]{1,0:T(8,128)(2,1)} %collective-permute-done.6.refs_0_, bf16[512,1024]{1,0:T(8,128)(2,1)} %collective-permute-done.7.refs_1_, ...), custom_call_target="tpu_custom_call", output_to_operand_aliasing={{1}: (8, {})} | custom-call | flops 1073741824 | bytes 12582912 | tf_op jit(solution)/shard_map/accumulate/pallas_call | solution.py:112
  101.6 9.4 %accumulate.9 = (f32[3,512,1024]{2,1,0:T(8,128)}, f32[512,128]{1,0:T(8,128)S(1)}, f32[3,8,1024]{2,1,0:T(8,128)S(1)}) custom-call(s32[3]{0:T(128)S(1)} %add_add_fusion.1.place_ref, bf16[512,512]{1,0:T(8,128)(2,1)S(1)} %collective-permute-done.8.refs_0_, bf16[512,512]{1,0:T(8,128)(2,1)S(1)} %collective-permute-done.9.refs_1_, ...), custom_call_target="tpu_custom_call", output_to_operand_aliasing={{1}: (8, {})} | custom-call | flops 536870912 | bytes 6291456 | tf_op jit(solution)/shard_map/accumulate/pallas_call | solution.py:112
  113.2 11.3 %convolve.1 = (f32[512,8,128]{2,1,0:T(8,128)S(1)}, f32[512,8,128]{2,1,0:T(8,128)S(1)}, f32[16,8,128]{2,1,0:T(8,128)S(1)}) custom-call(f32[3,512,1024]{2,1,0:T(8,128)} %get-tuple-element.61.refs_8_.refs_0_, f32[3,512,1024]{2,1,0:T(8,128)} %get-tuple-element.65.refs_9_.refs_1_, f32[3,512,1024]{2,1,0:T(8,128)} %get-tuple-element.70.refs_2_, ...), custom_call_target="tpu_custom_call" | custom-call | flops 57671680 | bytes 10485760 | tf_op jit(solution)/shard_map/convolve/pallas_call | solution.py:376
  127.7 2.7 %respond.2 = (bf16[256,1024]{1,0:T(8,128)(2,1)S(1)}, f32[16,8,128]{2,1,0:T(8,128)S(1)}) custom-call(f32[512,8,128]{2,1,0:T(8,128)S(1)} %get-tuple-element.75.q_ref, f32[512,8,128]{2,1,0:T(8,128)S(1)} %get-tuple-element.76.prod_ref, f32[16,8,128]{2,1,0:T(8,128)S(1)} %collective-permute-done.12.enter_ref, f32[16,8,128]{2,1,0:T(8,128)S(1)} %bitcast.28, ...), custom_call_target="tpu_custom_call" | custom-call | flops 18350080 | bytes 20971520 | tf_op jit(solution)/shard_map/respond/pallas_call | solution.py:449
  130.5 2.3 pieces.10.refs_0_
  132.8 3.3 %respond.3 = (bf16[256,1024]{1,0:T(8,128)(2,1)S(1)}, f32[16,8,128]{2,1,0:T(8,128)}) custom-call(f32[512,8,128]{2,1,0:T(8,128)S(1)} %get-tuple-element.75.q_ref, f32[512,8,128]{2,1,0:T(8,128)S(1)} %get-tuple-element.76.prod_ref, f32[16,8,128]{2,1,0:T(8,128)S(1)} %get-tuple-element.81.enter_ref, f32[16,8,128]{2,1,0:T(8,128)S(1)} %bitcast.29, ...), custom_call_target="tpu_custom_call" | custom-call | flops 18350080 | bytes 20971520 | tf_op jit(solution)/shard_map/respond/pallas_call | solution.py:449
  136.1 2.3 pieces.11.refs_0_
  138.4 4.4 %collective-permute-start.23 = (bf16[256,1024]{1,0:T(8,128)(2,1)S(1)}, bf16[256,1024]{1,0:T(8,128)(2,1)S(1)}, u32[]{:S(2)}, u32[]{:S(2)}) collective-permute-start(bf16[256,1024]{1,0:T(8,128)(2,1)S(1)} %pieces.11.refs_0_), channel_id=1, source_target_pairs={{0,4},{2,6},{12,8},{14,10},{1,5},{3,7},{13,9},{15,11},{16,20},{18,... | collective-permute-start | bytes 1572872 | tf_op jit(solution)/shard_map/ppermute | solution.py:206
  143.4 3.7 %pieces.12 = (bf16[256,1024]{1,0:T(8,128)(2,1)S(1)}, f32[256,1024]{1,0:T(8,128)S(1)}) custom-call(s32[2]{0:T(128)S(1)} %pad_add_fusion.2.place_ref, bf16[256,1024]{1,0:T(8,128)(2,1)S(1)} %get-tuple-element.80.gated_ref, bf16[1024,8192]{1,0:T(8,128)(2,1)} %w_ref.19, bf16[256,1024]{1,0:T(8,128)(2,1)S(1)} %pieces.11.refs_0_), custom_call_target="tpu_custom_call" | custom-call | flops 2000000 | bytes 200000 | tf_op jit(solution)/shard_map/pieces/pallas_call | solution.py:154
  147.1 3.7 %pieces.18 = (bf16[256,1024]{1,0:T(8,128)(2,1)S(1)}, bf16[256,1024]{1,0:T(8,128)(2,1)S(1)}) custom-call(s32[2]{0:T(128)S(1)} %pad_add_fusion.2.place_ref, bf16[256,1024]{1,0:T(8,128)(2,1)S(1)} %get-tuple-element.82.gated_ref, bf16[1024,8192]{1,0:T(8,128)(2,1)} %w_ref.19, bf16[256,1024]{1,0:T(8,128)(2,1)S(1)} %get-tuple-element.84.refs_0_), custom_call_target="tpu_custom_call" | custom-call | flops 2000000 | bytes 200000 | tf_op jit(solution)/shard_map/pieces/pallas_call | solution.py:154
  150.8 3.6 %collective-permute-done.23 = bf16[256,1024]{1,0:T(8,128)(2,1)S(1)} collective-permute-done((bf16[256,1024]{1,0:T(8,128)(2,1)S(1)}, bf16[256,1024]{1,0:T(8,128)(2,1)S(1)}, u32[]{:S(2)}, u32[]{:S(2)}) %collective-permute-start.23) | collective-permute-done | bytes 524320 | tf_op jit(solution)/shard_map/ppermute | solution.py:206
  157.2 2.4 %collective-permute-start.27 = (bf16[256,1024]{1,0:T(8,128)(2,1)S(1)}, bf16[256,1024]{1,0:T(8,128)(2,1)S(1)}, u32[]{:S(2)}, u32[]{:S(2)}) collective-permute-start(bf16[256,1024]{1,0:T(8,128)(2,1)S(1)} %get-tuple-element.100), channel_id=1, source_target_pairs={{0,4},{2,6},{12,8},{14,10},{1,5},{3,7},{13,9},{15,11},{16,20},{18,... | collective-permute-start | bytes 1572872 | tf_op jit(solution)/shard_map/ppermute | solution.py:206
  162.2 3.8 %collective-permute-start.17 = (bf16[256,1024]{1,0:T(8,128)(2,1)S(1)}, bf16[256,1024]{1,0:T(8,128)(2,1)S(1)}, u32[]{:S(2)}, u32[]{:S(2)}) collective-permute-start(bf16[256,1024]{1,0:T(8,128)(2,1)S(1)} %add_convert_fusion.8), channel_id=1, source_target_pairs={{0,4},{2,6},{12,8},{14,10},{1,5},{3,7},{13,9},{15,11},{16,20},{18,... | collective-permute-start | bytes 1572872 | tf_op jit(solution)/shard_map/ppermute | solution.py:206
  166.0 3.7 %pieces.19 = (f32[256,1024]{1,0:T(8,128)S(1)}, bf16[256,1024]{1,0:T(8,128)(2,1)S(1)}) custom-call(s32[2]{0:T(128)S(1)} %pad_add_fusion.4.place_ref, bf16[256,1024]{1,0:T(8,128)(2,1)S(1)} %get-tuple-element.82.gated_ref, bf16[1024,8192]{1,0:T(8,128)(2,1)} %w_ref.19, bf16[256,1024]{1,0:T(8,128)(2,1)S(1)} %add_convert_fusion.3.refs_0_), custom_call_target="tpu_custom_call" | custom-call | flops 2000000 | bytes 200000 | tf_op jit(solution)/shard_map/pieces/pallas_call | solution.py:154
  169.7 3.7 %pieces.15 = (f32[256,1024]{1,0:T(8,128)S(1)}, bf16[256,1024]{1,0:T(8,128)(2,1)S(1)}) custom-call(s32[2]{0:T(128)S(1)} %pad_add_fusion.4.place_ref, bf16[256,1024]{1,0:T(8,128)(2,1)S(1)} %get-tuple-element.80.gated_ref, bf16[1024,8192]{1,0:T(8,128)(2,1)} %w_ref.19, bf16[256,1024]{1,0:T(8,128)(2,1)S(1)} %collective-permute-done.13.refs_0_), custom_call_target="tpu_custom_call" | custom-call | flops 2000000 | bytes 200000 | tf_op jit(solution)/shard_map/pieces/pallas_call | solution.py:154
  173.4 3.7 %pieces.17 = (f32[256,1024]{1,0:T(8,128)S(1)}, bf16[256,1024]{1,0:T(8,128)(2,1)S(1)}) custom-call(s32[2]{0:T(128)S(1)} %pad_add_fusion.3.place_ref, bf16[256,1024]{1,0:T(8,128)(2,1)S(1)} %get-tuple-element.82.gated_ref, bf16[1024,8192]{1,0:T(8,128)(2,1)} %w_ref.19, bf16[256,1024]{1,0:T(8,128)(2,1)S(1)} %collective-permute-done.13.refs_0_), custom_call_target="tpu_custom_call" | custom-call | flops 2000000 | bytes 200000 | tf_op jit(solution)/shard_map/pieces/pallas_call | solution.py:154
  177.1 3.7 %pieces.14 = (f32[256,1024]{1,0:T(8,128)S(1)}, bf16[256,1024]{1,0:T(8,128)(2,1)S(1)}) custom-call(s32[2]{0:T(128)S(1)} %pad_add_fusion.3.place_ref, bf16[256,1024]{1,0:T(8,128)(2,1)S(1)} %get-tuple-element.80.gated_ref, bf16[1024,8192]{1,0:T(8,128)(2,1)} %w_ref.19, bf16[256,1024]{1,0:T(8,128)(2,1)S(1)} %collective-permute-done.13.refs_0_), custom_call_target="tpu_custom_call" | custom-call | flops 2000000 | bytes 200000 | tf_op jit(solution)/shard_map/pieces/pallas_call | solution.py:154
  184.1 3.4 %collective-permute-start.20 = (bf16[256,1024]{1,0:T(8,128)(2,1)S(1)}, bf16[256,1024]{1,0:T(8,128)(2,1)S(1)}, u32[]{:S(2)}, u32[]{:S(2)}) collective-permute-start(bf16[256,1024]{1,0:T(8,128)(2,1)S(1)} %add_convert_fusion.7), channel_id=1, source_target_pairs={{0,4},{2,6},{12,8},{14,10},{1,5},{3,7},{13,9},{15,11},{16,20},{18,... | collective-permute-start | bytes 1572872 | tf_op jit(solution)/shard_map/ppermute | solution.py:206
  188.2 4.9 %collective-permute-done.25 = bf16[256,1024]{1,0:T(8,128)(2,1)S(1)} collective-permute-done((bf16[256,1024]{1,0:T(8,128)(2,1)S(1)}, bf16[256,1024]{1,0:T(8,128)(2,1)S(1)}, u32[]{:S(2)}, u32[]{:S(2)}) %collective-permute-start.25) | collective-permute-done | bytes 524320 | tf_op jit(solution)/shard_map/ppermute | solution.py:217
  197.9 10.0 %collective-permute-done.15 = bf16[256,1024]{1,0:T(8,128)(2,1)S(1)} collective-permute-done((bf16[256,1024]{1,0:T(8,128)(2,1)S(1)}, bf16[256,1024]{1,0:T(8,128)(2,1)S(1)}, u32[]{:S(2)}, u32[]{:S(2)}) %collective-permute-start.15) | collective-permute-done | bytes 524320 | tf_op jit(solution)/shard_map/ppermute | solution.py:217
  209.6 9.6 %collective-permute-done.26.refs_5_ = bf16[256,1024]{1,0:T(8,128)(2,1)S(1)} collective-permute-done((bf16[256,1024]{1,0:T(8,128)(2,1)S(1)}, bf16[256,1024]{1,0:T(8,128)(2,1)S(1)}, u32[]{:S(2)}, u32[]{:S(2)}) %collective-permute-start.26) | collective-permute-done | bytes 524320 | tf_op jit(solution)/shard_map/ppermute | solution.py:217
  219.2 2.3 pieces.16
  221.5 2.4 %pieces.13 = f32[256,1024]{1,0:T(8,128)S(1)} custom-call(s32[1]{0:T(128)} %bitcast.place_ref, bf16[256,1024]{1,0:T(8,128)(2,1)S(1)} %get-tuple-element.80.gated_ref, bf16[1024,8192]{1,0:T(8,128)(2,1)} %w_ref.19, bf16[256,1024]{1,0:T(8,128)(2,1)S(1)} %collective-permute-done.14.refs_0_), custom_call_target="tpu_custom_call" | custom-call | flops 1000000 | bytes 100000 | tf_op jit(solution)/shard_map/pieces/pallas_call | solution.py:154
  224.3 2.6 %collective-permute-done.16.refs_1_ = bf16[256,1024]{1,0:T(8,128)(2,1)S(1)} collective-permute-done((bf16[256,1024]{1,0:T(8,128)(2,1)S(1)}, bf16[256,1024]{1,0:T(8,128)(2,1)S(1)}, u32[]{:S(2)}, u32[]{:S(2)}) %collective-permute-start.16) | collective-permute-done | bytes 524320 | tf_op jit(solution)/shard_map/ppermute | solution.py:217
  (95 shorter events, 46.2 us)
Async XLA Ops:
  0.0 26.5 %collective-permute-start = (bf16[512,1024]{1,0:T(8,128)(2,1)}, bf16[512,1024]{1,0:T(8,128)(2,1)}, u32[]{:S(2)}, u32[]{:S(2)}) collective-permute-start(bf16[512,1024]{1,0:T(8,128)(2,1)} %refs_0_.1), channel_id=1, source_target_pairs={{0,4},{2,6},{4,0},{6,2},{8,12},{10,14},{12,8},{14,10},{1,5},{3,7},... | collective-permute-start | bytes 3145736 | tf_op jit(solution)/shard_map/ppermute | solution.py:206
  3.0 23.5 %collective-permute-start.3 = (bf16[512,1024]{1,0:T(8,128)(2,1)}, bf16[512,1024]{1,0:T(8,128)(2,1)S(1)}, u32[]{:S(2)}, u32[]{:S(2)}) collective-permute-start(bf16[512,1024]{1,0:T(8,128)(2,1)} %refs_0_.1), channel_id=1, source_target_pairs={{4,8},{6,10},{8,4},{10,6},{5,9},{7,11},{9,5},{11,7},{20,24},{22,26... | collective-permute-start | bytes 3145736 | tf_op jit(solution)/shard_map/ppermute | solution.py:206
  3.7 25.7 %collective-permute-start.1 = (bf16[512,1024]{1,0:T(8,128)(2,1)}, bf16[512,1024]{1,0:T(8,128)(2,1)S(1)}, u32[]{:S(2)}, u32[]{:S(2)}) collective-permute-start(bf16[512,1024]{1,0:T(8,128)(2,1)} %refs_0_.1), channel_id=1, source_target_pairs={{0,2},{2,0},{4,6},{6,4},{8,10},{10,8},{12,14},{14,12},{1,3},{3,1},... | collective-permute-start | bytes 3145736 | tf_op jit(solution)/shard_map/ppermute | solution.py:217
  26.5 28.3 %collective-permute-start.4 = (bf16[512,1024]{1,0:T(8,128)(2,1)S(1)}, bf16[512,1024]{1,0:T(8,128)(2,1)}, u32[]{:S(2)}, u32[]{:S(2)}) collective-permute-start(bf16[512,1024]{1,0:T(8,128)(2,1)S(1)} %collective-permute-done.3.refs_2_), channel_id=1, source_target_pairs={{4,0},{6,2},{8,12},{10,14},{5,1},{7,3},{9,13},{11,15},{20,16},{22,... | collective-permute-start | bytes 3145736 | tf_op jit(solution)/shard_map/ppermute | solution.py:206
  27.8 27.0 %collective-permute-start.5 = (bf16[512,1024]{1,0:T(8,128)(2,1)}, bf16[512,1024]{1,0:T(8,128)(2,1)}, u32[]{:S(2)}, u32[]{:S(2)}) collective-permute-start(bf16[512,1024]{1,0:T(8,128)(2,1)} %collective-permute-done.refs_1_), channel_id=1, source_target_pairs={{4,8},{6,10},{8,4},{10,6},{5,9},{7,11},{9,5},{11,7},{20,24},{22,26... | collective-permute-start | bytes 3145736 | tf_op jit(solution)/shard_map/ppermute | solution.py:206
  29.4 26.7 %collective-permute-start.2 = (bf16[512,1024]{1,0:T(8,128)(2,1)}, bf16[512,1024]{1,0:T(8,128)(2,1)}, u32[]{:S(2)}, u32[]{:S(2)}) collective-permute-start(bf16[512,1024]{1,0:T(8,128)(2,1)} %collective-permute-done.refs_1_), channel_id=1, source_target_pairs={{0,2},{2,0},{4,6},{6,4},{8,10},{10,8},{12,14},{14,12},{1,3},{3,1},... | collective-permute-start | bytes 3145736 | tf_op jit(solution)/shard_map/ppermute | solution.py:217
  56.2 23.6 %collective-permute-start.6 = (bf16[512,1024]{1,0:T(8,128)(2,1)S(1)}, bf16[512,1024]{1,0:T(8,128)(2,1)}, u32[]{:S(2)}, u32[]{:S(2)}) collective-permute-start(bf16[512,1024]{1,0:T(8,128)(2,1)S(1)} %broadcast_select_fusion.refs_1_), channel_id=1, source_target_pairs={{0,2},{2,0},{4,6},{6,4},{8,10},{10,8},{12,14},{14,12},{1,3},{3,1},... | collective-permute-start | bytes 3145736 | tf_op jit(solution)/shard_map/ppermute | solution.py:217
  57.8 28.0 %collective-permute-start.7 = (bf16[512,1024]{1,0:T(8,128)(2,1)}, bf16[512,1024]{1,0:T(8,128)(2,1)}, u32[]{:S(2)}, u32[]{:S(2)}) collective-permute-start(bf16[512,1024]{1,0:T(8,128)(2,1)} %collective-permute-done.5), channel_id=1, source_target_pairs={{4,0},{6,2},{8,12},{10,14},{5,1},{7,3},{9,13},{11,15},{20,16},{22,... | collective-permute-start | bytes 3145736 | tf_op jit(solution)/shard_map/ppermute | solution.py:206
  60.0 41.5 %collective-permute-start.10 = (bf16[512,512]{1,0:T(8,128)(2,1)}, bf16[512,512]{1,0:T(8,128)(2,1)S(1)}, u32[]{:S(2)}, u32[]{:S(2)}) collective-permute-start(bf16[512,512]{1,0:T(8,128)(2,1)} %slice.27), channel_id=1, source_target_pairs={{4,8},{6,10},{8,4},{10,6},{5,9},{7,11},{9,5},{11,7},{20,24},{22,26... | collective-permute-start | bytes 1572872 | tf_op jit(solution)/shard_map/ppermute | solution.py:206
  80.8 20.7 %collective-permute-start.9 = (bf16[512,512]{1,0:T(8,128)(2,1)S(1)}, bf16[512,512]{1,0:T(8,128)(2,1)S(1)}, u32[]{:S(2)}, u32[]{:S(2)}) collective-permute-start(bf16[512,512]{1,0:T(8,128)(2,1)S(1)} %slice.26), channel_id=1, source_target_pairs={{4,0},{6,2},{8,12},{10,14},{5,1},{7,3},{9,13},{11,15},{20,16},{22,... | collective-permute-start | bytes 1572872 | tf_op jit(solution)/shard_map/ppermute | solution.py:206
  87.6 13.9 %collective-permute-start.8 = (bf16[512,512]{1,0:T(8,128)(2,1)}, bf16[512,512]{1,0:T(8,128)(2,1)S(1)}, u32[]{:S(2)}, u32[]{:S(2)}) collective-permute-start(bf16[512,512]{1,0:T(8,128)(2,1)} %slice_select_fusion), channel_id=1, source_target_pairs={{0,2},{2,0},{4,6},{6,4},{8,10},{10,8},{12,14},{14,12},{1,3},{3,1},... | collective-permute-start | bytes 1572872 | tf_op jit(solution)/shard_map/ppermute | solution.py:217
  111.0 2.2 collective-permute-start.11
  124.6 3.2 %collective-permute-start.12 = (f32[16,8,128]{2,1,0:T(8,128)S(1)}, f32[16,8,128]{2,1,0:T(8,128)S(1)}, u32[]{:S(2)}, u32[]{:S(2)}) collective-permute-start(f32[16,8,128]{2,1,0:T(8,128)S(1)} %get-tuple-element.77), channel_id=1, source_target_pairs={{0,1},{2,3},{4,5},{6,7},{8,9},{10,11},{12,13},{14,15},{16,17},{18,... | collective-permute-start | bytes 196616 | tf_op jit(solution)/shard_map/ppermute | solution.py:19
  138.4 16.1 %collective-permute-start.23 = (bf16[256,1024]{1,0:T(8,128)(2,1)S(1)}, bf16[256,1024]{1,0:T(8,128)(2,1)S(1)}, u32[]{:S(2)}, u32[]{:S(2)}) collective-permute-start(bf16[256,1024]{1,0:T(8,128)(2,1)S(1)} %pieces.11.refs_0_), channel_id=1, source_target_pairs={{0,4},{2,6},{12,8},{14,10},{1,5},{3,7},{13,9},{15,11},{16,20},{18,... | collective-permute-start | bytes 1572872 | tf_op jit(solution)/shard_map/ppermute | solution.py:206
  142.8 14.0 %collective-permute-start.13 = (bf16[256,1024]{1,0:T(8,128)(2,1)S(1)}, bf16[256,1024]{1,0:T(8,128)(2,1)S(1)}, u32[]{:S(2)}, u32[]{:S(2)}) collective-permute-start(bf16[256,1024]{1,0:T(8,128)(2,1)S(1)} %pieces.10.refs_0_), channel_id=1, source_target_pairs={{0,2},{2,0},{4,6},{6,4},{8,10},{10,8},{12,14},{14,12},{1,3},{3,1},... | collective-permute-start | bytes 1572872 | tf_op jit(solution)/shard_map/ppermute | solution.py:217
  156.7 24.0 %collective-permute-start.24 = (bf16[256,1024]{1,0:T(8,128)(2,1)S(1)}, bf16[256,1024]{1,0:T(8,128)(2,1)S(1)}, u32[]{:S(2)}, u32[]{:S(2)}) collective-permute-start(bf16[256,1024]{1,0:T(8,128)(2,1)S(1)} %add_convert_fusion.3.refs_0_), channel_id=1, source_target_pairs={{0,2},{2,0},{4,6},{6,4},{8,10},{10,8},{12,14},{14,12},{1,3},{3,1},... | collective-permute-start | bytes 1572872 | tf_op jit(solution)/shard_map/ppermute | solution.py:217
  157.2 24.1 %collective-permute-start.27 = (bf16[256,1024]{1,0:T(8,128)(2,1)S(1)}, bf16[256,1024]{1,0:T(8,128)(2,1)S(1)}, u32[]{:S(2)}, u32[]{:S(2)}) collective-permute-start(bf16[256,1024]{1,0:T(8,128)(2,1)S(1)} %get-tuple-element.100), channel_id=1, source_target_pairs={{0,4},{2,6},{12,8},{14,10},{1,5},{3,7},{13,9},{15,11},{16,20},{18,... | collective-permute-start | bytes 1572872 | tf_op jit(solution)/shard_map/ppermute | solution.py:206
  159.8 23.1 %collective-permute-start.22 = (bf16[256,1024]{1,0:T(8,128)(2,1)S(1)}, bf16[256,1024]{1,0:T(8,128)(2,1)S(1)}, u32[]{:S(2)}, u32[]{:S(2)}) collective-permute-start(bf16[256,1024]{1,0:T(8,128)(2,1)S(1)} %pieces.11.refs_0_), channel_id=1, source_target_pairs={{4,8},{6,10},{8,4},{10,6},{5,9},{7,11},{9,5},{11,7},{20,24},{22,26... | collective-permute-start | bytes 1572872 | tf_op jit(solution)/shard_map/ppermute | solution.py:206
  160.5 23.4 %collective-permute-start.14 = (bf16[256,1024]{1,0:T(8,128)(2,1)S(1)}, bf16[256,1024]{1,0:T(8,128)(2,1)S(1)}, u32[]{:S(2)}, u32[]{:S(2)}) collective-permute-start(bf16[256,1024]{1,0:T(8,128)(2,1)S(1)} %get-tuple-element.84.refs_0_), channel_id=1, source_target_pairs={{0,2},{2,0},{4,6},{6,4},{8,10},{10,8},{12,14},{14,12},{1,3},{3,1},... | collective-permute-start | bytes 1572872 | tf_op jit(solution)/shard_map/ppermute | solution.py:217
  162.2 21.6 %collective-permute-start.17 = (bf16[256,1024]{1,0:T(8,128)(2,1)S(1)}, bf16[256,1024]{1,0:T(8,128)(2,1)S(1)}, u32[]{:S(2)}, u32[]{:S(2)}) collective-permute-start(bf16[256,1024]{1,0:T(8,128)(2,1)S(1)} %add_convert_fusion.8), channel_id=1, source_target_pairs={{0,4},{2,6},{12,8},{14,10},{1,5},{3,7},{13,9},{15,11},{16,20},{18,... | collective-permute-start | bytes 1572872 | tf_op jit(solution)/shard_map/ppermute | solution.py:206
  180.8 12.3 %collective-permute-start.25 = (bf16[256,1024]{1,0:T(8,128)(2,1)S(1)}, bf16[256,1024]{1,0:T(8,128)(2,1)S(1)}, u32[]{:S(2)}, u32[]{:S(2)}) collective-permute-start(bf16[256,1024]{1,0:T(8,128)(2,1)S(1)} %get-tuple-element.96), channel_id=1, source_target_pairs={{0,2},{2,0},{4,6},{6,4},{8,10},{10,8},{12,14},{14,12},{1,3},{3,1},... | collective-permute-start | bytes 1572872 | tf_op jit(solution)/shard_map/ppermute | solution.py:217
  181.6 13.7 %collective-permute-start.30 = (bf16[256,1024]{1,0:T(8,128)(2,1)S(1)}, bf16[256,1024]{1,0:T(8,128)(2,1)S(1)}, u32[]{:S(2)}, u32[]{:S(2)}) collective-permute-start(bf16[256,1024]{1,0:T(8,128)(2,1)S(1)} %add_convert_fusion.2), channel_id=1, source_target_pairs={{0,4},{2,6},{12,8},{14,10},{1,5},{3,7},{13,9},{15,11},{16,20},{18,... | collective-permute-start | bytes 1572872 | tf_op jit(solution)/shard_map/ppermute | solution.py:206
  183.1 13.8 %collective-permute-start.28 = (bf16[256,1024]{1,0:T(8,128)(2,1)S(1)}, bf16[256,1024]{1,0:T(8,128)(2,1)S(1)}, u32[]{:S(2)}, u32[]{:S(2)}) collective-permute-start(bf16[256,1024]{1,0:T(8,128)(2,1)S(1)} %add_convert_fusion.2), channel_id=1, source_target_pairs={{4,8},{6,10},{8,4},{10,6},{5,9},{7,11},{9,5},{11,7},{20,24},{22,26... | collective-permute-start | bytes 1572872 | tf_op jit(solution)/shard_map/ppermute | solution.py:206
  184.1 23.9 %collective-permute-start.20 = (bf16[256,1024]{1,0:T(8,128)(2,1)S(1)}, bf16[256,1024]{1,0:T(8,128)(2,1)S(1)}, u32[]{:S(2)}, u32[]{:S(2)}) collective-permute-start(bf16[256,1024]{1,0:T(8,128)(2,1)S(1)} %add_convert_fusion.7), channel_id=1, source_target_pairs={{0,4},{2,6},{12,8},{14,10},{1,5},{3,7},{13,9},{15,11},{16,20},{18,... | collective-permute-start | bytes 1572872 | tf_op jit(solution)/shard_map/ppermute | solution.py:206
  187.5 21.1 %collective-permute-start.18 = (bf16[256,1024]{1,0:T(8,128)(2,1)S(1)}, bf16[256,1024]{1,0:T(8,128)(2,1)S(1)}, u32[]{:S(2)}, u32[]{:S(2)}) collective-permute-start(bf16[256,1024]{1,0:T(8,128)(2,1)S(1)} %add_convert_fusion.7), channel_id=1, source_target_pairs={{4,8},{6,10},{8,4},{10,6},{5,9},{7,11},{9,5},{11,7},{20,24},{22,26... | collective-permute-start | bytes 1572872 | tf_op jit(solution)/shard_map/ppermute | solution.py:206
  193.1 14.9 %collective-permute-start.15 = (bf16[256,1024]{1,0:T(8,128)(2,1)S(1)}, bf16[256,1024]{1,0:T(8,128)(2,1)S(1)}, u32[]{:S(2)}, u32[]{:S(2)}) collective-permute-start(bf16[256,1024]{1,0:T(8,128)(2,1)S(1)} %get-tuple-element.87), channel_id=1, source_target_pairs={{0,2},{2,0},{4,6},{6,4},{8,10},{10,8},{12,14},{14,12},{1,3},{3,1},... | collective-permute-start | bytes 1572872 | tf_op jit(solution)/shard_map/ppermute | solution.py:217
  195.2 23.9 %collective-permute-start.26 = (bf16[256,1024]{1,0:T(8,128)(2,1)S(1)}, bf16[256,1024]{1,0:T(8,128)(2,1)S(1)}, u32[]{:S(2)}, u32[]{:S(2)}) collective-permute-start(bf16[256,1024]{1,0:T(8,128)(2,1)S(1)} %add_convert_fusion.4), channel_id=1, source_target_pairs={{0,2},{2,0},{4,6},{6,4},{8,10},{10,8},{12,14},{14,12},{1,3},{3,1},... | collective-permute-start | bytes 1572872 | tf_op jit(solution)/shard_map/ppermute | solution.py:217
  197.0 27.3 %collective-permute-start.31 = (bf16[256,1024]{1,0:T(8,128)(2,1)S(1)}, bf16[256,1024]{1,0:T(8,128)(2,1)S(1)}, u32[]{:S(2)}, u32[]{:S(2)}) collective-permute-start(bf16[256,1024]{1,0:T(8,128)(2,1)S(1)} %add_convert_fusion), channel_id=1, source_target_pairs={{4,8},{6,10},{8,4},{10,6},{5,9},{7,11},{9,5},{11,7},{20,24},{22,26... | collective-permute-start | bytes 1572872 | tf_op jit(solution)/shard_map/ppermute | solution.py:206
  207.9 16.3 %collective-permute-start.29 = (bf16[256,1024]{1,0:T(8,128)(2,1)S(1)}, bf16[256,1024]{1,0:T(8,128)(2,1)S(1)}, u32[]{:S(2)}, u32[]{:S(2)}) collective-permute-start(bf16[256,1024]{1,0:T(8,128)(2,1)S(1)} %add_convert_fusion.1), channel_id=1, source_target_pairs={{0,4},{2,6},{4,0},{6,2},{8,12},{10,14},{12,8},{14,10},{1,5},{3,7},... | collective-permute-start | bytes 1572872 | tf_op jit(solution)/shard_map/ppermute | solution.py:206
  207.9 18.9 %collective-permute-start.16 = (bf16[256,1024]{1,0:T(8,128)(2,1)S(1)}, bf16[256,1024]{1,0:T(8,128)(2,1)S(1)}, u32[]{:S(2)}, u32[]{:S(2)}) collective-permute-start(bf16[256,1024]{1,0:T(8,128)(2,1)S(1)} %get-tuple-element.88), channel_id=1, source_target_pairs={{0,2},{2,0},{4,6},{6,4},{8,10},{10,8},{12,14},{14,12},{1,3},{3,1},... | collective-permute-start | bytes 1572872 | tf_op jit(solution)/shard_map/ppermute | solution.py:217
  208.6 18.2 %collective-permute-start.21 = (bf16[256,1024]{1,0:T(8,128)(2,1)S(1)}, bf16[256,1024]{1,0:T(8,128)(2,1)S(1)}, u32[]{:S(2)}, u32[]{:S(2)}) collective-permute-start(bf16[256,1024]{1,0:T(8,128)(2,1)S(1)} %add_convert_fusion.5), channel_id=1, source_target_pairs={{4,8},{6,10},{8,4},{10,6},{5,9},{7,11},{9,5},{11,7},{20,24},{22,26... | collective-permute-start | bytes 1572872 | tf_op jit(solution)/shard_map/ppermute | solution.py:206
  219.2 9.2 %collective-permute-start.19 = (bf16[256,1024]{1,0:T(8,128)(2,1)S(1)}, bf16[256,1024]{1,0:T(8,128)(2,1)S(1)}, u32[]{:S(2)}, u32[]{:S(2)}) collective-permute-start(bf16[256,1024]{1,0:T(8,128)(2,1)S(1)} %add_convert_fusion.6), channel_id=1, source_target_pairs={{0,4},{2,6},{4,0},{6,2},{8,12},{10,14},{12,8},{14,10},{1,5},{3,7},... | collective-permute-start | bytes 1572872 | tf_op jit(solution)/shard_map/ppermute | solution.py:206
  (10 other events, 142.3 us)
where the time goes:
time: 231 us; the launch traced here: 230 us
  Pallas kernels  112 us (48%)
  waiting for transfers between devices  63.3 us (27%)
  starting transfers between devices  42.9 us (19%)
  other arithmetic  6.06 us (3%)
  local copies, waits for them, and re-layouts  5.29 us (2%)
    pallas_call x5, Pallas kernels, accumulate(): pl.pallas_call(functools.partial(accumulate_kernel, depths, pairs, width,...  61.7 us
    ppermute x11, waiting for transfers between devices, across(): return lax.ppermute(block, 'chan', [(c, c ^ 1) for c in range(count)])  33.4 us
    pallas_call x10, Pallas kernels, pieces(): pl.pallas_call(functools.partial(pieces_kernel, count), grid_spec=pltpu.P...  31.4 us
    ppermute x19, starting transfers between devices, along_line(): lax.ppermute(block, 'chan', [(2 * a + y, 2 * b + y) for a, b in pairs for...  28.7 us
    ppermute x19, waiting for transfers between devices, along_line(): lax.ppermute(block, 'chan', [(2 * a + y, 2 * b + y) for a, b in pairs for...  28.1 us
    pallas_call x1, Pallas kernels, convolve(): pl.pallas_call(functools.partial(convolve_kernel, len(parts)), grid=(rows...  11.3 us
    ppermute x11, starting transfers between devices, across(): return lax.ppermute(block, 'chan', [(c, c ^ 1) for c in range(count)])  10.6 us
    pallas_call x2, Pallas kernels, respond(): pl.pallas_call(respond_kernel, grid=(rows // blk,), in_specs=[row_spec, r...  6.03 us
  transfers between devices with their start and end apart: 32, of which 14 were waited for; matrix products, arithmetic and copies ran while one was open for 4% of the time, Pallas kernels for 34%

commit v1 on v0

--- a/solution.py
+++ b/solution.py
@@ -242,7 +242,7 @@
     acc, square = accumulate([own_over, next_one], [me ^ 1, me ^ 2], gain, in_weight, acc, square)
     second = jnp.where(at_end, second_out, second_mid)
     second_over = across(second, next_over, square)
-    third_out = along_line(after(second_mid, second_out, square), OUTWARD)
+    third_out = along_line(after(second_mid, square), OUTWARD)
     rest_mid = along_line(after(own_over[:, half:], second_mid, square), MIDDLE)
     acc, square = accumulate([next_over, second], [me ^ 3, me ^ 4], gain, in_weight, acc, square)
     third_over = across(jnp.where(at_end, third_out[:, :half], middle[:, :half]), second_over, square)
@@ -287,18 +287,20 @@
     second_send = [second_send_0, narrow(total(second_send_1, rest_in))]
     second_over = [across(second_send[h], third_over) for h in both]
     halves = (upper, lower)
-    later = [make(halves[h], [keep(2), send(1)], (third_over, second_send[1])[h]) for h in both]
+    later_0 = make(upper, [keep(2), send(1)], third_1)
+    later = [later_0, make(lower, [keep(2), send(1)], third_in[0])]
     second = [narrow(total(later[h][0], second_over[h], third_in[h])) for h in both]
     second_in = [along_line(second[h], INWARD) for h in both]
     second_mid = [along_line(second[h], MIDDLE) for h in both]
     next_over = [across(later[h][1], second_over[h]) for h in both]
-    later = [make(halves[h], [keep(1), send(0)], third_over) for h in both]
+    later_0 = make(upper, [keep(1), send(0)], later[1][0])
+    later = [later_0, make(lower, [keep(1), send(0)], second_over[0])]
     own_send = [later[0][1], narrow(total(later[1][1], rest_mid))]
     next_one = [narrow(total(later[h][0], next_over[h], second_mid[h])) for h in both]
     next_in = [along_line(next_one[h], PAIRS) for h in both]
     middle_in = [along_line(narrow(total(third[h], second_in[h])), MIDDLE) for h in both]
     own_over = [across(own_send[h], next_over[h]) for h in both]
-    own_keep = [make(halves[h], [keep(0)], second_over[0])[0] for h in both]
+    own_keep = [make(halves[h], [keep(0)], second_over[1])[0] for h in both]
     base = [total(own_keep[h], tokens[h * half : (h + 1) * half]) for h in both]
     return finish(*[[base[h], own_over[h], next_in[h], middle_in[h]] for h in both])
 

time: 231 us -> 226 us (0.978)
  waiting for transfers between devices: 63.3 us -> 31.7 us
  starting transfers between devices: 42.9 us -> 69.3 us
    ppermute x11, waiting for transfers between devices: 33.4 us -> 7.46 us  [across(): return lax.ppermute(block, 'chan', [(c, c ^ 1) for c in range(count)])]
    ppermute x19, starting transfers between devices: 28.7 us -> 51.4 us  [along_line(): lax.ppermute(block, 'chan', [(2 * a + y, 2 * b + y) for a, b in pairs for...]
    ppermute x19, waiting for transfers between devices: 28.1 us -> 22.5 us  [along_line(): lax.ppermute(block, 'chan', [(2 * a + y, 2 * b + y) for a, b in pairs for...]
    ppermute x11, starting transfers between devices: 10.6 us -> 14.4 us  [across(): return lax.ppermute(block, 'chan', [(c, c ^ 1) for c in range(count)])]
  transfers between devices with their start and end apart: 32 -> 32, of which waited for: 14 -> 9; matrix products, arithmetic and copies ran while one was open for 4% -> 4% of each run, Pallas kernels for 34% -> 38%
where the time goes in v1:
time: 226 us; the launch traced here: 225 us
  Pallas kernels  112 us (50%)
  starting transfers between devices  69.3 us (31%)
  waiting for transfers between devices  31.7 us (14%)
  other arithmetic  5.98 us (3%)
  local copies, waits for them, and re-layouts  5.29 us (2%)
    pallas_call x5, Pallas kernels, accumulate(): pl.pallas_call(functools.partial(accumulate_kernel, depths, pairs, width,...  61.7 us
    ppermute x19, starting transfers between devices, along_line(): lax.ppermute(block, 'chan', [(2 * a + y, 2 * b + y) for a, b in pairs for...  51.4 us
    pallas_call x10, Pallas kernels, pieces(): pl.pallas_call(functools.partial(pieces_kernel, count), grid_spec=pltpu.P...  31.4 us
    ppermute x19, waiting for transfers between devices, along_line(): lax.ppermute(block, 'chan', [(2 * a + y, 2 * b + y) for a, b in pairs for...  22.5 us
    ppermute x11, starting transfers between devices, across(): return lax.ppermute(block, 'chan', [(c, c ^ 1) for c in range(count)])  14.4 us
    pallas_call x1, Pallas kernels, convolve(): pl.pallas_call(functools.partial(convolve_kernel, len(parts)), grid=(rows...  11.3 us
    ppermute x11, waiting for transfers between devices, across(): return lax.ppermute(block, 'chan', [(c, c ^ 1) for c in range(count)])  7.46 us
    pallas_call x2, Pallas kernels, respond(): pl.pallas_call(respond_kernel, grid=(rows // blk,), in_specs=[row_spec, r...  6.01 us
  transfers between devices with their start and end apart: 32, of which 9 were waited for; matrix products, arithmetic and copies ran while one was open for 4% of the time, Pallas kernels for 38%

profile of v1, /device:TPU:0, one launch (start us, length us, event | category | flops | bytes accessed | tf_op | source)
XLA Modules:
  0.0 225.1 jit_solution(8358866089998971702)
XLA Ops:
  0.0 3.0 %collective-permute-start = (bf16[512,1024]{1,0:T(8,128)(2,1)}, bf16[512,1024]{1,0:T(8,128)(2,1)}, u32[]{:S(2)}, u32[]{:S(2)}) collective-permute-start(bf16[512,1024]{1,0:T(8,128)(2,1)} %refs_0_.1), channel_id=1, source_target_pairs={{0,4},{2,6},{4,0},{6,2},{8,12},{10,14},{12,8},{14,10},{1,5},{3,7},... | collective-permute-start | bytes 3145736 | tf_op jit(solution)/shard_map/ppermute | solution.py:206
  7.4 8.9 %accumulate.5 = (f32[3,512,1024]{2,1,0:T(8,128)}, f32[512,128]{1,0:T(8,128)S(1)}) custom-call(s32[1]{0:T(128)} %bitcast.place_ref, bf16[512,1024]{1,0:T(8,128)(2,1)S(1)} %copy-done, f32[8,1,1024]{2,1,0:T(1,128)S(1)} %bitcast.18, bf16[3,8192,1024]{2,1,0:T(8,128)(2,1)} %refs_6_.3), custom_call_target="tpu_custom_call" | custom-call | flops 536870912 | bytes 6291456 | tf_op jit(solution)/shard_map/accumulate/pallas_call | solution.py:112
  16.2 10.3 %collective-permute-done.refs_1_ = bf16[512,1024]{1,0:T(8,128)(2,1)} collective-permute-done((bf16[512,1024]{1,0:T(8,128)(2,1)}, bf16[512,1024]{1,0:T(8,128)(2,1)}, u32[]{:S(2)}, u32[]{:S(2)}) %collective-permute-start) | collective-permute-done | bytes 1048608 | tf_op jit(solution)/shard_map/ppermute | solution.py:206
  32.6 14.8 %accumulate.6 = (f32[3,512,1024]{2,1,0:T(8,128)}, f32[512,128]{1,0:T(8,128)S(1)}) custom-call(s32[2]{0:T(128)S(1)} %pad_add_fusion.1.place_ref, bf16[512,1024]{1,0:T(8,128)(2,1)S(1)} %collective-permute-done.1.refs_0_, bf16[512,1024]{1,0:T(8,128)(2,1)} %collective-permute-done.refs_1_, ...), custom_call_target="tpu_custom_call", output_to_operand_aliasing={{0}: (7, {}), {1}: (8, {})} | custom-call | flops 1073741824 | bytes 12582912 | tf_op jit(solution)/shard_map/accumulate/pallas_call | solution.py:112
  48.7 6.5 %collective-permute-done.4 = bf16[512,1024]{1,0:T(8,128)(2,1)} collective-permute-done((bf16[512,1024]{1,0:T(8,128)(2,1)S(1)}, bf16[512,1024]{1,0:T(8,128)(2,1)}, u32[]{:S(2)}, u32[]{:S(2)}) %collective-permute-start.4) | collective-permute-done | bytes 1048608 | tf_op jit(solution)/shard_map/ppermute | solution.py:206
  59.8 14.8 %accumulate.7 = (f32[3,512,1024]{2,1,0:T(8,128)}, f32[512,128]{1,0:T(8,128)S(1)}) custom-call(s32[2]{0:T(128)S(1)} %pad_add_fusion.place_ref, bf16[512,1024]{1,0:T(8,128)(2,1)} %collective-permute-done.2.refs_0_, bf16[512,1024]{1,0:T(8,128)(2,1)S(1)} %broadcast_select_fusion.refs_1_, ...), custom_call_target="tpu_custom_call", output_to_operand_aliasing={{0}: (7, {}), {1}: (8, {})} | custom-call | flops 1073741824 | bytes 12582912 | tf_op jit(solution)/shard_map/accumulate/pallas_call | solution.py:112
  74.6 3.0 %collective-permute-done.7.refs_1_ = bf16[512,1024]{1,0:T(8,128)(2,1)} collective-permute-done((bf16[512,1024]{1,0:T(8,128)(2,1)}, bf16[512,1024]{1,0:T(8,128)(2,1)}, u32[]{:S(2)}, u32[]{:S(2)}) %collective-permute-start.7) | collective-permute-done | bytes 1048608 | tf_op jit(solution)/shard_map/ppermute | solution.py:206
  83.9 13.7 %accumulate.8 = (f32[3,512,1024]{2,1,0:T(8,128)}, f32[512,128]{1,0:T(8,128)S(1)}) custom-call(s32[3]{0:T(128)S(1)} %add_add_fusion.place_ref, bf16[512,1024]{1,0:T(8,128)(2,1)} %collective-permute-done.6.refs_0_, bf16[512,1024]{1,0:T(8,128)(2,1)} %collective-permute-done.7.refs_1_, ...), custom_call_target="tpu_custom_call", output_to_operand_aliasing={{1}: (8, {})} | custom-call | flops 1073741824 | bytes 12582912 | tf_op jit(solution)/shard_map/accumulate/pallas_call | solution.py:112
  97.6 9.4 %accumulate.9 = (f32[3,512,1024]{2,1,0:T(8,128)}, f32[512,128]{1,0:T(8,128)S(1)}, f32[3,8,1024]{2,1,0:T(8,128)S(1)}) custom-call(s32[3]{0:T(128)S(1)} %add_add_fusion.1.place_ref, bf16[512,512]{1,0:T(8,128)(2,1)S(1)} %collective-permute-done.8.refs_0_, bf16[512,512]{1,0:T(8,128)(2,1)S(1)} %collective-permute-done.9.refs_1_, ...), custom_call_target="tpu_custom_call", output_to_operand_aliasing={{1}: (8, {})} | custom-call | flops 536870912 | bytes 6291456 | tf_op jit(solution)/shard_map/accumulate/pallas_call | solution.py:112
  109.3 11.3 %convolve.1 = (f32[512,8,128]{2,1,0:T(8,128)S(1)}, f32[512,8,128]{2,1,0:T(8,128)S(1)}, f32[16,8,128]{2,1,0:T(8,128)S(1)}) custom-call(f32[3,512,1024]{2,1,0:T(8,128)} %get-tuple-element.61.refs_8_.refs_0_, f32[3,512,1024]{2,1,0:T(8,128)} %get-tuple-element.65.refs_9_.refs_1_, f32[3,512,1024]{2,1,0:T(8,128)} %get-tuple-element.70.refs_2_, ...), custom_call_target="tpu_custom_call" | custom-call | flops 57671680 | bytes 10485760 | tf_op jit(solution)/shard_map/convolve/pallas_call | solution.py:378
  120.6 2.3 %collective-permute-start.12 = (f32[16,8,128]{2,1,0:T(8,128)S(1)}, f32[16,8,128]{2,1,0:T(8,128)S(1)}, u32[]{:S(2)}, u32[]{:S(2)}) collective-permute-start(f32[16,8,128]{2,1,0:T(8,128)S(1)} %get-tuple-element.77), channel_id=1, source_target_pairs={{0,1},{2,3},{4,5},{6,7},{8,9},{10,11},{12,13},{14,15},{16,17},{18,... | collective-permute-start | bytes 196616 | tf_op jit(solution)/shard_map/ppermute | solution.py:19
  123.8 2.7 %respond.2 = (bf16[256,1024]{1,0:T(8,128)(2,1)S(1)}, f32[16,8,128]{2,1,0:T(8,128)S(1)}) custom-call(f32[512,8,128]{2,1,0:T(8,128)S(1)} %get-tuple-element.75.q_ref, f32[512,8,128]{2,1,0:T(8,128)S(1)} %get-tuple-element.76.prod_ref, f32[16,8,128]{2,1,0:T(8,128)S(1)} %collective-permute-done.12.enter_ref, f32[16,8,128]{2,1,0:T(8,128)S(1)} %bitcast.28, ...), custom_call_target="tpu_custom_call" | custom-call | flops 18350080 | bytes 20971520 | tf_op jit(solution)/shard_map/respond/pallas_call | solution.py:451
  126.5 2.3 %pieces.10.refs_0_ = bf16[256,1024]{1,0:T(8,128)(2,1)S(1)} custom-call(s32[1]{0:T(128)} %bitcast.13.place_ref, bf16[256,1024]{1,0:T(8,128)(2,1)S(1)} %get-tuple-element.80.gated_ref, bf16[1024,8192]{1,0:T(8,128)(2,1)} %w_ref.19), custom_call_target="tpu_custom_call" | custom-call | flops 1000000 | bytes 100000 | tf_op jit(solution)/shard_map/pieces/pallas_call | solution.py:154
  129.4 3.3 %respond.3 = (bf16[256,1024]{1,0:T(8,128)(2,1)S(1)}, f32[16,8,128]{2,1,0:T(8,128)}) custom-call(f32[512,8,128]{2,1,0:T(8,128)S(1)} %get-tuple-element.75.q_ref, f32[512,8,128]{2,1,0:T(8,128)S(1)} %get-tuple-element.76.prod_ref, f32[16,8,128]{2,1,0:T(8,128)S(1)} %get-tuple-element.81.enter_ref, f32[16,8,128]{2,1,0:T(8,128)S(1)} %bitcast.29, ...), custom_call_target="tpu_custom_call" | custom-call | flops 18350080 | bytes 20971520 | tf_op jit(solution)/shard_map/respond/pallas_call | solution.py:451
  132.7 2.3 %pieces.11.refs_0_ = bf16[256,1024]{1,0:T(8,128)(2,1)S(1)} custom-call(s32[1]{0:T(128)} %bitcast.13.place_ref, bf16[256,1024]{1,0:T(8,128)(2,1)S(1)} %get-tuple-element.82.gated_ref, bf16[1024,8192]{1,0:T(8,128)(2,1)} %w_ref.19), custom_call_target="tpu_custom_call" | custom-call | flops 1000000 | bytes 100000 | tf_op jit(solution)/shard_map/pieces/pallas_call | solution.py:154
  135.0 4.6 %collective-permute-start.13 = (bf16[256,1024]{1,0:T(8,128)(2,1)S(1)}, bf16[256,1024]{1,0:T(8,128)(2,1)S(1)}, u32[]{:S(2)}, u32[]{:S(2)}) collective-permute-start(bf16[256,1024]{1,0:T(8,128)(2,1)S(1)} %pieces.11.refs_0_), channel_id=1, source_target_pairs={{0,4},{2,6},{12,8},{14,10},{1,5},{3,7},{13,9},{15,11},{16,20},{18,... | collective-permute-start | bytes 1572872 | tf_op jit(solution)/shard_map/ppermute | solution.py:206
  139.7 3.7 %pieces.12 = (bf16[256,1024]{1,0:T(8,128)(2,1)S(1)}, f32[256,1024]{1,0:T(8,128)S(1)}) custom-call(s32[2]{0:T(128)S(1)} %pad_add_fusion.2.place_ref, bf16[256,1024]{1,0:T(8,128)(2,1)S(1)} %get-tuple-element.80.gated_ref, bf16[1024,8192]{1,0:T(8,128)(2,1)} %w_ref.19, bf16[256,1024]{1,0:T(8,128)(2,1)S(1)} %pieces.11.refs_0_), custom_call_target="tpu_custom_call" | custom-call | flops 2000000 | bytes 200000 | tf_op jit(solution)/shard_map/pieces/pallas_call | solution.py:154
  145.2 3.2 %collective-permute-start.16 = (bf16[256,1024]{1,0:T(8,128)(2,1)S(1)}, bf16[256,1024]{1,0:T(8,128)(2,1)S(1)}, u32[]{:S(2)}, u32[]{:S(2)}) collective-permute-start(bf16[256,1024]{1,0:T(8,128)(2,1)S(1)} %add_convert_fusion.7), channel_id=1, source_target_pairs={{0,4},{2,6},{12,8},{14,10},{1,5},{3,7},{13,9},{15,11},{16,20},{18,... | collective-permute-start | bytes 1572872 | tf_op jit(solution)/shard_map/ppermute | solution.py:206
  148.4 3.7 %pieces.13 = (bf16[256,1024]{1,0:T(8,128)(2,1)S(1)}, bf16[256,1024]{1,0:T(8,128)(2,1)S(1)}) custom-call(s32[2]{0:T(128)S(1)} %pad_add_fusion.2.place_ref, bf16[256,1024]{1,0:T(8,128)(2,1)S(1)} %get-tuple-element.82.gated_ref, bf16[1024,8192]{1,0:T(8,128)(2,1)} %w_ref.19, bf16[256,1024]{1,0:T(8,128)(2,1)S(1)} %get-tuple-element.91.refs_0_), custom_call_target="tpu_custom_call" | custom-call | flops 2000000 | bytes 200000 | tf_op jit(solution)/shard_map/pieces/pallas_call | solution.py:154
  153.9 4.2 %collective-permute-start.27 = (bf16[256,1024]{1,0:T(8,128)(2,1)S(1)}, bf16[256,1024]{1,0:T(8,128)(2,1)S(1)}, u32[]{:S(2)}, u32[]{:S(2)}) collective-permute-start(bf16[256,1024]{1,0:T(8,128)(2,1)S(1)} %get-tuple-element.89.refs_0_), channel_id=1, source_target_pairs={{0,4},{2,6},{12,8},{14,10},{1,5},{3,7},{13,9},{15,11},{16,20},{18,... | collective-permute-start | bytes 1572872 | tf_op jit(solution)/shard_map/ppermute | solution.py:206
  159.0 3.7 %pieces.17 = (f32[256,1024]{1,0:T(8,128)S(1)}, bf16[256,1024]{1,0:T(8,128)(2,1)S(1)}) custom-call(s32[2]{0:T(128)S(1)} %pad_add_fusion.4.place_ref, bf16[256,1024]{1,0:T(8,128)(2,1)S(1)} %get-tuple-element.80.gated_ref, bf16[1024,8192]{1,0:T(8,128)(2,1)} %w_ref.19, bf16[256,1024]{1,0:T(8,128)(2,1)S(1)} %get-tuple-element.89.refs_0_), custom_call_target="tpu_custom_call" | custom-call | flops 2000000 | bytes 200000 | tf_op jit(solution)/shard_map/pieces/pallas_call | solution.py:154
  163.3 4.4 %collective-permute-start.22 = (bf16[256,1024]{1,0:T(8,128)(2,1)S(1)}, bf16[256,1024]{1,0:T(8,128)(2,1)S(1)}, u32[]{:S(2)}, u32[]{:S(2)}) collective-permute-start(bf16[256,1024]{1,0:T(8,128)(2,1)S(1)} %add_convert_fusion.6), channel_id=1, source_target_pairs={{0,4},{2,6},{12,8},{14,10},{1,5},{3,7},{13,9},{15,11},{16,20},{18,... | collective-permute-start | bytes 1572872 | tf_op jit(solution)/shard_map/ppermute | solution.py:206
  168.5 3.7 %pieces.15 = (f32[256,1024]{1,0:T(8,128)S(1)}, bf16[256,1024]{1,0:T(8,128)(2,1)S(1)}) custom-call(s32[2]{0:T(128)S(1)} %pad_add_fusion.4.place_ref, bf16[256,1024]{1,0:T(8,128)(2,1)S(1)} %get-tuple-element.82.gated_ref, bf16[1024,8192]{1,0:T(8,128)(2,1)} %w_ref.19, bf16[256,1024]{1,0:T(8,128)(2,1)S(1)} %collective-permute-done.16.refs_0_), custom_call_target="tpu_custom_call" | custom-call | flops 2000000 | bytes 200000 | tf_op jit(solution)/shard_map/pieces/pallas_call | solution.py:154
  173.7 3.7 %pieces.16 = (f32[256,1024]{1,0:T(8,128)S(1)}, bf16[256,1024]{1,0:T(8,128)(2,1)S(1)}) custom-call(s32[2]{0:T(128)S(1)} %pad_add_fusion.3.place_ref, bf16[256,1024]{1,0:T(8,128)(2,1)S(1)} %get-tuple-element.80.gated_ref, bf16[1024,8192]{1,0:T(8,128)(2,1)} %w_ref.19, f32[256,1024]{1,0:T(8,128)S(1)} %get-tuple-element.87.refs_0_), custom_call_target="tpu_custom_call" | custom-call | flops 2000000 | bytes 200000 | tf_op jit(solution)/shard_map/pieces/pallas_call | solution.py:154
  177.4 3.7 %pieces.19 = (f32[256,1024]{1,0:T(8,128)S(1)}, bf16[256,1024]{1,0:T(8,128)(2,1)S(1)}) custom-call(s32[2]{0:T(128)S(1)} %pad_add_fusion.3.place_ref, bf16[256,1024]{1,0:T(8,128)(2,1)S(1)} %get-tuple-element.82.gated_ref, bf16[1024,8192]{1,0:T(8,128)(2,1)} %w_ref.19, bf16[256,1024]{1,0:T(8,128)(2,1)S(1)} %collective-permute-done.17.refs_0_), custom_call_target="tpu_custom_call" | custom-call | flops 2000000 | bytes 200000 | tf_op jit(solution)/shard_map/pieces/pallas_call | solution.py:154
  182.0 4.4 %collective-permute-start.30 = (bf16[256,1024]{1,0:T(8,128)(2,1)S(1)}, bf16[256,1024]{1,0:T(8,128)(2,1)S(1)}, u32[]{:S(2)}, u32[]{:S(2)}) collective-permute-start(bf16[256,1024]{1,0:T(8,128)(2,1)S(1)} %add_convert_fusion.2), channel_id=1, source_target_pairs={{0,4},{2,6},{12,8},{14,10},{1,5},{3,7},{13,9},{15,11},{16,20},{18,... | collective-permute-start | bytes 1572872 | tf_op jit(solution)/shard_map/ppermute | solution.py:206
  188.2 7.2 %collective-permute-done.25 = bf16[256,1024]{1,0:T(8,128)(2,1)S(1)} collective-permute-done((bf16[256,1024]{1,0:T(8,128)(2,1)S(1)}, bf16[256,1024]{1,0:T(8,128)(2,1)S(1)}, u32[]{:S(2)}, u32[]{:S(2)}) %collective-permute-start.25) | collective-permute-done | bytes 524320 | tf_op jit(solution)/shard_map/ppermute | solution.py:217
  197.7 2.5 %collective-permute-start.21 = (bf16[256,1024]{1,0:T(8,128)(2,1)S(1)}, bf16[256,1024]{1,0:T(8,128)(2,1)S(1)}, u32[]{:S(2)}, u32[]{:S(2)}) collective-permute-start(bf16[256,1024]{1,0:T(8,128)(2,1)S(1)} %add_convert_fusion.5), channel_id=1, source_target_pairs={{0,4},{2,6},{4,0},{6,2},{8,12},{10,14},{12,8},{14,10},{1,5},{3,7},... | collective-permute-start | bytes 1572872 | tf_op jit(solution)/shard_map/ppermute | solution.py:206
  201.4 14.6 %collective-permute-start.29 = (bf16[256,1024]{1,0:T(8,128)(2,1)S(1)}, bf16[256,1024]{1,0:T(8,128)(2,1)S(1)}, u32[]{:S(2)}, u32[]{:S(2)}) collective-permute-start(bf16[256,1024]{1,0:T(8,128)(2,1)S(1)} %add_convert_fusion.1), channel_id=1, source_target_pairs={{0,4},{2,6},{4,0},{6,2},{8,12},{10,14},{12,8},{14,10},{1,5},{3,7},... | collective-permute-start | bytes 1572872 | tf_op jit(solution)/shard_map/ppermute | solution.py:206
  215.9 2.3 %pieces.18 = f32[256,1024]{1,0:T(8,128)S(1)} custom-call(s32[1]{0:T(128)} %bitcast.place_ref, bf16[256,1024]{1,0:T(8,128)(2,1)S(1)} %get-tuple-element.82.gated_ref, bf16[1024,8192]{1,0:T(8,128)(2,1)} %w_ref.19, bf16[256,1024]{1,0:T(8,128)(2,1)S(1)} %collective-permute-done.15.refs_0_), custom_call_target="tpu_custom_call" | custom-call | flops 1000000 | bytes 100000 | tf_op jit(solution)/shard_map/pieces/pallas_call | solution.py:154
  218.2 2.4 %pieces.14 = f32[256,1024]{1,0:T(8,128)S(1)} custom-call(s32[1]{0:T(128)} %bitcast.place_ref, bf16[256,1024]{1,0:T(8,128)(2,1)S(1)} %get-tuple-element.80.gated_ref, bf16[1024,8192]{1,0:T(8,128)(2,1)} %w_ref.19, bf16[256,1024]{1,0:T(8,128)(2,1)S(1)} %collective-permute-done.15.refs_0_), custom_call_target="tpu_custom_call" | custom-call | flops 1000000 | bytes 100000 | tf_op jit(solution)/shard_map/pieces/pallas_call | solution.py:154
  221.0 2.3 %collective-permute-done.29.refs_6_ = bf16[256,1024]{1,0:T(8,128)(2,1)S(1)} collective-permute-done((bf16[256,1024]{1,0:T(8,128)(2,1)S(1)}, bf16[256,1024]{1,0:T(8,128)(2,1)S(1)}, u32[]{:S(2)}, u32[]{:S(2)}) %collective-permute-start.29) | collective-permute-done | bytes 524320 | tf_op jit(solution)/shard_map/ppermute | solution.py:206
  (95 shorter events, 41.8 us)
Async XLA Ops:
  0.0 26.5 %collective-permute-start = (bf16[512,1024]{1,0:T(8,128)(2,1)}, bf16[512,1024]{1,0:T(8,128)(2,1)}, u32[]{:S(2)}, u32[]{:S(2)}) collective-permute-start(bf16[512,1024]{1,0:T(8,128)(2,1)} %refs_0_.1), channel_id=1, source_target_pairs={{0,4},{2,6},{4,0},{6,2},{8,12},{10,14},{12,8},{14,10},{1,5},{3,7},... | collective-permute-start | bytes 3145736 | tf_op jit(solution)/shard_map/ppermute | solution.py:206
  3.0 25.1 %collective-permute-start.3 = (bf16[512,1024]{1,0:T(8,128)(2,1)}, bf16[512,1024]{1,0:T(8,128)(2,1)S(1)}, u32[]{:S(2)}, u32[]{:S(2)}) collective-permute-start(bf16[512,1024]{1,0:T(8,128)(2,1)} %refs_0_.1), channel_id=1, source_target_pairs={{4,8},{6,10},{8,4},{10,6},{5,9},{7,11},{9,5},{11,7},{20,24},{22,26... | collective-permute-start | bytes 3145736 | tf_op jit(solution)/shard_map/ppermute | solution.py:206
  3.7 25.7 %collective-permute-start.1 = (bf16[512,1024]{1,0:T(8,128)(2,1)}, bf16[512,1024]{1,0:T(8,128)(2,1)S(1)}, u32[]{:S(2)}, u32[]{:S(2)}) collective-permute-start(bf16[512,1024]{1,0:T(8,128)(2,1)} %refs_0_.1), channel_id=1, source_target_pairs={{0,2},{2,0},{4,6},{6,4},{8,10},{10,8},{12,14},{14,12},{1,3},{3,1},... | collective-permute-start | bytes 3145736 | tf_op jit(solution)/shard_map/ppermute | solution.py:217
  26.5 20.9 %collective-permute-start.5 = (bf16[512,1024]{1,0:T(8,128)(2,1)}, bf16[512,1024]{1,0:T(8,128)(2,1)}, u32[]{:S(2)}, u32[]{:S(2)}) collective-permute-start(bf16[512,1024]{1,0:T(8,128)(2,1)} %collective-permute-done.refs_1_), channel_id=1, source_target_pairs={{4,8},{6,10},{8,4},{10,6},{5,9},{7,11},{9,5},{11,7},{20,24},{22,26... | collective-permute-start | bytes 3145736 | tf_op jit(solution)/shard_map/ppermute | solution.py:206
  28.1 27.1 %collective-permute-start.4 = (bf16[512,1024]{1,0:T(8,128)(2,1)S(1)}, bf16[512,1024]{1,0:T(8,128)(2,1)}, u32[]{:S(2)}, u32[]{:S(2)}) collective-permute-start(bf16[512,1024]{1,0:T(8,128)(2,1)S(1)} %collective-permute-done.3.refs_2_), channel_id=1, source_target_pairs={{4,0},{6,2},{8,12},{10,14},{5,1},{7,3},{9,13},{11,15},{20,16},{22,... | collective-permute-start | bytes 3145736 | tf_op jit(solution)/shard_map/ppermute | solution.py:206
  29.4 27.1 %collective-permute-start.2 = (bf16[512,1024]{1,0:T(8,128)(2,1)}, bf16[512,1024]{1,0:T(8,128)(2,1)}, u32[]{:S(2)}, u32[]{:S(2)}) collective-permute-start(bf16[512,1024]{1,0:T(8,128)(2,1)} %collective-permute-done.refs_1_), channel_id=1, source_target_pairs={{0,2},{2,0},{4,6},{6,4},{8,10},{10,8},{12,14},{14,12},{1,3},{3,1},... | collective-permute-start | bytes 3145736 | tf_op jit(solution)/shard_map/ppermute | solution.py:217
  47.4 30.2 %collective-permute-start.7 = (bf16[512,1024]{1,0:T(8,128)(2,1)}, bf16[512,1024]{1,0:T(8,128)(2,1)}, u32[]{:S(2)}, u32[]{:S(2)}) collective-permute-start(bf16[512,1024]{1,0:T(8,128)(2,1)} %collective-permute-done.5), channel_id=1, source_target_pairs={{4,0},{6,2},{8,12},{10,14},{5,1},{7,3},{9,13},{11,15},{20,16},{22,... | collective-permute-start | bytes 3145736 | tf_op jit(solution)/shard_map/ppermute | solution.py:206
  56.6 23.2 %collective-permute-start.6 = (bf16[512,1024]{1,0:T(8,128)(2,1)S(1)}, bf16[512,1024]{1,0:T(8,128)(2,1)}, u32[]{:S(2)}, u32[]{:S(2)}) collective-permute-start(bf16[512,1024]{1,0:T(8,128)(2,1)S(1)} %broadcast_select_fusion.refs_1_), channel_id=1, source_target_pairs={{0,2},{2,0},{4,6},{6,4},{8,10},{10,8},{12,14},{14,12},{1,3},{3,1},... | collective-permute-start | bytes 3145736 | tf_op jit(solution)/shard_map/ppermute | solution.py:217
  59.1 38.5 %collective-permute-start.10 = (bf16[512,512]{1,0:T(8,128)(2,1)}, bf16[512,512]{1,0:T(8,128)(2,1)S(1)}, u32[]{:S(2)}, u32[]{:S(2)}) collective-permute-start(bf16[512,512]{1,0:T(8,128)(2,1)} %slice.27), channel_id=1, source_target_pairs={{4,8},{6,10},{8,4},{10,6},{5,9},{7,11},{9,5},{11,7},{20,24},{22,26... | collective-permute-start | bytes 1572872 | tf_op jit(solution)/shard_map/ppermute | solution.py:206
  80.8 16.8 %collective-permute-start.9 = (bf16[512,512]{1,0:T(8,128)(2,1)S(1)}, bf16[512,512]{1,0:T(8,128)(2,1)S(1)}, u32[]{:S(2)}, u32[]{:S(2)}) collective-permute-start(bf16[512,512]{1,0:T(8,128)(2,1)S(1)} %slice.26), channel_id=1, source_target_pairs={{4,0},{6,2},{8,12},{10,14},{5,1},{7,3},{9,13},{11,15},{20,16},{22,... | collective-permute-start | bytes 1572872 | tf_op jit(solution)/shard_map/ppermute | solution.py:206
  82.1 15.5 %collective-permute-start.8 = (bf16[512,512]{1,0:T(8,128)(2,1)}, bf16[512,512]{1,0:T(8,128)(2,1)S(1)}, u32[]{:S(2)}, u32[]{:S(2)}) collective-permute-start(bf16[512,512]{1,0:T(8,128)(2,1)} %slice_select_fusion), channel_id=1, source_target_pairs={{0,2},{2,0},{4,6},{6,4},{8,10},{10,8},{12,14},{14,12},{1,3},{3,1},... | collective-permute-start | bytes 1572872 | tf_op jit(solution)/shard_map/ppermute | solution.py:217
  107.1 2.2 collective-permute-start.11
  120.6 3.2 %collective-permute-start.12 = (f32[16,8,128]{2,1,0:T(8,128)S(1)}, f32[16,8,128]{2,1,0:T(8,128)S(1)}, u32[]{:S(2)}, u32[]{:S(2)}) collective-permute-start(f32[16,8,128]{2,1,0:T(8,128)S(1)} %get-tuple-element.77), channel_id=1, source_target_pairs={{0,1},{2,3},{4,5},{6,7},{8,9},{10,11},{12,13},{14,15},{16,17},{18,... | collective-permute-start | bytes 196616 | tf_op jit(solution)/shard_map/ppermute | solution.py:19
  128.9 14.6 %collective-permute-start.14 = (bf16[256,1024]{1,0:T(8,128)(2,1)S(1)}, bf16[256,1024]{1,0:T(8,128)(2,1)S(1)}, u32[]{:S(2)}, u32[]{:S(2)}) collective-permute-start(bf16[256,1024]{1,0:T(8,128)(2,1)S(1)} %pieces.10.refs_0_), channel_id=1, source_target_pairs={{0,2},{2,0},{4,6},{6,4},{8,10},{10,8},{12,14},{14,12},{1,3},{3,1},... | collective-permute-start | bytes 1572872 | tf_op jit(solution)/shard_map/ppermute | solution.py:217
  135.0 17.1 %collective-permute-start.13 = (bf16[256,1024]{1,0:T(8,128)(2,1)S(1)}, bf16[256,1024]{1,0:T(8,128)(2,1)S(1)}, u32[]{:S(2)}, u32[]{:S(2)}) collective-permute-start(bf16[256,1024]{1,0:T(8,128)(2,1)S(1)} %pieces.11.refs_0_), channel_id=1, source_target_pairs={{0,4},{2,6},{12,8},{14,10},{1,5},{3,7},{13,9},{15,11},{16,20},{18,... | collective-permute-start | bytes 1572872 | tf_op jit(solution)/shard_map/ppermute | solution.py:206
  143.4 19.3 %collective-permute-start.17 = (bf16[256,1024]{1,0:T(8,128)(2,1)S(1)}, bf16[256,1024]{1,0:T(8,128)(2,1)S(1)}, u32[]{:S(2)}, u32[]{:S(2)}) collective-permute-start(bf16[256,1024]{1,0:T(8,128)(2,1)S(1)} %get-tuple-element.91.refs_0_), channel_id=1, source_target_pairs={{0,2},{2,0},{4,6},{6,4},{8,10},{10,8},{12,14},{14,12},{1,3},{3,1},... | collective-permute-start | bytes 1572872 | tf_op jit(solution)/shard_map/ppermute | solution.py:217
  145.2 17.9 %collective-permute-start.16 = (bf16[256,1024]{1,0:T(8,128)(2,1)S(1)}, bf16[256,1024]{1,0:T(8,128)(2,1)S(1)}, u32[]{:S(2)}, u32[]{:S(2)}) collective-permute-start(bf16[256,1024]{1,0:T(8,128)(2,1)S(1)} %add_convert_fusion.7), channel_id=1, source_target_pairs={{0,4},{2,6},{12,8},{14,10},{1,5},{3,7},{13,9},{15,11},{16,20},{18,... | collective-permute-start | bytes 1572872 | tf_op jit(solution)/shard_map/ppermute | solution.py:206
  152.3 19.9 %collective-permute-start.15 = (bf16[256,1024]{1,0:T(8,128)(2,1)S(1)}, bf16[256,1024]{1,0:T(8,128)(2,1)S(1)}, u32[]{:S(2)}, u32[]{:S(2)}) collective-permute-start(bf16[256,1024]{1,0:T(8,128)(2,1)S(1)} %add_convert_fusion.8), channel_id=1, source_target_pairs={{0,2},{2,0},{4,6},{6,4},{8,10},{10,8},{12,14},{14,12},{1,3},{3,1},... | collective-permute-start | bytes 1572872 | tf_op jit(solution)/shard_map/ppermute | solution.py:217
  153.9 27.2 %collective-permute-start.27 = (bf16[256,1024]{1,0:T(8,128)(2,1)S(1)}, bf16[256,1024]{1,0:T(8,128)(2,1)S(1)}, u32[]{:S(2)}, u32[]{:S(2)}) collective-permute-start(bf16[256,1024]{1,0:T(8,128)(2,1)S(1)} %get-tuple-element.89.refs_0_), channel_id=1, source_target_pairs={{0,4},{2,6},{12,8},{14,10},{1,5},{3,7},{13,9},{15,11},{16,20},{18,... | collective-permute-start | bytes 1572872 | tf_op jit(solution)/shard_map/ppermute | solution.py:206
  158.2 23.8 %collective-permute-start.24 = (bf16[256,1024]{1,0:T(8,128)(2,1)S(1)}, bf16[256,1024]{1,0:T(8,128)(2,1)S(1)}, u32[]{:S(2)}, u32[]{:S(2)}) collective-permute-start(bf16[256,1024]{1,0:T(8,128)(2,1)S(1)} %pieces.11.refs_0_), channel_id=1, source_target_pairs={{4,8},{6,10},{8,4},{10,6},{5,9},{7,11},{9,5},{11,7},{20,24},{22,26... | collective-permute-start | bytes 1572872 | tf_op jit(solution)/shard_map/ppermute | solution.py:206
  163.3 23.2 %collective-permute-start.22 = (bf16[256,1024]{1,0:T(8,128)(2,1)S(1)}, bf16[256,1024]{1,0:T(8,128)(2,1)S(1)}, u32[]{:S(2)}, u32[]{:S(2)}) collective-permute-start(bf16[256,1024]{1,0:T(8,128)(2,1)S(1)} %add_convert_fusion.6), channel_id=1, source_target_pairs={{0,4},{2,6},{12,8},{14,10},{1,5},{3,7},{13,9},{15,11},{16,20},{18,... | collective-permute-start | bytes 1572872 | tf_op jit(solution)/shard_map/ppermute | solution.py:206
  167.8 29.3 %collective-permute-start.20 = (bf16[256,1024]{1,0:T(8,128)(2,1)S(1)}, bf16[256,1024]{1,0:T(8,128)(2,1)S(1)}, u32[]{:S(2)}, u32[]{:S(2)}) collective-permute-start(bf16[256,1024]{1,0:T(8,128)(2,1)S(1)} %add_convert_fusion.6), channel_id=1, source_target_pairs={{4,8},{6,10},{8,4},{10,6},{5,9},{7,11},{9,5},{11,7},{20,24},{22,26... | collective-permute-start | bytes 1572872 | tf_op jit(solution)/shard_map/ppermute | solution.py:206
  172.2 15.3 %collective-permute-start.18 = (bf16[256,1024]{1,0:T(8,128)(2,1)S(1)}, bf16[256,1024]{1,0:T(8,128)(2,1)S(1)}, u32[]{:S(2)}, u32[]{:S(2)}) collective-permute-start(bf16[256,1024]{1,0:T(8,128)(2,1)S(1)} %get-tuple-element.92), channel_id=1, source_target_pairs={{0,2},{2,0},{4,6},{6,4},{8,10},{10,8},{12,14},{14,12},{1,3},{3,1},... | collective-permute-start | bytes 1572872 | tf_op jit(solution)/shard_map/ppermute | solution.py:217
  181.1 14.2 %collective-permute-start.25 = (bf16[256,1024]{1,0:T(8,128)(2,1)S(1)}, bf16[256,1024]{1,0:T(8,128)(2,1)S(1)}, u32[]{:S(2)}, u32[]{:S(2)}) collective-permute-start(bf16[256,1024]{1,0:T(8,128)(2,1)S(1)} %get-tuple-element.98), channel_id=1, source_target_pairs={{0,2},{2,0},{4,6},{6,4},{8,10},{10,8},{12,14},{14,12},{1,3},{3,1},... | collective-permute-start | bytes 1572872 | tf_op jit(solution)/shard_map/ppermute | solution.py:217
  182.0 15.7 %collective-permute-start.30 = (bf16[256,1024]{1,0:T(8,128)(2,1)S(1)}, bf16[256,1024]{1,0:T(8,128)(2,1)S(1)}, u32[]{:S(2)}, u32[]{:S(2)}) collective-permute-start(bf16[256,1024]{1,0:T(8,128)(2,1)S(1)} %add_convert_fusion.2), channel_id=1, source_target_pairs={{0,4},{2,6},{12,8},{14,10},{1,5},{3,7},{13,9},{15,11},{16,20},{18,... | collective-permute-start | bytes 1572872 | tf_op jit(solution)/shard_map/ppermute | solution.py:206
  186.6 13.8 %collective-permute-start.28 = (bf16[256,1024]{1,0:T(8,128)(2,1)S(1)}, bf16[256,1024]{1,0:T(8,128)(2,1)S(1)}, u32[]{:S(2)}, u32[]{:S(2)}) collective-permute-start(bf16[256,1024]{1,0:T(8,128)(2,1)S(1)} %add_convert_fusion.2), channel_id=1, source_target_pairs={{4,8},{6,10},{8,4},{10,6},{5,9},{7,11},{9,5},{11,7},{20,24},{22,26... | collective-permute-start | bytes 1572872 | tf_op jit(solution)/shard_map/ppermute | solution.py:206
  187.5 13.8 %collective-permute-start.23 = (bf16[256,1024]{1,0:T(8,128)(2,1)S(1)}, bf16[256,1024]{1,0:T(8,128)(2,1)S(1)}, u32[]{:S(2)}, u32[]{:S(2)}) collective-permute-start(bf16[256,1024]{1,0:T(8,128)(2,1)S(1)} %add_convert_fusion.4), channel_id=1, source_target_pairs={{4,8},{6,10},{8,4},{10,6},{5,9},{7,11},{9,5},{11,7},{20,24},{22,26... | collective-permute-start | bytes 1572872 | tf_op jit(solution)/shard_map/ppermute | solution.py:206
  195.4 25.6 %collective-permute-start.26 = (bf16[256,1024]{1,0:T(8,128)(2,1)S(1)}, bf16[256,1024]{1,0:T(8,128)(2,1)S(1)}, u32[]{:S(2)}, u32[]{:S(2)}) collective-permute-start(bf16[256,1024]{1,0:T(8,128)(2,1)S(1)} %add_convert_fusion.3), channel_id=1, source_target_pairs={{0,2},{2,0},{4,6},{6,4},{8,10},{10,8},{12,14},{14,12},{1,3},{3,1},... | collective-permute-start | bytes 1572872 | tf_op jit(solution)/shard_map/ppermute | solution.py:217
  197.1 23.9 %collective-permute-start.19 = (bf16[256,1024]{1,0:T(8,128)(2,1)S(1)}, bf16[256,1024]{1,0:T(8,128)(2,1)S(1)}, u32[]{:S(2)}, u32[]{:S(2)}) collective-permute-start(bf16[256,1024]{1,0:T(8,128)(2,1)S(1)} %get-tuple-element.93), channel_id=1, source_target_pairs={{0,2},{2,0},{4,6},{6,4},{8,10},{10,8},{12,14},{14,12},{1,3},{3,1},... | collective-permute-start | bytes 1572872 | tf_op jit(solution)/shard_map/ppermute | solution.py:217
  197.7 23.3 %collective-permute-start.21 = (bf16[256,1024]{1,0:T(8,128)(2,1)S(1)}, bf16[256,1024]{1,0:T(8,128)(2,1)S(1)}, u32[]{:S(2)}, u32[]{:S(2)}) collective-permute-start(bf16[256,1024]{1,0:T(8,128)(2,1)S(1)} %add_convert_fusion.5), channel_id=1, source_target_pairs={{0,4},{2,6},{4,0},{6,2},{8,12},{10,14},{12,8},{14,10},{1,5},{3,7},... | collective-permute-start | bytes 1572872 | tf_op jit(solution)/shard_map/ppermute | solution.py:206
  200.4 20.6 %collective-permute-start.31 = (bf16[256,1024]{1,0:T(8,128)(2,1)S(1)}, bf16[256,1024]{1,0:T(8,128)(2,1)S(1)}, u32[]{:S(2)}, u32[]{:S(2)}) collective-permute-start(bf16[256,1024]{1,0:T(8,128)(2,1)S(1)} %add_convert_fusion), channel_id=1, source_target_pairs={{4,8},{6,10},{8,4},{10,6},{5,9},{7,11},{9,5},{11,7},{20,24},{22,26... | collective-permute-start | bytes 1572872 | tf_op jit(solution)/shard_map/ppermute | solution.py:206
  201.4 21.9 %collective-permute-start.29 = (bf16[256,1024]{1,0:T(8,128)(2,1)S(1)}, bf16[256,1024]{1,0:T(8,128)(2,1)S(1)}, u32[]{:S(2)}, u32[]{:S(2)}) collective-permute-start(bf16[256,1024]{1,0:T(8,128)(2,1)S(1)} %add_convert_fusion.1), channel_id=1, source_target_pairs={{0,4},{2,6},{4,0},{6,2},{8,12},{10,14},{12,8},{14,10},{1,5},{3,7},... | collective-permute-start | bytes 1572872 | tf_op jit(solution)/shard_map/ppermute | solution.py:206
  (10 other events, 142.5 us)

commit v2 on v1

--- a/solution.py
+++ b/solution.py
@@ -49,7 +49,7 @@
             x = chunk_refs[at][...]
             at += 1
             if pairs[j]:
-                x = jnp.where(place_ref[len(depths)] == 1, x, chunk_refs[at][...])
+                x = jnp.where(place_ref[place_ref.shape[0] - 1] == 1, x, chunk_refs[at][...])
                 at += 1
             x = x.astype(jnp.float32)
             parts = [x[:, g : g + LANES] * x[:, g : g + LANES] for g in range(0, depth, LANES)]
@@ -78,7 +78,7 @@
         rim_ref[0] = (rim * sq_ref[rows - keep :, :1]).astype(jnp.bfloat16).astype(jnp.float32)
 
 
-def accumulate(chunks, places, gain, in_weight, acc=None, square=None, parts=None, use_first=None):
+def accumulate(table, chunks, places, gain, in_weight, acc=None, square=None, parts=None):
     pairs = [isinstance(c, tuple) for c in chunks]
     arrays = [a for c in chunks for a in (c if isinstance(c, tuple) else (c,))]
     depths = [(c[0] if isinstance(c, tuple) else c).shape[1] for c in chunks]
@@ -88,8 +88,12 @@
     acc_spec = pl.BlockSpec((1, rows, tile), lambda i, c, p: (i, 0, c))
     sq_spec = pl.BlockSpec((rows, LANES), lambda i, c, p: (0, 0))
     in_specs = [pl.BlockSpec(a.shape, lambda i, c, p: (0, 0)) for a in arrays]
-    in_specs += [pl.BlockSpec((1, 1, d), lambda i, c, p, j=j: (p[j], 0, 0)) for j, d in enumerate(depths)]
-    in_specs += [pl.BlockSpec((1, d, tile), lambda i, c, p, j=j: (i, p[j], c)) for j, d in enumerate(depths)]
+    for d, (k, per_shard, part) in zip(depths, places):
+        place = lambda p, k=k, n=per_shard, part=part: p[k] * n + part
+        in_specs.append(pl.BlockSpec((1, 1, d), lambda i, c, p, place=place: (place(p), 0, 0)))
+    for d, (k, per_shard, part) in zip(depths, places):
+        place = lambda p, k=k, n=per_shard, part=part: p[k] * n + part
+        in_specs.append(pl.BlockSpec((1, d, tile), lambda i, c, p, place=place: (i, place(p), c)))
     out_specs = [acc_spec, sq_spec]
     out_shape = [
         jax.ShapeDtypeStruct((3, rows, chans), jnp.float32),
@@ -107,7 +111,6 @@
         in_specs += [pl.BlockSpec((1, KEEP, tile), lambda i, c, p: (i, rows // KEEP - 1, c))] * len(parts)
         out_specs.append(pl.BlockSpec((1, KEEP, tile), lambda i, c, p: (i, 0, c)))
         out_shape.append(jax.ShapeDtypeStruct((3, KEEP, chans), jnp.float32))
-    scalars = list(places) + ([] if use_first is None else [use_first])
     part_count = None if parts is None else len(parts)
     return pl.pallas_call(
         functools.partial(
@@ -130,7 +133,7 @@
         ),
         name="accumulate",
     )(
-        jnp.stack([jnp.asarray(n, jnp.int32) for n in scalars]),
+        table,
         *arrays,
         *[gain.reshape(-1, 1, d) for d in depths],
         *[in_weight] * len(depths),
@@ -148,9 +151,16 @@
             outs[j][...] = total.astype(outs[j].dtype)
 
 
-def pieces(out_weight, gated, wanted, *earlier):
+def pieces(table, out_weight, gated, wanted, *earlier):
     rows, chans = gated.shape
     count = len(wanted)
+
+    def place(t, p):
+        shard = p[wanted[0][0]]
+        for j in range(1, count):
+            shard = jnp.where(t == j, p[wanted[j][0]], shard)
+        return shard
+
     out = pl.pallas_call(
         functools.partial(pieces_kernel, count),
         grid_spec=pltpu.PrefetchScalarGridSpec(
@@ -158,16 +168,16 @@
             grid=(count,),
             in_specs=[
                 pl.BlockSpec((rows, chans), lambda t, p: (0, 0)),
-                pl.BlockSpec((chans, chans), lambda t, p: (0, p[t])),
+                pl.BlockSpec((chans, chans), lambda t, p: (0, place(t, p))),
             ]
             + [pl.BlockSpec(memory_space=pl.ANY)] * len(earlier),
             out_specs=[pl.BlockSpec((rows, chans), lambda t, p: (0, 0))] * count,
         ),
-        out_shape=[jax.ShapeDtypeStruct((rows, chans), dtype) for place, dtype in wanted],
+        out_shape=[jax.ShapeDtypeStruct((rows, chans), dtype) for k, dtype in wanted],
         compiler_params=pltpu.CompilerParams(vmem_limit_bytes=VMEM_LIMIT),
         cost_estimate=pl.CostEstimate(flops=count * 1000000, bytes_accessed=count * 100000, transcendentals=0),
         name="pieces",
-    )(jnp.stack([place.astype(jnp.int32) for place, dtype in wanted]), gated, out_weight, *earlier)
+    )(table, gated, out_weight, *earlier)
     return list(out)
 
 
@@ -227,51 +237,45 @@
 INWARD = [(0, 1), (3, 2)]
 
 
-def gather_and_project(tokens, gain, in_weight, params):
+def gather_and_project(table, tokens, gain, in_weight, params):
     me = lax.axis_index("chan")
     half = tokens.shape[1] // 2
     at_end = (me < 2) | (me >= 6)
+    whole = lambda k: (k, 1, 0)
     own_over = across(tokens)
     next_one = along_line(tokens, PAIRS)
     middle = along_line(tokens, MIDDLE)
-    acc, square = accumulate([tokens], [me], gain, in_weight)
+    acc, square = accumulate(table, [tokens], [whole(0)], gain, in_weight)
     next_over = across(next_one, own_over, square)
     second_out = along_line(after(middle, square), OUTWARD)
     second_mid = along_line(after(next_one, square), MIDDLE)
     square, *params = lax.optimization_barrier((square, *params))
-    acc, square = accumulate([own_over, next_one], [me ^ 1, me ^ 2], gain, in_weight, acc, square)
+    acc, square = accumulate(table, [own_over, next_one], [whole(1), whole(2)], gain, in_weight, acc, square)
     second = jnp.where(at_end, second_out, second_mid)
     second_over = across(second, next_over, square)
     third_out = along_line(after(second_mid, square), OUTWARD)
     rest_mid = along_line(after(own_over[:, half:], second_mid, square), MIDDLE)
-    acc, square = accumulate([next_over, second], [me ^ 3, me ^ 4], gain, in_weight, acc, square)
+    acc, square = accumulate(table, [next_over, second], [whole(3), whole(4)], gain, in_weight, acc, square)
     third_over = across(jnp.where(at_end, third_out[:, :half], middle[:, :half]), second_over, square)
     rest_out = along_line(after(second_over[:, half:], square), OUTWARD)
     third = (third_out, middle)
     more, square = accumulate(
-        [second_over, third], [me ^ 5, me ^ 6], gain, in_weight, None, square, use_first=at_end
+        table, [second_over, third], [whole(5), whole(6)], gain, in_weight, None, square
     )
-    place = (me ^ 7) * 2
+    last = [third_over, (rest_out, rest_mid)]
+    places = [(7, 2, 0), (7, 2, 1)]
     rest, inv_rms, rim = accumulate(
-        [third_over, (rest_out, rest_mid)],
-        [place, place + 1],
-        gain,
-        in_weight,
-        None,
-        square,
-        [acc, more],
-        use_first=at_end,
+        table, last, places, gain, in_weight, None, square, [acc, more]
     )
     return [acc, more, rest], inv_rms, rim, params
 
 
-def project_and_reduce(upper, lower, out_weight, tokens):
-    me = lax.axis_index("chan")
+def project_and_reduce(table, upper, lower, out_weight, tokens):
     half = tokens.shape[0] // 2
-    send = lambda k: (me ^ (2 * k + 1), jnp.bfloat16)
-    keep = lambda k: (me ^ (2 * k), jnp.float32)
+    send = lambda k: (2 * k + 1, jnp.bfloat16)
+    keep = lambda k: (2 * k, jnp.float32)
     narrow = lambda a: a.astype(jnp.bfloat16)
-    make = functools.partial(pieces, out_weight)
+    make = functools.partial(pieces, table, out_weight)
     both = (0, 1)
 
     third_send_0 = make(upper, [send(3)])[0]
@@ -281,7 +285,7 @@
     rest_in = along_line(third_send_1, INWARD)
     rest_mid = along_line(third_send_1, MIDDLE)
     second_send_0, third_keep_0 = make(upper, [send(2), keep(3)], third_send_1)
-    second_send_1, third_1 = make(lower, [send(2), (keep(3)[0], jnp.bfloat16)], second_send_0)
+    second_send_1, third_1 = make(lower, [send(2), (keep(3)[0], jnp.bfloat16)], third_over)
     third = [narrow(total(third_keep_0, third_over)), third_1]
     third_in = [along_line(third[h], INWARD) for h in both]
     second_send = [second_send_0, narrow(total(second_send_1, rest_in))]
@@ -293,8 +297,8 @@
     second_in = [along_line(second[h], INWARD) for h in both]
     second_mid = [along_line(second[h], MIDDLE) for h in both]
     next_over = [across(later[h][1], second_over[h]) for h in both]
-    later_0 = make(upper, [keep(1), send(0)], later[1][0])
-    later = [later_0, make(lower, [keep(1), send(0)], second_over[0])]
+    later_0 = make(upper, [keep(1), send(0)], second_in[0])
+    later = [later_0, make(lower, [keep(1), send(0)], second[1])]
     own_send = [later[0][1], narrow(total(later[1][1], rest_mid))]
     next_one = [narrow(total(later[h][0], next_over[h], second_mid[h])) for h in both]
     next_in = [along_line(next_one[h], PAIRS) for h in both]
@@ -305,29 +309,42 @@
     return finish(*[[base[h], own_over[h], next_in[h], middle_in[h]] for h in both])
 
 
-def convolve_kernel(part_count, *refs):
+def convolve_kernel(part_count, after_rows, *refs):
     part_refs, refs = refs[:part_count], refs[part_count:]
-    rms_ref, rim_ref, taps_ref, decay_ref, q_ref, prod_ref, end_ref, win_ref, state_ref = refs
+    rms_ref, refs = refs[0], refs[1:]
+    taps_ref, decay_ref, refs = refs[0], refs[1], refs[2:]
+    own_rim = after_rows is None
+    if own_rim:
+        rim_refs, rim_rms_ref = refs[:part_count], refs[part_count]
+    else:
+        rim_ref, later_ref = refs[:2]
+    q_ref, prod_ref, end_ref, win_ref, state_ref = refs[-5:]
     step = pl.program_id(0)
     rows = q_ref.shape[0]
     tap_count, groups = taps_ref.shape[1:3]
     poles = decay_ref.shape[0]
-    keep = rim_ref.shape[1]
+    keep = win_ref.shape[1] // groups - rows
     unroll = 8
+
+    def rounded(sources, scale, i, g):
+        cols = tree_sum([ref[i, :, g * LANES : (g + 1) * LANES] for ref in sources]) * scale
+        return cols.astype(jnp.bfloat16).astype(jnp.float32)
 
     @pl.when(step == 0)
     def _():
         for g in range(groups):
             for i in range(3):
-                win_ref[i, pl.ds(g, keep, stride=groups), :] = rim_ref[i, :, g * LANES : (g + 1) * LANES]
+                if own_rim:
+                    rim = rounded(rim_refs, rim_rms_ref[:, :1], i, g)
+                else:
+                    rim = rim_ref[i, :, g * LANES : (g + 1) * LANES]
+                win_ref[i, pl.ds(g, keep, stride=groups), :] = rim
         state_ref[...] = jnp.zeros_like(state_ref)
 
     inv_rms = rms_ref[:, :1]
     for i in range(3):
         for g in range(groups):
-            cols = tree_sum([ref[i, :, g * LANES : (g + 1) * LANES] for ref in part_refs]) * inv_rms
-            cols = cols.astype(jnp.bfloat16).astype(jnp.float32)
-            win_ref[i, pl.ds(keep * groups + g, rows, stride=groups), :] = cols
+            win_ref[i, pl.ds(keep * groups + g, rows, stride=groups), :] = rounded(part_refs, inv_rms, i, g)
     decay = [jnp.exp(decay_ref[n]) for n in range(poles)]
 
     def row_of(i, t):
@@ -364,43 +381,56 @@
     @pl.when(step == pl.num_programs(0) - 1)
     def _():
         for n in range(poles):
-            end_ref[n] = state[n]
-
-
-def convolve(parts, inv_rms, rim, taps, log_decay):
+            if own_rim:
+                end_ref[n] = state[n]
+            else:
+                end_ref[n] = later_ref[n] + jnp.exp(float(after_rows) * decay_ref[n]) * state[n]
+
+
+def convolve(parts, inv_rms, taps, log_decay, rim=None, done=None):
     rows, chans = parts[0].shape[1:]
     groups = chans // LANES
     tap_count, poles = taps.shape[1], log_decay.shape[0]
-    keep = rim.shape[1]
-    blk = min(128, rows)
+    count = len(parts)
+    blk = min(128, rows // 2)
     whole = lambda *shape: pl.BlockSpec(shape, lambda t: (0,) * len(shape))
-    row_spec = pl.BlockSpec((blk, groups, LANES), lambda t: (t, 0, 0))
+    start = 1 if rim is None else 0
+    row_spec = pl.BlockSpec((blk, groups, LANES), lambda t: (t + start, 0, 0))
+    state_spec = whole(poles, groups, LANES)
+    in_specs = [pl.BlockSpec((3, blk, chans), lambda t: (0, t + start, 0))] * count
+    in_specs += [pl.BlockSpec((blk, LANES), lambda t: (t + start, 0)), whole(3, tap_count, groups, LANES), state_spec]
+    operands, aliases = [*parts, inv_rms, taps, log_decay], {}
+    if rim is None:
+        at = blk // KEEP - 1
+        in_specs += [pl.BlockSpec((3, KEEP, chans), lambda t: (0, at, 0))] * count
+        in_specs += [pl.BlockSpec((KEEP, LANES), lambda t: (at, 0))]
+        operands += [*parts, inv_rms]
+    else:
+        query, product, end = done
+        in_specs += [whole(3, KEEP, chans), state_spec] + [pl.BlockSpec(memory_space=pl.ANY)] * 2
+        operands += [rim, end, query, product]
+        aliases = {len(operands) - 2: 0, len(operands) - 1: 1}
     return pl.pallas_call(
-        functools.partial(convolve_kernel, len(parts)),
-        grid=(rows // blk,),
-        in_specs=[pl.BlockSpec((3, blk, chans), lambda t: (0, t, 0))] * len(parts)
-        + [
-            pl.BlockSpec((blk, LANES), lambda t: (t, 0)),
-            whole(3, keep, chans),
-            whole(3, tap_count, groups, LANES),
-            whole(poles, groups, LANES),
-        ],
-        out_specs=[row_spec, row_spec, whole(poles, groups, LANES)],
+        functools.partial(convolve_kernel, count, None if rim is None else rows - blk),
+        grid=(rows // blk - 1 if rim is None else 1,),
+        in_specs=in_specs,
+        out_specs=[row_spec, row_spec, state_spec],
         out_shape=[
             jax.ShapeDtypeStruct((rows, groups, LANES), jnp.float32),
             jax.ShapeDtypeStruct((rows, groups, LANES), jnp.float32),
             jax.ShapeDtypeStruct((poles, groups, LANES), jnp.float32),
         ],
         scratch_shapes=[
-            pltpu.VMEM((3, (keep + blk) * groups, LANES), jnp.float32),
+            pltpu.VMEM((3, (KEEP + blk) * groups, LANES), jnp.float32),
             pltpu.VMEM((poles, groups, LANES), jnp.float32),
         ],
+        input_output_aliases=aliases,
         compiler_params=pltpu.CompilerParams(vmem_limit_bytes=VMEM_LIMIT),
         cost_estimate=pl.CostEstimate(
-            flops=110 * rows * groups * LANES, bytes_accessed=20 * rows * groups * LANES, transcendentals=0
+            flops=80 * rows * groups * LANES, bytes_accessed=20 * rows * groups * LANES, transcendentals=0
         ),
         name="convolve",
-    )(*parts, inv_rms, rim, taps, log_decay)
+    )(*operands)
 
 
 def respond_kernel(q_ref, prod_ref, enter_ref, decay_ref, res_ref, skip_ref, *refs):
@@ -481,20 +511,26 @@
 
     paired_line = lax.axis_size("chan") == 8
     if paired_line:
+        me = lax.axis_index("chan")
+        at_end = ((me < 2) | (me >= 6)).astype(jnp.int32)
+        table = jnp.concatenate([me ^ jnp.arange(8, dtype=jnp.int32), at_end[None]])
         params = (taps, log_decay, residue, skip)
-        parts, inv_rms, rim, params = gather_and_project(tokens, norm_gain, in_weight, params)
+        parts, inv_rms, rim, params = gather_and_project(table, tokens, norm_gain, in_weight, params)
         taps, log_decay, residue, skip = params
     else:
         gathered = lax.all_gather(tokens, "chan", axis=1, tiled=True)
         depth = min(1024, gathered.shape[1])
         chunks = [gathered[:, k : k + depth] for k in range(0, gathered.shape[1], depth)]
+        table = jnp.arange(len(chunks), dtype=jnp.int32)
         acc = square = None
         for k, chunk in enumerate(chunks[:-1]):
-            acc, square = accumulate([chunk], [k], norm_gain, in_weight, acc, square)
-        acc, inv_rms, rim = accumulate(chunks[-1:], [len(chunks) - 1], norm_gain, in_weight, acc, square, [])
+            acc, square = accumulate(table, [chunk], [(k, 1, 0)], norm_gain, in_weight, acc, square)
+        places = [(len(chunks) - 1, 1, 0)]
+        acc, inv_rms, rim = accumulate(table, chunks[-1:], places, norm_gain, in_weight, acc, square, [])
         parts = [acc]
     rim = from_behind(rim, "seq", 1)
-    query, product, end = convolve(parts, inv_rms, rim, taps, log_decay)
+    done = convolve(parts, inv_rms, taps, log_decay)
+    query, product, end = convolve(parts, inv_rms, taps, log_decay, rim, done)
     shard_decay = jnp.exp(rows * log_decay)
     state, passing = jnp.zeros_like(end), end
     for _ in range(lax.axis_size("seq") - 1):
@@ -506,7 +542,7 @@
         half = rows // 2
         upper, state = respond(query, product, state, *filt, 0, half)
         lower = lambda *earlier: respond(query, product, state, *filt, half, half, *earlier)[0]
-        return project_and_reduce(upper, lower, out_weight, tokens)
+        return project_and_reduce(table, upper, lower, out_weight, tokens)
     gated = respond(query, product, state, *filt, 0, rows)[0]
     partial = jnp.dot(gated, out_weight, preferred_element_type=jnp.float32)
     branch = lax.psum_scatter(partial.astype(jnp.bfloat16), "chan", scatter_dimension=1, tiled=True)

time: 226 us -> 225 us (level)
  starting transfers between devices: 69.3 us -> 57.9 us
  waiting for transfers between devices: 31.7 us -> 40.3 us
  Pallas kernels: 112 us -> 116 us
    ppermute x19, starting transfers between devices: 51.4 us -> 40.8 us  [along_line(): lax.ppermute(block, 'chan', [(2 * a + y, 2 * b + y) for a, b in pairs for...]
    ppermute x11, waiting for transfers between devices: 7.46 us -> 13.9 us  [across(): return lax.ppermute(block, 'chan', [(c, c ^ 1) for c in range(count)])]
    ppermute x19, waiting for transfers between devices: 22.5 us -> 25.5 us  [along_line(): lax.ppermute(block, 'chan', [(2 * a + y, 2 * b + y) for a, b in pairs for...]
    pallas_call x1 -> x2, Pallas kernels: 11.3 us -> 13.8 us  [convolve(): pl.pallas_call(functools.partial(convolve_kernel, count, None if rim is N...]
  transfers between devices with their start and end apart: 32 -> 32, of which waited for: 9 -> 13; matrix products, arithmetic and copies ran while one was open for 4% -> 3% of each run, Pallas kernels for 38% -> 42%
where the time goes in v2:
time: 225 us; the launch traced here: 223 us
  Pallas kernels  116 us (52%)
  starting transfers between devices  57.9 us (26%)
  waiting for transfers between devices  40.3 us (18%)
  local copies, waits for them, and re-layouts  4.29 us (2%)
  other arithmetic  3.79 us (2%)
    pallas_call x5, Pallas kernels, accumulate(): pl.pallas_call(functools.partial(accumulate_kernel, depths, pairs, width,...  60.9 us
    ppermute x19, starting transfers between devices, along_line(): lax.ppermute(block, 'chan', [(2 * a + y, 2 * b + y) for a, b in pairs for...  40.8 us
    pallas_call x10, Pallas kernels, pieces(): pl.pallas_call(functools.partial(pieces_kernel, count), grid_spec=pltpu.P...  33.4 us
    ppermute x19, waiting for transfers between devices, along_line(): lax.ppermute(block, 'chan', [(2 * a + y, 2 * b + y) for a, b in pairs for...  25.5 us
    ppermute x11, starting transfers between devices, across(): return lax.ppermute(block, 'chan', [(c, c ^ 1) for c in range(count)])  14.5 us
    ppermute x11, waiting for transfers between devices, across(): return lax.ppermute(block, 'chan', [(c, c ^ 1) for c in range(count)])  13.9 us
    pallas_call x2, Pallas kernels, convolve(): pl.pallas_call(functools.partial(convolve_kernel, count, None if rim is N...  13.8 us
    pallas_call x2, Pallas kernels, respond(): pl.pallas_call(respond_kernel, grid=(rows // blk,), in_specs=[row_spec, r...  5.99 us
  transfers between devices with their start and end apart: 32, of which 13 were waited for; matrix products, arithmetic and copies ran while one was open for 3% of the time, Pallas kernels for 42%

profile of v2, /device:TPU:0, one launch (start us, length us, event | category | flops | bytes accessed | tf_op | source)
XLA Modules:
  0.0 222.7 jit_solution(12903927844070451128)
XLA Ops:
  0.0 3.0 %collective-permute-start = (bf16[512,1024]{1,0:T(8,128)(2,1)}, bf16[512,1024]{1,0:T(8,128)(2,1)S(1)}, u32[]{:S(2)}, u32[]{:S(2)}) collective-permute-start(bf16[512,1024]{1,0:T(8,128)(2,1)} %refs_0_.1), channel_id=1, source_target_pairs={{0,4},{2,6},{4,0},{6,2},{8,12},{10,14},{12,8},{14,10},{1,5},{3,7},... | collective-permute-start | bytes 3145736 | tf_op jit(solution)/shard_map/ppermute | solution.py:216
  7.4 9.4 %accumulate.5 = (f32[3,512,1024]{2,1,0:T(8,128)}, f32[512,128]{1,0:T(8,128)S(1)}) custom-call(s32[9]{0:T(128)S(1)} %pad_add_fusion.place_ref, bf16[512,1024]{1,0:T(8,128)(2,1)S(1)} %copy-done, f32[8,1,1024]{2,1,0:T(1,128)S(1)} %bitcast.8, bf16[3,8192,1024]{2,1,0:T(8,128)(2,1)} %refs_6_.3), custom_call_target="tpu_custom_call" | custom-call | flops 536870912 | bytes 6291456 | tf_op jit(solution)/shard_map/accumulate/pallas_call | solution.py:115
  16.8 9.6 %collective-permute-done.refs_1_ = bf16[512,1024]{1,0:T(8,128)(2,1)S(1)} collective-permute-done((bf16[512,1024]{1,0:T(8,128)(2,1)}, bf16[512,1024]{1,0:T(8,128)(2,1)S(1)}, u32[]{:S(2)}, u32[]{:S(2)}) %collective-permute-start) | collective-permute-done | bytes 1048608 | tf_op jit(solution)/shard_map/ppermute | solution.py:216
  33.3 14.2 %accumulate.6 = (f32[3,512,1024]{2,1,0:T(8,128)}, f32[512,128]{1,0:T(8,128)S(1)}) custom-call(s32[9]{0:T(128)S(1)} %pad_add_fusion.place_ref, bf16[512,1024]{1,0:T(8,128)(2,1)S(1)} %collective-permute-done.1.refs_0_, bf16[512,1024]{1,0:T(8,128)(2,1)S(1)} %collective-permute-done.refs_1_, ...), custom_call_target="tpu_custom_call", output_to_operand_aliasing={{0}: (7, {}), {1}: (8, {})} | custom-call | flops 1073741824 | bytes 12582912 | tf_op jit(solution)/shard_map/accumulate/pallas_call | solution.py:115
  48.8 6.6 %collective-permute-done.4 = bf16[512,1024]{1,0:T(8,128)(2,1)} collective-permute-done((bf16[512,1024]{1,0:T(8,128)(2,1)S(1)}, bf16[512,1024]{1,0:T(8,128)(2,1)}, u32[]{:S(2)}, u32[]{:S(2)}) %collective-permute-start.4) | collective-permute-done | bytes 1048608 | tf_op jit(solution)/shard_map/ppermute | solution.py:216
  59.0 14.8 %accumulate.7 = (f32[3,512,1024]{2,1,0:T(8,128)}, f32[512,128]{1,0:T(8,128)S(1)}) custom-call(s32[9]{0:T(128)S(1)} %pad_add_fusion.place_ref, bf16[512,1024]{1,0:T(8,128)(2,1)} %collective-permute-done.2.refs_0_, bf16[512,1024]{1,0:T(8,128)(2,1)S(1)} %broadcast_select_fusion.refs_1_, ...), custom_call_target="tpu_custom_call", output_to_operand_aliasing={{0}: (7, {}), {1}: (8, {})} | custom-call | flops 1073741824 | bytes 12582912 | tf_op jit(solution)/shard_map/accumulate/pallas_call | solution.py:115
  73.8 3.5 %collective-permute-done.7.refs_1_ = bf16[512,1024]{1,0:T(8,128)(2,1)S(1)} collective-permute-done((bf16[512,1024]{1,0:T(8,128)(2,1)}, bf16[512,1024]{1,0:T(8,128)(2,1)S(1)}, u32[]{:S(2)}, u32[]{:S(2)}) %collective-permute-start.7) | collective-permute-done | bytes 1048608 | tf_op jit(solution)/shard_map/ppermute | solution.py:216
  82.5 13.1 %accumulate.8 = (f32[3,512,1024]{2,1,0:T(8,128)}, f32[512,128]{1,0:T(8,128)S(1)}) custom-call(s32[9]{0:T(128)S(1)} %pad_add_fusion.place_ref, bf16[512,1024]{1,0:T(8,128)(2,1)S(1)} %collective-permute-done.6.refs_0_, bf16[512,1024]{1,0:T(8,128)(2,1)S(1)} %collective-permute-done.7.refs_1_, ...), custom_call_target="tpu_custom_call", output_to_operand_aliasing={{1}: (8, {})} | custom-call | flops 1073741824 | bytes 12582912 | tf_op jit(solution)/shard_map/accumulate/pallas_call | solution.py:115
  95.6 9.4 %accumulate.9 = (f32[3,512,1024]{2,1,0:T(8,128)}, f32[512,128]{1,0:T(8,128)S(1)}, f32[3,8,1024]{2,1,0:T(8,128)S(1)}) custom-call(s32[9]{0:T(128)S(1)} %pad_add_fusion.place_ref, bf16[512,512]{1,0:T(8,128)(2,1)S(1)} %collective-permute-done.8.refs_0_, bf16[512,512]{1,0:T(8,128)(2,1)S(1)} %collective-permute-done.9.refs_1_, ...), custom_call_target="tpu_custom_call", output_to_operand_aliasing={{1}: (8, {})} | custom-call | flops 536870912 | bytes 6291456 | tf_op jit(solution)/shard_map/accumulate/pallas_call | solution.py:115
  106.4 9.2 %convolve.2 = (f32[512,8,128]{2,1,0:T(8,128)S(1)}, f32[512,8,128]{2,1,0:T(8,128)S(1)}, f32[16,8,128]{2,1,0:T(8,128)S(1)}) custom-call(f32[3,512,1024]{2,1,0:T(8,128)} %get-tuple-element.64.refs_8_.refs_0_.refs_6_, f32[3,512,1024]{2,1,0:T(8,128)} %get-tuple-element.68.refs_9_.refs_1_.refs_7_, f32[3,512,1024]{2,1,0:T(8,128)} %get-tuple-element.73.refs_2_.refs_8_, ...), custom_call_target="tpu_custom_call" | custom-call | flops 41943040 | bytes 10485760 | tf_op jit(solution)/shard_map/convolve/pallas_call | solution.py:413
  115.6 4.6 %convolve.3 = (f32[512,8,128]{2,1,0:T(8,128)S(1)}, f32[512,8,128]{2,1,0:T(8,128)S(1)}, f32[16,8,128]{2,1,0:T(8,128)S(1)}) custom-call(f32[3,512,1024]{2,1,0:T(8,128)} %get-tuple-element.64.refs_8_.refs_0_.refs_6_, f32[3,512,1024]{2,1,0:T(8,128)} %get-tuple-element.68.refs_9_.refs_1_.refs_7_, ...), custom_call_target="tpu_custom_call", output_to_operand_aliasing={{0}: (8, {}), {1}: (9, {})} | custom-call | flops 41943040 | bytes 10485760 | tf_op jit(solution)/shard_map/convolve/pallas_call | solution.py:413
  122.4 2.7 %respond.2 = (bf16[256,1024]{1,0:T(8,128)(2,1)S(1)}, f32[16,8,128]{2,1,0:T(8,128)S(1)}) custom-call(f32[512,8,128]{2,1,0:T(8,128)S(1)} %get-tuple-element.81.q_ref, f32[512,8,128]{2,1,0:T(8,128)S(1)} %get-tuple-element.82.prod_ref, f32[16,8,128]{2,1,0:T(8,128)S(1)} %collective-permute-done.12.enter_ref, f32[16,8,128]{2,1,0:T(8,128)S(1)} %bitcast.19, ...), custom_call_target="tpu_custom_call" | custom-call | flops 18350080 | bytes 20971520 | tf_op jit(solution)/shard_map/respond/pallas_call | solution.py:481
  125.1 2.8 %pieces.10.refs_0_ = bf16[256,1024]{1,0:T(8,128)(2,1)S(1)} custom-call(s32[9]{0:T(128)S(1)} %pad_add_fusion.place_ref, bf16[256,1024]{1,0:T(8,128)(2,1)S(1)} %get-tuple-element.86.gated_ref, bf16[1024,8192]{1,0:T(8,128)(2,1)} %w_ref.19), custom_call_target="tpu_custom_call" | custom-call | flops 1000000 | bytes 100000 | tf_op jit(solution)/shard_map/pieces/pallas_call | solution.py:164
  128.5 3.3 %respond.3 = (bf16[256,1024]{1,0:T(8,128)(2,1)S(1)}, f32[16,8,128]{2,1,0:T(8,128)}) custom-call(f32[512,8,128]{2,1,0:T(8,128)S(1)} %get-tuple-element.81.q_ref, f32[512,8,128]{2,1,0:T(8,128)S(1)} %get-tuple-element.82.prod_ref, f32[16,8,128]{2,1,0:T(8,128)S(1)} %get-tuple-element.87.enter_ref, f32[16,8,128]{2,1,0:T(8,128)S(1)} %bitcast.20, ...), custom_call_target="tpu_custom_call" | custom-call | flops 18350080 | bytes 20971520 | tf_op jit(solution)/shard_map/respond/pallas_call | solution.py:481
  131.8 2.8 %pieces.12.refs_0_ = bf16[256,1024]{1,0:T(8,128)(2,1)S(1)} custom-call(s32[9]{0:T(128)S(1)} %pad_add_fusion.place_ref, bf16[256,1024]{1,0:T(8,128)(2,1)S(1)} %get-tuple-element.88.gated_ref, bf16[1024,8192]{1,0:T(8,128)(2,1)} %w_ref.19), custom_call_target="tpu_custom_call" | custom-call | flops 1000000 | bytes 100000 | tf_op jit(solution)/shard_map/pieces/pallas_call | solution.py:164
  134.6 4.6 %collective-permute-start.14 = (bf16[256,1024]{1,0:T(8,128)(2,1)S(1)}, bf16[256,1024]{1,0:T(8,128)(2,1)S(1)}, u32[]{:S(2)}, u32[]{:S(2)}) collective-permute-start(bf16[256,1024]{1,0:T(8,128)(2,1)S(1)} %pieces.12.refs_0_), channel_id=1, source_target_pairs={{0,4},{2,6},{12,8},{14,10},{1,5},{3,7},{13,9},{15,11},{16,20},{18,... | collective-permute-start | bytes 1572872 | tf_op jit(solution)/shard_map/ppermute | solution.py:216
  139.3 3.7 %pieces.15 = (bf16[256,1024]{1,0:T(8,128)(2,1)S(1)}, f32[256,1024]{1,0:T(8,128)S(1)}) custom-call(s32[9]{0:T(128)S(1)} %pad_add_fusion.place_ref, bf16[256,1024]{1,0:T(8,128)(2,1)S(1)} %get-tuple-element.86.gated_ref, bf16[1024,8192]{1,0:T(8,128)(2,1)} %w_ref.19, bf16[256,1024]{1,0:T(8,128)(2,1)S(1)} %pieces.12.refs_0_), custom_call_target="tpu_custom_call" | custom-call | flops 2000000 | bytes 200000 | tf_op jit(solution)/shard_map/pieces/pallas_call | solution.py:164
  143.1 4.0 %collective-permute-start.17 = (bf16[256,1024]{1,0:T(8,128)(2,1)S(1)}, bf16[256,1024]{1,0:T(8,128)(2,1)S(1)}, u32[]{:S(2)}, u32[]{:S(2)}) collective-permute-start(bf16[256,1024]{1,0:T(8,128)(2,1)S(1)} %add_convert_fusion.7), channel_id=1, source_target_pairs={{0,4},{2,6},{12,8},{14,10},{1,5},{3,7},{13,9},{15,11},{16,20},{18,... | collective-permute-start | bytes 1572872 | tf_op jit(solution)/shard_map/ppermute | solution.py:216
  147.7 3.7 %pieces.11 = (bf16[256,1024]{1,0:T(8,128)(2,1)S(1)}, bf16[256,1024]{1,0:T(8,128)(2,1)S(1)}) custom-call(s32[9]{0:T(128)S(1)} %pad_add_fusion.place_ref, bf16[256,1024]{1,0:T(8,128)(2,1)S(1)} %get-tuple-element.88.gated_ref, bf16[1024,8192]{1,0:T(8,128)(2,1)} %w_ref.19, bf16[256,1024]{1,0:T(8,128)(2,1)S(1)} %collective-permute-done.13.refs_0_), custom_call_target="tpu_custom_call" | custom-call | flops 2000000 | bytes 200000 | tf_op jit(solution)/shard_map/pieces/pallas_call | solution.py:164
  153.3 4.4 %collective-permute-start.24 = (bf16[256,1024]{1,0:T(8,128)(2,1)S(1)}, bf16[256,1024]{1,0:T(8,128)(2,1)S(1)}, u32[]{:S(2)}, u32[]{:S(2)}) collective-permute-start(bf16[256,1024]{1,0:T(8,128)(2,1)S(1)} %get-tuple-element.91.refs_0_), channel_id=1, source_target_pairs={{0,4},{2,6},{12,8},{14,10},{1,5},{3,7},{13,9},{15,11},{16,20},{18,... | collective-permute-start | bytes 1572872 | tf_op jit(solution)/shard_map/ppermute | solution.py:216
  158.4 3.7 %pieces.14 = (f32[256,1024]{1,0:T(8,128)S(1)}, bf16[256,1024]{1,0:T(8,128)(2,1)S(1)}) custom-call(s32[9]{0:T(128)S(1)} %pad_add_fusion.place_ref, bf16[256,1024]{1,0:T(8,128)(2,1)S(1)} %get-tuple-element.86.gated_ref, bf16[1024,8192]{1,0:T(8,128)(2,1)} %w_ref.19, bf16[256,1024]{1,0:T(8,128)(2,1)S(1)} %get-tuple-element.91.refs_0_), custom_call_target="tpu_custom_call" | custom-call | flops 2000000 | bytes 200000 | tf_op jit(solution)/shard_map/pieces/pallas_call | solution.py:164
  163.7 7.5 %collective-permute-start.18 = (bf16[256,1024]{1,0:T(8,128)(2,1)S(1)}, bf16[256,1024]{1,0:T(8,128)(2,1)S(1)}, u32[]{:S(2)}, u32[]{:S(2)}) collective-permute-start(bf16[256,1024]{1,0:T(8,128)(2,1)S(1)} %add_convert_fusion.6), channel_id=1, source_target_pairs={{0,4},{2,6},{12,8},{14,10},{1,5},{3,7},{13,9},{15,11},{16,20},{18,... | collective-permute-start | bytes 1572872 | tf_op jit(solution)/shard_map/ppermute | solution.py:216
  171.2 3.7 %pieces.18 = (f32[256,1024]{1,0:T(8,128)S(1)}, bf16[256,1024]{1,0:T(8,128)(2,1)S(1)}) custom-call(s32[9]{0:T(128)S(1)} %pad_add_fusion.place_ref, bf16[256,1024]{1,0:T(8,128)(2,1)S(1)} %get-tuple-element.88.gated_ref, bf16[1024,8192]{1,0:T(8,128)(2,1)} %w_ref.19, bf16[256,1024]{1,0:T(8,128)(2,1)S(1)} %collective-permute-done.17.refs_0_), custom_call_target="tpu_custom_call" | custom-call | flops 2000000 | bytes 200000 | tf_op jit(solution)/shard_map/pieces/pallas_call | solution.py:164
  178.7 3.7 %pieces.19 = (f32[256,1024]{1,0:T(8,128)S(1)}, bf16[256,1024]{1,0:T(8,128)(2,1)S(1)}) custom-call(s32[9]{0:T(128)S(1)} %pad_add_fusion.place_ref, bf16[256,1024]{1,0:T(8,128)(2,1)S(1)} %get-tuple-element.88.gated_ref, bf16[1024,8192]{1,0:T(8,128)(2,1)} %w_ref.19, bf16[256,1024]{1,0:T(8,128)(2,1)S(1)} %add_convert_fusion.3.refs_0_), custom_call_target="tpu_custom_call" | custom-call | flops 2000000 | bytes 200000 | tf_op jit(solution)/shard_map/pieces/pallas_call | solution.py:164
  186.7 3.7 %pieces.16 = (f32[256,1024]{1,0:T(8,128)S(1)}, bf16[256,1024]{1,0:T(8,128)(2,1)S(1)}) custom-call(s32[9]{0:T(128)S(1)} %pad_add_fusion.place_ref, bf16[256,1024]{1,0:T(8,128)(2,1)S(1)} %get-tuple-element.86.gated_ref, bf16[1024,8192]{1,0:T(8,128)(2,1)} %w_ref.19, bf16[256,1024]{1,0:T(8,128)(2,1)S(1)} %collective-permute-done.18.refs_0_), custom_call_target="tpu_custom_call" | custom-call | flops 2000000 | bytes 200000 | tf_op jit(solution)/shard_map/pieces/pallas_call | solution.py:164
  191.2 2.6 %collective-permute-start.22 = (bf16[256,1024]{1,0:T(8,128)(2,1)S(1)}, bf16[256,1024]{1,0:T(8,128)(2,1)S(1)}, u32[]{:S(2)}, u32[]{:S(2)}) collective-permute-start(bf16[256,1024]{1,0:T(8,128)(2,1)S(1)} %add_convert_fusion.5), channel_id=1, source_target_pairs={{0,4},{2,6},{4,0},{6,2},{8,12},{10,14},{12,8},{14,10},{1,5},{3,7},... | collective-permute-start | bytes 1572872 | tf_op jit(solution)/shard_map/ppermute | solution.py:216
  194.0 2.4 %collective-permute-done.30 = bf16[256,1024]{1,0:T(8,128)(2,1)S(1)} collective-permute-done((bf16[256,1024]{1,0:T(8,128)(2,1)S(1)}, bf16[256,1024]{1,0:T(8,128)(2,1)S(1)}, u32[]{:S(2)}, u32[]{:S(2)}) %collective-permute-start.30) | collective-permute-done | bytes 524320 | tf_op jit(solution)/shard_map/ppermute | solution.py:216
  197.3 2.7 %collective-permute-done.26 = bf16[256,1024]{1,0:T(8,128)(2,1)S(1)} collective-permute-done((bf16[256,1024]{1,0:T(8,128)(2,1)S(1)}, bf16[256,1024]{1,0:T(8,128)(2,1)S(1)}, u32[]{:S(2)}, u32[]{:S(2)}) %collective-permute-start.26) | collective-permute-done | bytes 524320 | tf_op jit(solution)/shard_map/ppermute | solution.py:227
  202.6 8.7 %collective-permute-done.20.refs_1_ = bf16[256,1024]{1,0:T(8,128)(2,1)S(1)} collective-permute-done((bf16[256,1024]{1,0:T(8,128)(2,1)S(1)}, bf16[256,1024]{1,0:T(8,128)(2,1)S(1)}, u32[]{:S(2)}, u32[]{:S(2)}) %collective-permute-start.20) | collective-permute-done | bytes 524320 | tf_op jit(solution)/shard_map/ppermute | solution.py:227
  211.3 2.5 %collective-permute-start.29 = (bf16[256,1024]{1,0:T(8,128)(2,1)S(1)}, bf16[256,1024]{1,0:T(8,128)(2,1)S(1)}, u32[]{:S(2)}, u32[]{:S(2)}) collective-permute-start(bf16[256,1024]{1,0:T(8,128)(2,1)S(1)} %add_convert_fusion.1), channel_id=1, source_target_pairs={{0,4},{2,6},{4,0},{6,2},{8,12},{10,14},{12,8},{14,10},{1,5},{3,7},... | collective-permute-start | bytes 1572872 | tf_op jit(solution)/shard_map/ppermute | solution.py:216
  213.8 2.8 %pieces.17 = f32[256,1024]{1,0:T(8,128)S(1)} custom-call(s32[9]{0:T(128)S(1)} %pad_add_fusion.place_ref, bf16[256,1024]{1,0:T(8,128)(2,1)S(1)} %get-tuple-element.88.gated_ref, bf16[1024,8192]{1,0:T(8,128)(2,1)} %w_ref.19, bf16[256,1024]{1,0:T(8,128)(2,1)S(1)} %collective-permute-done.15.refs_0_), custom_call_target="tpu_custom_call" | custom-call | flops 1000000 | bytes 100000 | tf_op jit(solution)/shard_map/pieces/pallas_call | solution.py:164
  216.6 2.8 %pieces.13 = f32[256,1024]{1,0:T(8,128)S(1)} custom-call(s32[9]{0:T(128)S(1)} %pad_add_fusion.place_ref, bf16[256,1024]{1,0:T(8,128)(2,1)S(1)} %get-tuple-element.86.gated_ref, bf16[1024,8192]{1,0:T(8,128)(2,1)} %w_ref.19, bf16[256,1024]{1,0:T(8,128)(2,1)S(1)} %collective-permute-done.15.refs_0_), custom_call_target="tpu_custom_call" | custom-call | flops 1000000 | bytes 100000 | tf_op jit(solution)/shard_map/pieces/pallas_call | solution.py:164
  (89 shorter events, 45.9 us)
Async XLA Ops:
  0.0 26.4 %collective-permute-start = (bf16[512,1024]{1,0:T(8,128)(2,1)}, bf16[512,1024]{1,0:T(8,128)(2,1)S(1)}, u32[]{:S(2)}, u32[]{:S(2)}) collective-permute-start(bf16[512,1024]{1,0:T(8,128)(2,1)} %refs_0_.1), channel_id=1, source_target_pairs={{0,4},{2,6},{4,0},{6,2},{8,12},{10,14},{12,8},{14,10},{1,5},{3,7},... | collective-permute-start | bytes 3145736 | tf_op jit(solution)/shard_map/ppermute | solution.py:216
  3.0 25.0 %collective-permute-start.3 = (bf16[512,1024]{1,0:T(8,128)(2,1)}, bf16[512,1024]{1,0:T(8,128)(2,1)S(1)}, u32[]{:S(2)}, u32[]{:S(2)}) collective-permute-start(bf16[512,1024]{1,0:T(8,128)(2,1)} %refs_0_.1), channel_id=1, source_target_pairs={{4,8},{6,10},{8,4},{10,6},{5,9},{7,11},{9,5},{11,7},{20,24},{22,26... | collective-permute-start | bytes 3145736 | tf_op jit(solution)/shard_map/ppermute | solution.py:216
  3.7 25.6 %collective-permute-start.1 = (bf16[512,1024]{1,0:T(8,128)(2,1)}, bf16[512,1024]{1,0:T(8,128)(2,1)S(1)}, u32[]{:S(2)}, u32[]{:S(2)}) collective-permute-start(bf16[512,1024]{1,0:T(8,128)(2,1)} %refs_0_.1), channel_id=1, source_target_pairs={{0,2},{2,0},{4,6},{6,4},{8,10},{10,8},{12,14},{14,12},{1,3},{3,1},... | collective-permute-start | bytes 3145736 | tf_op jit(solution)/shard_map/ppermute | solution.py:227
  26.4 21.1 %collective-permute-start.5 = (bf16[512,1024]{1,0:T(8,128)(2,1)S(1)}, bf16[512,1024]{1,0:T(8,128)(2,1)}, u32[]{:S(2)}, u32[]{:S(2)}) collective-permute-start(bf16[512,1024]{1,0:T(8,128)(2,1)S(1)} %collective-permute-done.refs_1_), channel_id=1, source_target_pairs={{4,8},{6,10},{8,4},{10,6},{5,9},{7,11},{9,5},{11,7},{20,24},{22,26... | collective-permute-start | bytes 3145736 | tf_op jit(solution)/shard_map/ppermute | solution.py:216
  28.0 27.3 %collective-permute-start.4 = (bf16[512,1024]{1,0:T(8,128)(2,1)S(1)}, bf16[512,1024]{1,0:T(8,128)(2,1)}, u32[]{:S(2)}, u32[]{:S(2)}) collective-permute-start(bf16[512,1024]{1,0:T(8,128)(2,1)S(1)} %collective-permute-done.3.refs_2_), channel_id=1, source_target_pairs={{4,0},{6,2},{8,12},{10,14},{5,1},{7,3},{9,13},{11,15},{20,16},{22,... | collective-permute-start | bytes 3145736 | tf_op jit(solution)/shard_map/ppermute | solution.py:216
  29.3 27.4 %collective-permute-start.2 = (bf16[512,1024]{1,0:T(8,128)(2,1)S(1)}, bf16[512,1024]{1,0:T(8,128)(2,1)}, u32[]{:S(2)}, u32[]{:S(2)}) collective-permute-start(bf16[512,1024]{1,0:T(8,128)(2,1)S(1)} %collective-permute-done.refs_1_), channel_id=1, source_target_pairs={{0,2},{2,0},{4,6},{6,4},{8,10},{10,8},{12,14},{14,12},{1,3},{3,1},... | collective-permute-start | bytes 3145736 | tf_op jit(solution)/shard_map/ppermute | solution.py:227
  47.5 29.9 %collective-permute-start.7 = (bf16[512,1024]{1,0:T(8,128)(2,1)}, bf16[512,1024]{1,0:T(8,128)(2,1)S(1)}, u32[]{:S(2)}, u32[]{:S(2)}) collective-permute-start(bf16[512,1024]{1,0:T(8,128)(2,1)} %collective-permute-done.5), channel_id=1, source_target_pairs={{4,0},{6,2},{8,12},{10,14},{5,1},{7,3},{9,13},{11,15},{20,16},{22,... | collective-permute-start | bytes 3145736 | tf_op jit(solution)/shard_map/ppermute | solution.py:216
  56.7 22.8 %collective-permute-start.6 = (bf16[512,1024]{1,0:T(8,128)(2,1)S(1)}, bf16[512,1024]{1,0:T(8,128)(2,1)S(1)}, u32[]{:S(2)}, u32[]{:S(2)}) collective-permute-start(bf16[512,1024]{1,0:T(8,128)(2,1)S(1)} %broadcast_select_fusion.refs_1_), channel_id=1, source_target_pairs={{0,2},{2,0},{4,6},{6,4},{8,10},{10,8},{12,14},{14,12},{1,3},{3,1},... | collective-permute-start | bytes 3145736 | tf_op jit(solution)/shard_map/ppermute | solution.py:227
  58.3 37.3 %collective-permute-start.10 = (bf16[512,512]{1,0:T(8,128)(2,1)S(1)}, bf16[512,512]{1,0:T(8,128)(2,1)S(1)}, u32[]{:S(2)}, u32[]{:S(2)}) collective-permute-start(bf16[512,512]{1,0:T(8,128)(2,1)S(1)} %slice.27), channel_id=1, source_target_pairs={{4,8},{6,10},{8,4},{10,6},{5,9},{7,11},{9,5},{11,7},{20,24},{22,26... | collective-permute-start | bytes 1572872 | tf_op jit(solution)/shard_map/ppermute | solution.py:216
  79.6 16.0 %collective-permute-start.9 = (bf16[512,512]{1,0:T(8,128)(2,1)S(1)}, bf16[512,512]{1,0:T(8,128)(2,1)S(1)}, u32[]{:S(2)}, u32[]{:S(2)}) collective-permute-start(bf16[512,512]{1,0:T(8,128)(2,1)S(1)} %slice.26), channel_id=1, source_target_pairs={{4,0},{6,2},{8,12},{10,14},{5,1},{7,3},{9,13},{11,15},{20,16},{22,... | collective-permute-start | bytes 1572872 | tf_op jit(solution)/shard_map/ppermute | solution.py:216
  80.9 14.7 %collective-permute-start.8 = (bf16[512,512]{1,0:T(8,128)(2,1)S(1)}, bf16[512,512]{1,0:T(8,128)(2,1)S(1)}, u32[]{:S(2)}, u32[]{:S(2)}) collective-permute-start(bf16[512,512]{1,0:T(8,128)(2,1)S(1)} %slice_select_fusion), channel_id=1, source_target_pairs={{0,2},{2,0},{4,6},{6,4},{8,10},{10,8},{12,14},{14,12},{1,3},{3,1},... | collective-permute-start | bytes 1572872 | tf_op jit(solution)/shard_map/ppermute | solution.py:227
  105.1 10.5 %collective-permute-start.11 = (f32[3,8,1024]{2,1,0:T(8,128)S(1)}, f32[3,8,1024]{2,1,0:T(8,128)S(1)}, u32[]{:S(2)}, u32[]{:S(2)}) collective-permute-start(f32[3,8,1024]{2,1,0:T(8,128)S(1)} %get-tuple-element.77), channel_id=1, source_target_pairs={{0,1},{2,3},{4,5},{6,7},{8,9},{10,11},{12,13},{14,15},{16,17},{18,... | collective-permute-start | bytes 294920 | tf_op jit(solution)/shard_map/ppermute | solution.py:19
  120.2 2.2 collective-permute-start.12
  128.0 15.0 %collective-permute-start.13 = (bf16[256,1024]{1,0:T(8,128)(2,1)S(1)}, bf16[256,1024]{1,0:T(8,128)(2,1)S(1)}, u32[]{:S(2)}, u32[]{:S(2)}) collective-permute-start(bf16[256,1024]{1,0:T(8,128)(2,1)S(1)} %pieces.10.refs_0_), channel_id=1, source_target_pairs={{0,2},{2,0},{4,6},{6,4},{8,10},{10,8},{12,14},{14,12},{1,3},{3,1},... | collective-permute-start | bytes 1572872 | tf_op jit(solution)/shard_map/ppermute | solution.py:227
  134.6 16.9 %collective-permute-start.14 = (bf16[256,1024]{1,0:T(8,128)(2,1)S(1)}, bf16[256,1024]{1,0:T(8,128)(2,1)S(1)}, u32[]{:S(2)}, u32[]{:S(2)}) collective-permute-start(bf16[256,1024]{1,0:T(8,128)(2,1)S(1)} %pieces.12.refs_0_), channel_id=1, source_target_pairs={{0,4},{2,6},{12,8},{14,10},{1,5},{3,7},{13,9},{15,11},{16,20},{18,... | collective-permute-start | bytes 1572872 | tf_op jit(solution)/shard_map/ppermute | solution.py:216
  143.1 19.6 %collective-permute-start.17 = (bf16[256,1024]{1,0:T(8,128)(2,1)S(1)}, bf16[256,1024]{1,0:T(8,128)(2,1)S(1)}, u32[]{:S(2)}, u32[]{:S(2)}) collective-permute-start(bf16[256,1024]{1,0:T(8,128)(2,1)S(1)} %add_convert_fusion.7), channel_id=1, source_target_pairs={{0,4},{2,6},{12,8},{14,10},{1,5},{3,7},{13,9},{15,11},{16,20},{18,... | collective-permute-start | bytes 1572872 | tf_op jit(solution)/shard_map/ppermute | solution.py:216
  147.2 15.6 %collective-permute-start.16 = (bf16[256,1024]{1,0:T(8,128)(2,1)S(1)}, bf16[256,1024]{1,0:T(8,128)(2,1)S(1)}, u32[]{:S(2)}, u32[]{:S(2)}) collective-permute-start(bf16[256,1024]{1,0:T(8,128)(2,1)S(1)} %get-tuple-element.94), channel_id=1, source_target_pairs={{0,2},{2,0},{4,6},{6,4},{8,10},{10,8},{12,14},{14,12},{1,3},{3,1},... | collective-permute-start | bytes 1572872 | tf_op jit(solution)/shard_map/ppermute | solution.py:227
  151.7 23.2 %collective-permute-start.15 = (bf16[256,1024]{1,0:T(8,128)(2,1)S(1)}, bf16[256,1024]{1,0:T(8,128)(2,1)S(1)}, u32[]{:S(2)}, u32[]{:S(2)}) collective-permute-start(bf16[256,1024]{1,0:T(8,128)(2,1)S(1)} %add_convert_fusion.8), channel_id=1, source_target_pairs={{0,2},{2,0},{4,6},{6,4},{8,10},{10,8},{12,14},{14,12},{1,3},{3,1},... | collective-permute-start | bytes 1572872 | tf_op jit(solution)/shard_map/ppermute | solution.py:227
  153.3 23.2 %collective-permute-start.24 = (bf16[256,1024]{1,0:T(8,128)(2,1)S(1)}, bf16[256,1024]{1,0:T(8,128)(2,1)S(1)}, u32[]{:S(2)}, u32[]{:S(2)}) collective-permute-start(bf16[256,1024]{1,0:T(8,128)(2,1)S(1)} %get-tuple-element.91.refs_0_), channel_id=1, source_target_pairs={{0,4},{2,6},{12,8},{14,10},{1,5},{3,7},{13,9},{15,11},{16,20},{18,... | collective-permute-start | bytes 1572872 | tf_op jit(solution)/shard_map/ppermute | solution.py:216
  157.7 24.6 %collective-permute-start.25 = (bf16[256,1024]{1,0:T(8,128)(2,1)S(1)}, bf16[256,1024]{1,0:T(8,128)(2,1)S(1)}, u32[]{:S(2)}, u32[]{:S(2)}) collective-permute-start(bf16[256,1024]{1,0:T(8,128)(2,1)S(1)} %pieces.12.refs_0_), channel_id=1, source_target_pairs={{4,8},{6,10},{8,4},{10,6},{5,9},{7,11},{9,5},{11,7},{20,24},{22,26... | collective-permute-start | bytes 1572872 | tf_op jit(solution)/shard_map/ppermute | solution.py:216
  163.0 28.0 %collective-permute-start.21 = (bf16[256,1024]{1,0:T(8,128)(2,1)S(1)}, bf16[256,1024]{1,0:T(8,128)(2,1)S(1)}, u32[]{:S(2)}, u32[]{:S(2)}) collective-permute-start(bf16[256,1024]{1,0:T(8,128)(2,1)S(1)} %add_convert_fusion.6), channel_id=1, source_target_pairs={{4,8},{6,10},{8,4},{10,6},{5,9},{7,11},{9,5},{11,7},{20,24},{22,26... | collective-permute-start | bytes 1572872 | tf_op jit(solution)/shard_map/ppermute | solution.py:216
  163.7 21.5 %collective-permute-start.18 = (bf16[256,1024]{1,0:T(8,128)(2,1)S(1)}, bf16[256,1024]{1,0:T(8,128)(2,1)S(1)}, u32[]{:S(2)}, u32[]{:S(2)}) collective-permute-start(bf16[256,1024]{1,0:T(8,128)(2,1)S(1)} %add_convert_fusion.6), channel_id=1, source_target_pairs={{0,4},{2,6},{12,8},{14,10},{1,5},{3,7},{13,9},{15,11},{16,20},{18,... | collective-permute-start | bytes 1572872 | tf_op jit(solution)/shard_map/ppermute | solution.py:216
  174.9 15.5 %collective-permute-start.19 = (bf16[256,1024]{1,0:T(8,128)(2,1)S(1)}, bf16[256,1024]{1,0:T(8,128)(2,1)S(1)}, u32[]{:S(2)}, u32[]{:S(2)}) collective-permute-start(bf16[256,1024]{1,0:T(8,128)(2,1)S(1)} %get-tuple-element.98), channel_id=1, source_target_pairs={{0,2},{2,0},{4,6},{6,4},{8,10},{10,8},{12,14},{14,12},{1,3},{3,1},... | collective-permute-start | bytes 1572872 | tf_op jit(solution)/shard_map/ppermute | solution.py:227
  176.8 19.7 %collective-permute-start.30 = (bf16[256,1024]{1,0:T(8,128)(2,1)S(1)}, bf16[256,1024]{1,0:T(8,128)(2,1)S(1)}, u32[]{:S(2)}, u32[]{:S(2)}) collective-permute-start(bf16[256,1024]{1,0:T(8,128)(2,1)S(1)} %add_convert_fusion.3.refs_0_), channel_id=1, source_target_pairs={{0,4},{2,6},{12,8},{14,10},{1,5},{3,7},{13,9},{15,11},{16,20},{18,... | collective-permute-start | bytes 1572872 | tf_op jit(solution)/shard_map/ppermute | solution.py:216
  182.3 18.4 %collective-permute-start.28 = (bf16[256,1024]{1,0:T(8,128)(2,1)S(1)}, bf16[256,1024]{1,0:T(8,128)(2,1)S(1)}, u32[]{:S(2)}, u32[]{:S(2)}) collective-permute-start(bf16[256,1024]{1,0:T(8,128)(2,1)S(1)} %add_convert_fusion.3.refs_0_), channel_id=1, source_target_pairs={{4,8},{6,10},{8,4},{10,6},{5,9},{7,11},{9,5},{11,7},{20,24},{22,26... | collective-permute-start | bytes 1572872 | tf_op jit(solution)/shard_map/ppermute | solution.py:216
  185.2 14.9 %collective-permute-start.26 = (bf16[256,1024]{1,0:T(8,128)(2,1)S(1)}, bf16[256,1024]{1,0:T(8,128)(2,1)S(1)}, u32[]{:S(2)}, u32[]{:S(2)}) collective-permute-start(bf16[256,1024]{1,0:T(8,128)(2,1)S(1)} %get-tuple-element.104), channel_id=1, source_target_pairs={{0,2},{2,0},{4,6},{6,4},{8,10},{10,8},{12,14},{14,12},{1,3},{3,1},... | collective-permute-start | bytes 1572872 | tf_op jit(solution)/shard_map/ppermute | solution.py:227
  190.4 20.9 %collective-permute-start.20 = (bf16[256,1024]{1,0:T(8,128)(2,1)S(1)}, bf16[256,1024]{1,0:T(8,128)(2,1)S(1)}, u32[]{:S(2)}, u32[]{:S(2)}) collective-permute-start(bf16[256,1024]{1,0:T(8,128)(2,1)S(1)} %get-tuple-element.99), channel_id=1, source_target_pairs={{0,2},{2,0},{4,6},{6,4},{8,10},{10,8},{12,14},{14,12},{1,3},{3,1},... | collective-permute-start | bytes 1572872 | tf_op jit(solution)/shard_map/ppermute | solution.py:227
  191.2 28.7 %collective-permute-start.22 = (bf16[256,1024]{1,0:T(8,128)(2,1)S(1)}, bf16[256,1024]{1,0:T(8,128)(2,1)S(1)}, u32[]{:S(2)}, u32[]{:S(2)}) collective-permute-start(bf16[256,1024]{1,0:T(8,128)(2,1)S(1)} %add_convert_fusion.5), channel_id=1, source_target_pairs={{0,4},{2,6},{4,0},{6,2},{8,12},{10,14},{12,8},{14,10},{1,5},{3,7},... | collective-permute-start | bytes 1572872 | tf_op jit(solution)/shard_map/ppermute | solution.py:216
  196.4 23.5 %collective-permute-start.23 = (bf16[256,1024]{1,0:T(8,128)(2,1)S(1)}, bf16[256,1024]{1,0:T(8,128)(2,1)S(1)}, u32[]{:S(2)}, u32[]{:S(2)}) collective-permute-start(bf16[256,1024]{1,0:T(8,128)(2,1)S(1)} %add_convert_fusion.4), channel_id=1, source_target_pairs={{4,8},{6,10},{8,4},{10,6},{5,9},{7,11},{9,5},{11,7},{20,24},{22,26... | collective-permute-start | bytes 1572872 | tf_op jit(solution)/shard_map/ppermute | solution.py:216
  200.1 19.9 %collective-permute-start.31 = (bf16[256,1024]{1,0:T(8,128)(2,1)S(1)}, bf16[256,1024]{1,0:T(8,128)(2,1)S(1)}, u32[]{:S(2)}, u32[]{:S(2)}) collective-permute-start(bf16[256,1024]{1,0:T(8,128)(2,1)S(1)} %add_convert_fusion), channel_id=1, source_target_pairs={{4,8},{6,10},{8,4},{10,6},{5,9},{7,11},{9,5},{11,7},{20,24},{22,26... | collective-permute-start | bytes 1572872 | tf_op jit(solution)/shard_map/ppermute | solution.py:216
  200.8 19.5 %collective-permute-start.27 = (bf16[256,1024]{1,0:T(8,128)(2,1)S(1)}, bf16[256,1024]{1,0:T(8,128)(2,1)S(1)}, u32[]{:S(2)}, u32[]{:S(2)}) collective-permute-start(bf16[256,1024]{1,0:T(8,128)(2,1)S(1)} %add_convert_fusion.2), channel_id=1, source_target_pairs={{0,2},{2,0},{4,6},{6,4},{8,10},{10,8},{12,14},{14,12},{1,3},{3,1},... | collective-permute-start | bytes 1572872 | tf_op jit(solution)/shard_map/ppermute | solution.py:227
  211.3 9.6 %collective-permute-start.29 = (bf16[256,1024]{1,0:T(8,128)(2,1)S(1)}, bf16[256,1024]{1,0:T(8,128)(2,1)S(1)}, u32[]{:S(2)}, u32[]{:S(2)}) collective-permute-start(bf16[256,1024]{1,0:T(8,128)(2,1)S(1)} %add_convert_fusion.1), channel_id=1, source_target_pairs={{0,4},{2,6},{4,0},{6,2},{8,12},{10,14},{12,8},{14,10},{1,5},{3,7},... | collective-permute-start | bytes 1572872 | tf_op jit(solution)/shard_map/ppermute | solution.py:216
  (9 other events, 102.4 us)

commit v3 on v2

--- a/solution.py
+++ b/solution.py
@@ -309,42 +309,29 @@
     return finish(*[[base[h], own_over[h], next_in[h], middle_in[h]] for h in both])
 
 
-def convolve_kernel(part_count, after_rows, *refs):
+def convolve_kernel(part_count, *refs):
     part_refs, refs = refs[:part_count], refs[part_count:]
-    rms_ref, refs = refs[0], refs[1:]
-    taps_ref, decay_ref, refs = refs[0], refs[1], refs[2:]
-    own_rim = after_rows is None
-    if own_rim:
-        rim_refs, rim_rms_ref = refs[:part_count], refs[part_count]
-    else:
-        rim_ref, later_ref = refs[:2]
-    q_ref, prod_ref, end_ref, win_ref, state_ref = refs[-5:]
+    rms_ref, rim_ref, taps_ref, decay_ref, q_ref, prod_ref, end_ref, win_ref, state_ref = refs
     step = pl.program_id(0)
     rows = q_ref.shape[0]
     tap_count, groups = taps_ref.shape[1:3]
     poles = decay_ref.shape[0]
-    keep = win_ref.shape[1] // groups - rows
+    keep = rim_ref.shape[1]
     unroll = 8
-
-    def rounded(sources, scale, i, g):
-        cols = tree_sum([ref[i, :, g * LANES : (g + 1) * LANES] for ref in sources]) * scale
-        return cols.astype(jnp.bfloat16).astype(jnp.float32)
 
     @pl.when(step == 0)
     def _():
         for g in range(groups):
             for i in range(3):
-                if own_rim:
-                    rim = rounded(rim_refs, rim_rms_ref[:, :1], i, g)
-                else:
-                    rim = rim_ref[i, :, g * LANES : (g + 1) * LANES]
-                win_ref[i, pl.ds(g, keep, stride=groups), :] = rim
+                win_ref[i, pl.ds(g, keep, stride=groups), :] = rim_ref[i, :, g * LANES : (g + 1) * LANES]
         state_ref[...] = jnp.zeros_like(state_ref)
 
     inv_rms = rms_ref[:, :1]
     for i in range(3):
         for g in range(groups):
-            win_ref[i, pl.ds(keep * groups + g, rows, stride=groups), :] = rounded(part_refs, inv_rms, i, g)
+            cols = tree_sum([ref[i, :, g * LANES : (g + 1) * LANES] for ref in part_refs]) * inv_rms
+            cols = cols.astype(jnp.bfloat16).astype(jnp.float32)
+            win_ref[i, pl.ds(keep * groups + g, rows, stride=groups), :] = cols
     decay = [jnp.exp(decay_ref[n]) for n in range(poles)]
 
     def row_of(i, t):
@@ -381,56 +368,43 @@
     @pl.when(step == pl.num_programs(0) - 1)
     def _():
         for n in range(poles):
-            if own_rim:
-                end_ref[n] = state[n]
-            else:
-                end_ref[n] = later_ref[n] + jnp.exp(float(after_rows) * decay_ref[n]) * state[n]
-
-
-def convolve(parts, inv_rms, taps, log_decay, rim=None, done=None):
+            end_ref[n] = state[n]
+
+
+def convolve(parts, inv_rms, rim, taps, log_decay):
     rows, chans = parts[0].shape[1:]
     groups = chans // LANES
     tap_count, poles = taps.shape[1], log_decay.shape[0]
-    count = len(parts)
-    blk = min(128, rows // 2)
+    keep = rim.shape[1]
+    blk = min(128, rows)
     whole = lambda *shape: pl.BlockSpec(shape, lambda t: (0,) * len(shape))
-    start = 1 if rim is None else 0
-    row_spec = pl.BlockSpec((blk, groups, LANES), lambda t: (t + start, 0, 0))
-    state_spec = whole(poles, groups, LANES)
-    in_specs = [pl.BlockSpec((3, blk, chans), lambda t: (0, t + start, 0))] * count
-    in_specs += [pl.BlockSpec((blk, LANES), lambda t: (t + start, 0)), whole(3, tap_count, groups, LANES), state_spec]
-    operands, aliases = [*parts, inv_rms, taps, log_decay], {}
-    if rim is None:
-        at = blk // KEEP - 1
-        in_specs += [pl.BlockSpec((3, KEEP, chans), lambda t: (0, at, 0))] * count
-        in_specs += [pl.BlockSpec((KEEP, LANES), lambda t: (at, 0))]
-        operands += [*parts, inv_rms]
-    else:
-        query, product, end = done
-        in_specs += [whole(3, KEEP, chans), state_spec] + [pl.BlockSpec(memory_space=pl.ANY)] * 2
-        operands += [rim, end, query, product]
-        aliases = {len(operands) - 2: 0, len(operands) - 1: 1}
+    row_spec = pl.BlockSpec((blk, groups, LANES), lambda t: (t, 0, 0))
     return pl.pallas_call(
-        functools.partial(convolve_kernel, count, None if rim is None else rows - blk),
-        grid=(rows // blk - 1 if rim is None else 1,),
-        in_specs=in_specs,
-        out_specs=[row_spec, row_spec, state_spec],
+        functools.partial(convolve_kernel, len(parts)),
+        grid=(rows // blk,),
+        in_specs=[pl.BlockSpec((3, blk, chans), lambda t: (0, t, 0))] * len(parts)
+        + [
+            pl.BlockSpec((blk, LANES), lambda t: (t, 0)),
+            whole(3, keep, chans),
+            whole(3, tap_count, groups, LANES),
+            whole(poles, groups, LANES),
+        ],
+        out_specs=[row_spec, row_spec, whole(poles, groups, LANES)],
         out_shape=[
             jax.ShapeDtypeStruct((rows, groups, LANES), jnp.float32),
             jax.ShapeDtypeStruct((rows, groups, LANES), jnp.float32),
             jax.ShapeDtypeStruct((poles, groups, LANES), jnp.float32),
         ],
         scratch_shapes=[
-            pltpu.VMEM((3, (KEEP + blk) * groups, LANES), jnp.float32),
+            pltpu.VMEM((3, (keep + blk) * groups, LANES), jnp.float32),
             pltpu.VMEM((poles, groups, LANES), jnp.float32),
         ],
-        input_output_aliases=aliases,
         compiler_params=pltpu.CompilerParams(vmem_limit_bytes=VMEM_LIMIT),
         cost_estimate=pl.CostEstimate(
-            flops=80 * rows * groups * LANES, bytes_accessed=20 * rows * groups * LANES, transcendentals=0
+            flops=110 * rows * groups * LANES, bytes_accessed=20 * rows * groups * LANES, transcendentals=0
         ),
         name="convolve",
-    )(*operands)
+    )(*parts, inv_rms, rim, taps, log_decay)
 
 
 def respond_kernel(q_ref, prod_ref, enter_ref, decay_ref, res_ref, skip_ref, *refs):
@@ -529,8 +503,7 @@
         acc, inv_rms, rim = accumulate(table, chunks[-1:], places, norm_gain, in_weight, acc, square, [])
         parts = [acc]
     rim = from_behind(rim, "seq", 1)
-    done = convolve(parts, inv_rms, taps, log_decay)
-    query, product, end = convolve(parts, inv_rms, taps, log_decay, rim, done)
+    query, product, end = convolve(parts, inv_rms, rim, taps, log_decay)
     shard_decay = jnp.exp(rows * log_decay)
     state, passing = jnp.zeros_like(end), end
     for _ in range(lax.axis_size("seq") - 1):

time: 225 us -> 224 us (level)
    pallas_call x2 -> x1, Pallas kernels: 13.8 us -> 11.7 us  [convolve(): pl.pallas_call(functools.partial(convolve_kernel, len(parts)), grid=(rows...]
  transfers between devices with their start and end apart: 32 -> 32, of which waited for: 13 -> 14; matrix products, arithmetic and copies ran while one was open for 3% -> 3% of each run, Pallas kernels for 42% -> 38%
where the time goes in v3:
time: 224 us; the launch traced here: 223 us
  Pallas kernels  114 us (51%)
  starting transfers between devices  58.8 us (26%)
  waiting for transfers between devices  41.1 us (18%)
  local copies, waits for them, and re-layouts  4.28 us (2%)
  other arithmetic  3.83 us (2%)
    pallas_call x5, Pallas kernels, accumulate(): pl.pallas_call(functools.partial(accumulate_kernel, depths, pairs, width,...  60.9 us
    ppermute x19, starting transfers between devices, along_line(): lax.ppermute(block, 'chan', [(2 * a + y, 2 * b + y) for a, b in pairs for...  40.7 us
    pallas_call x10, Pallas kernels, pieces(): pl.pallas_call(functools.partial(pieces_kernel, count), grid_spec=pltpu.P...  33.6 us
    ppermute x19, waiting for transfers between devices, along_line(): lax.ppermute(block, 'chan', [(2 * a + y, 2 * b + y) for a, b in pairs for...  25.4 us
    ppermute x11, starting transfers between devices, across(): return lax.ppermute(block, 'chan', [(c, c ^ 1) for c in range(count)])  14.5 us
    ppermute x11, waiting for transfers between devices, across(): return lax.ppermute(block, 'chan', [(c, c ^ 1) for c in range(count)])  13.9 us
    pallas_call x1, Pallas kernels, convolve(): pl.pallas_call(functools.partial(convolve_kernel, len(parts)), grid=(rows...  11.7 us
    pallas_call x2, Pallas kernels, respond(): pl.pallas_call(respond_kernel, grid=(rows // blk,), in_specs=[row_spec, r...  6.07 us
  transfers between devices with their start and end apart: 32, of which 14 were waited for; matrix products, arithmetic and copies ran while one was open for 3% of the time, Pallas kernels for 38%

profile of v3, /device:TPU:0, one launch (start us, length us, event | category | flops | bytes accessed | tf_op | source)
XLA Modules:
  0.0 222.5 jit_solution(12100495243043880155)
XLA Ops:
  0.0 3.0 %collective-permute-start = (bf16[512,1024]{1,0:T(8,128)(2,1)}, bf16[512,1024]{1,0:T(8,128)(2,1)S(1)}, u32[]{:S(2)}, u32[]{:S(2)}) collective-permute-start(bf16[512,1024]{1,0:T(8,128)(2,1)} %refs_0_.1), channel_id=1, source_target_pairs={{0,4},{2,6},{4,0},{6,2},{8,12},{10,14},{12,8},{14,10},{1,5},{3,7},... | collective-permute-start | bytes 3145736 | tf_op jit(solution)/shard_map/ppermute | solution.py:216
  7.4 9.4 %accumulate.5 = (f32[3,512,1024]{2,1,0:T(8,128)}, f32[512,128]{1,0:T(8,128)S(1)}) custom-call(s32[9]{0:T(128)S(1)} %pad_add_fusion.place_ref, bf16[512,1024]{1,0:T(8,128)(2,1)S(1)} %copy-done, f32[8,1,1024]{2,1,0:T(1,128)S(1)} %bitcast.8, bf16[3,8192,1024]{2,1,0:T(8,128)(2,1)} %refs_6_.3), custom_call_target="tpu_custom_call" | custom-call | flops 536870912 | bytes 6291456 | tf_op jit(solution)/shard_map/accumulate/pallas_call | solution.py:115
  16.8 9.6 %collective-permute-done.refs_1_ = bf16[512,1024]{1,0:T(8,128)(2,1)S(1)} collective-permute-done((bf16[512,1024]{1,0:T(8,128)(2,1)}, bf16[512,1024]{1,0:T(8,128)(2,1)S(1)}, u32[]{:S(2)}, u32[]{:S(2)}) %collective-permute-start) | collective-permute-done | bytes 1048608 | tf_op jit(solution)/shard_map/ppermute | solution.py:216
  33.3 14.2 %accumulate.6 = (f32[3,512,1024]{2,1,0:T(8,128)}, f32[512,128]{1,0:T(8,128)S(1)}) custom-call(s32[9]{0:T(128)S(1)} %pad_add_fusion.place_ref, bf16[512,1024]{1,0:T(8,128)(2,1)S(1)} %collective-permute-done.1.refs_0_, bf16[512,1024]{1,0:T(8,128)(2,1)S(1)} %collective-permute-done.refs_1_, ...), custom_call_target="tpu_custom_call", output_to_operand_aliasing={{0}: (7, {}), {1}: (8, {})} | custom-call | flops 1073741824 | bytes 12582912 | tf_op jit(solution)/shard_map/accumulate/pallas_call | solution.py:115
  48.8 6.6 %collective-permute-done.4 = bf16[512,1024]{1,0:T(8,128)(2,1)} collective-permute-done((bf16[512,1024]{1,0:T(8,128)(2,1)S(1)}, bf16[512,1024]{1,0:T(8,128)(2,1)}, u32[]{:S(2)}, u32[]{:S(2)}) %collective-permute-start.4) | collective-permute-done | bytes 1048608 | tf_op jit(solution)/shard_map/ppermute | solution.py:216
  59.0 14.8 %accumulate.7 = (f32[3,512,1024]{2,1,0:T(8,128)}, f32[512,128]{1,0:T(8,128)S(1)}) custom-call(s32[9]{0:T(128)S(1)} %pad_add_fusion.place_ref, bf16[512,1024]{1,0:T(8,128)(2,1)} %collective-permute-done.2.refs_0_, bf16[512,1024]{1,0:T(8,128)(2,1)S(1)} %broadcast_select_fusion.refs_1_, ...), custom_call_target="tpu_custom_call", output_to_operand_aliasing={{0}: (7, {}), {1}: (8, {})} | custom-call | flops 1073741824 | bytes 12582912 | tf_op jit(solution)/shard_map/accumulate/pallas_call | solution.py:115
  73.9 3.5 %collective-permute-done.7.refs_1_ = bf16[512,1024]{1,0:T(8,128)(2,1)S(1)} collective-permute-done((bf16[512,1024]{1,0:T(8,128)(2,1)}, bf16[512,1024]{1,0:T(8,128)(2,1)S(1)}, u32[]{:S(2)}, u32[]{:S(2)}) %collective-permute-start.7) | collective-permute-done | bytes 1048608 | tf_op jit(solution)/shard_map/ppermute | solution.py:216
  82.5 13.1 %accumulate.8 = (f32[3,512,1024]{2,1,0:T(8,128)}, f32[512,128]{1,0:T(8,128)S(1)}) custom-call(s32[9]{0:T(128)S(1)} %pad_add_fusion.place_ref, bf16[512,1024]{1,0:T(8,128)(2,1)S(1)} %collective-permute-done.6.refs_0_, bf16[512,1024]{1,0:T(8,128)(2,1)S(1)} %collective-permute-done.7.refs_1_, ...), custom_call_target="tpu_custom_call", output_to_operand_aliasing={{1}: (8, {})} | custom-call | flops 1073741824 | bytes 12582912 | tf_op jit(solution)/shard_map/accumulate/pallas_call | solution.py:115
  95.6 9.4 %accumulate.9 = (f32[3,512,1024]{2,1,0:T(8,128)}, f32[512,128]{1,0:T(8,128)S(1)}, f32[3,8,1024]{2,1,0:T(8,128)S(1)}) custom-call(s32[9]{0:T(128)S(1)} %pad_add_fusion.place_ref, bf16[512,512]{1,0:T(8,128)(2,1)S(1)} %collective-permute-done.8.refs_0_, bf16[512,512]{1,0:T(8,128)(2,1)S(1)} %collective-permute-done.9.refs_1_, ...), custom_call_target="tpu_custom_call", output_to_operand_aliasing={{1}: (8, {})} | custom-call | flops 536870912 | bytes 6291456 | tf_op jit(solution)/shard_map/accumulate/pallas_call | solution.py:115
  107.2 11.7 %convolve.1 = (f32[512,8,128]{2,1,0:T(8,128)S(1)}, f32[512,8,128]{2,1,0:T(8,128)S(1)}, f32[16,8,128]{2,1,0:T(8,128)S(1)}) custom-call(f32[3,512,1024]{2,1,0:T(8,128)} %get-tuple-element.61.refs_8_.refs_0_, f32[3,512,1024]{2,1,0:T(8,128)} %get-tuple-element.65.refs_9_.refs_1_, f32[3,512,1024]{2,1,0:T(8,128)} %get-tuple-element.70.refs_2_, ...), custom_call_target="tpu_custom_call" | custom-call | flops 57671680 | bytes 10485760 | tf_op jit(solution)/shard_map/convolve/pallas_call | solution.py:382
  118.9 2.3 %collective-permute-start.12 = (f32[16,8,128]{2,1,0:T(8,128)S(1)}, f32[16,8,128]{2,1,0:T(8,128)S(1)}, u32[]{:S(2)}, u32[]{:S(2)}) collective-permute-start(f32[16,8,128]{2,1,0:T(8,128)S(1)} %get-tuple-element.77), channel_id=1, source_target_pairs={{0,1},{2,3},{4,5},{6,7},{8,9},{10,11},{12,13},{14,15},{16,17},{18,... | collective-permute-start | bytes 196616 | tf_op jit(solution)/shard_map/ppermute | solution.py:19
  122.1 2.8 %respond.2 = (bf16[256,1024]{1,0:T(8,128)(2,1)S(1)}, f32[16,8,128]{2,1,0:T(8,128)S(1)}) custom-call(f32[512,8,128]{2,1,0:T(8,128)S(1)} %get-tuple-element.75.q_ref, f32[512,8,128]{2,1,0:T(8,128)S(1)} %get-tuple-element.76.prod_ref, f32[16,8,128]{2,1,0:T(8,128)S(1)} %collective-permute-done.12.enter_ref, f32[16,8,128]{2,1,0:T(8,128)S(1)} %bitcast.18, ...), custom_call_target="tpu_custom_call" | custom-call | flops 18350080 | bytes 20971520 | tf_op jit(solution)/shard_map/respond/pallas_call | solution.py:455
  124.9 2.9 %pieces.10.refs_0_ = bf16[256,1024]{1,0:T(8,128)(2,1)S(1)} custom-call(s32[9]{0:T(128)S(1)} %pad_add_fusion.place_ref, bf16[256,1024]{1,0:T(8,128)(2,1)S(1)} %get-tuple-element.80.gated_ref, bf16[1024,8192]{1,0:T(8,128)(2,1)} %w_ref.19), custom_call_target="tpu_custom_call" | custom-call | flops 1000000 | bytes 100000 | tf_op jit(solution)/shard_map/pieces/pallas_call | solution.py:164
  128.3 3.3 %respond.3 = (bf16[256,1024]{1,0:T(8,128)(2,1)S(1)}, f32[16,8,128]{2,1,0:T(8,128)}) custom-call(f32[512,8,128]{2,1,0:T(8,128)S(1)} %get-tuple-element.75.q_ref, f32[512,8,128]{2,1,0:T(8,128)S(1)} %get-tuple-element.76.prod_ref, f32[16,8,128]{2,1,0:T(8,128)S(1)} %get-tuple-element.81.enter_ref, f32[16,8,128]{2,1,0:T(8,128)S(1)} %bitcast.19, ...), custom_call_target="tpu_custom_call" | custom-call | flops 18350080 | bytes 20971520 | tf_op jit(solution)/shard_map/respond/pallas_call | solution.py:455
  131.6 2.8 %pieces.12.refs_0_ = bf16[256,1024]{1,0:T(8,128)(2,1)S(1)} custom-call(s32[9]{0:T(128)S(1)} %pad_add_fusion.place_ref, bf16[256,1024]{1,0:T(8,128)(2,1)S(1)} %get-tuple-element.82.gated_ref, bf16[1024,8192]{1,0:T(8,128)(2,1)} %w_ref.19), custom_call_target="tpu_custom_call" | custom-call | flops 1000000 | bytes 100000 | tf_op jit(solution)/shard_map/pieces/pallas_call | solution.py:164
  134.4 4.6 %collective-permute-start.14 = (bf16[256,1024]{1,0:T(8,128)(2,1)S(1)}, bf16[256,1024]{1,0:T(8,128)(2,1)S(1)}, u32[]{:S(2)}, u32[]{:S(2)}) collective-permute-start(bf16[256,1024]{1,0:T(8,128)(2,1)S(1)} %pieces.12.refs_0_), channel_id=1, source_target_pairs={{0,4},{2,6},{12,8},{14,10},{1,5},{3,7},{13,9},{15,11},{16,20},{18,... | collective-permute-start | bytes 1572872 | tf_op jit(solution)/shard_map/ppermute | solution.py:216
  139.1 3.7 %pieces.15 = (bf16[256,1024]{1,0:T(8,128)(2,1)S(1)}, f32[256,1024]{1,0:T(8,128)S(1)}) custom-call(s32[9]{0:T(128)S(1)} %pad_add_fusion.place_ref, bf16[256,1024]{1,0:T(8,128)(2,1)S(1)} %get-tuple-element.80.gated_ref, bf16[1024,8192]{1,0:T(8,128)(2,1)} %w_ref.19, bf16[256,1024]{1,0:T(8,128)(2,1)S(1)} %pieces.12.refs_0_), custom_call_target="tpu_custom_call" | custom-call | flops 2000000 | bytes 200000 | tf_op jit(solution)/shard_map/pieces/pallas_call | solution.py:164
  143.0 3.8 %collective-permute-start.17 = (bf16[256,1024]{1,0:T(8,128)(2,1)S(1)}, bf16[256,1024]{1,0:T(8,128)(2,1)S(1)}, u32[]{:S(2)}, u32[]{:S(2)}) collective-permute-start(bf16[256,1024]{1,0:T(8,128)(2,1)S(1)} %add_convert_fusion.7), channel_id=1, source_target_pairs={{0,4},{2,6},{12,8},{14,10},{1,5},{3,7},{13,9},{15,11},{16,20},{18,... | collective-permute-start | bytes 1572872 | tf_op jit(solution)/shard_map/ppermute | solution.py:216
  147.3 3.7 %pieces.11 = (bf16[256,1024]{1,0:T(8,128)(2,1)S(1)}, bf16[256,1024]{1,0:T(8,128)(2,1)S(1)}) custom-call(s32[9]{0:T(128)S(1)} %pad_add_fusion.place_ref, bf16[256,1024]{1,0:T(8,128)(2,1)S(1)} %get-tuple-element.82.gated_ref, bf16[1024,8192]{1,0:T(8,128)(2,1)} %w_ref.19, bf16[256,1024]{1,0:T(8,128)(2,1)S(1)} %collective-permute-done.13.refs_0_), custom_call_target="tpu_custom_call" | custom-call | flops 2000000 | bytes 200000 | tf_op jit(solution)/shard_map/pieces/pallas_call | solution.py:164
  153.1 4.4 %collective-permute-start.24 = (bf16[256,1024]{1,0:T(8,128)(2,1)S(1)}, bf16[256,1024]{1,0:T(8,128)(2,1)S(1)}, u32[]{:S(2)}, u32[]{:S(2)}) collective-permute-start(bf16[256,1024]{1,0:T(8,128)(2,1)S(1)} %get-tuple-element.85.refs_0_), channel_id=1, source_target_pairs={{0,4},{2,6},{12,8},{14,10},{1,5},{3,7},{13,9},{15,11},{16,20},{18,... | collective-permute-start | bytes 1572872 | tf_op jit(solution)/shard_map/ppermute | solution.py:216
  158.4 3.7 %pieces.14 = (f32[256,1024]{1,0:T(8,128)S(1)}, bf16[256,1024]{1,0:T(8,128)(2,1)S(1)}) custom-call(s32[9]{0:T(128)S(1)} %pad_add_fusion.place_ref, bf16[256,1024]{1,0:T(8,128)(2,1)S(1)} %get-tuple-element.80.gated_ref, bf16[1024,8192]{1,0:T(8,128)(2,1)} %w_ref.19, bf16[256,1024]{1,0:T(8,128)(2,1)S(1)} %get-tuple-element.85.refs_0_), custom_call_target="tpu_custom_call" | custom-call | flops 2000000 | bytes 200000 | tf_op jit(solution)/shard_map/pieces/pallas_call | solution.py:164
  163.5 7.5 %collective-permute-start.18 = (bf16[256,1024]{1,0:T(8,128)(2,1)S(1)}, bf16[256,1024]{1,0:T(8,128)(2,1)S(1)}, u32[]{:S(2)}, u32[]{:S(2)}) collective-permute-start(bf16[256,1024]{1,0:T(8,128)(2,1)S(1)} %add_convert_fusion.6), channel_id=1, source_target_pairs={{0,4},{2,6},{12,8},{14,10},{1,5},{3,7},{13,9},{15,11},{16,20},{18,... | collective-permute-start | bytes 1572872 | tf_op jit(solution)/shard_map/ppermute | solution.py:216
  171.0 3.7 %pieces.18 = (f32[256,1024]{1,0:T(8,128)S(1)}, bf16[256,1024]{1,0:T(8,128)(2,1)S(1)}) custom-call(s32[9]{0:T(128)S(1)} %pad_add_fusion.place_ref, bf16[256,1024]{1,0:T(8,128)(2,1)S(1)} %get-tuple-element.82.gated_ref, bf16[1024,8192]{1,0:T(8,128)(2,1)} %w_ref.19, bf16[256,1024]{1,0:T(8,128)(2,1)S(1)} %collective-permute-done.17.refs_0_), custom_call_target="tpu_custom_call" | custom-call | flops 2000000 | bytes 200000 | tf_op jit(solution)/shard_map/pieces/pallas_call | solution.py:164
  178.4 3.7 %pieces.19 = (f32[256,1024]{1,0:T(8,128)S(1)}, bf16[256,1024]{1,0:T(8,128)(2,1)S(1)}) custom-call(s32[9]{0:T(128)S(1)} %pad_add_fusion.place_ref, bf16[256,1024]{1,0:T(8,128)(2,1)S(1)} %get-tuple-element.82.gated_ref, bf16[1024,8192]{1,0:T(8,128)(2,1)} %w_ref.19, bf16[256,1024]{1,0:T(8,128)(2,1)S(1)} %add_convert_fusion.3.refs_0_), custom_call_target="tpu_custom_call" | custom-call | flops 2000000 | bytes 200000 | tf_op jit(solution)/shard_map/pieces/pallas_call | solution.py:164
  186.5 3.7 %pieces.16 = (f32[256,1024]{1,0:T(8,128)S(1)}, bf16[256,1024]{1,0:T(8,128)(2,1)S(1)}) custom-call(s32[9]{0:T(128)S(1)} %pad_add_fusion.place_ref, bf16[256,1024]{1,0:T(8,128)(2,1)S(1)} %get-tuple-element.80.gated_ref, bf16[1024,8192]{1,0:T(8,128)(2,1)} %w_ref.19, bf16[256,1024]{1,0:T(8,128)(2,1)S(1)} %collective-permute-done.18.refs_0_), custom_call_target="tpu_custom_call" | custom-call | flops 2000000 | bytes 200000 | tf_op jit(solution)/shard_map/pieces/pallas_call | solution.py:164
  191.1 2.5 %collective-permute-start.22 = (bf16[256,1024]{1,0:T(8,128)(2,1)S(1)}, bf16[256,1024]{1,0:T(8,128)(2,1)S(1)}, u32[]{:S(2)}, u32[]{:S(2)}) collective-permute-start(bf16[256,1024]{1,0:T(8,128)(2,1)S(1)} %add_convert_fusion.5), channel_id=1, source_target_pairs={{0,4},{2,6},{4,0},{6,2},{8,12},{10,14},{12,8},{14,10},{1,5},{3,7},... | collective-permute-start | bytes 1572872 | tf_op jit(solution)/shard_map/ppermute | solution.py:216
  193.8 2.4 %collective-permute-done.30 = bf16[256,1024]{1,0:T(8,128)(2,1)S(1)} collective-permute-done((bf16[256,1024]{1,0:T(8,128)(2,1)S(1)}, bf16[256,1024]{1,0:T(8,128)(2,1)S(1)}, u32[]{:S(2)}, u32[]{:S(2)}) %collective-permute-start.30) | collective-permute-done | bytes 524320 | tf_op jit(solution)/shard_map/ppermute | solution.py:216
  197.1 2.7 %collective-permute-done.26 = bf16[256,1024]{1,0:T(8,128)(2,1)S(1)} collective-permute-done((bf16[256,1024]{1,0:T(8,128)(2,1)S(1)}, bf16[256,1024]{1,0:T(8,128)(2,1)S(1)}, u32[]{:S(2)}, u32[]{:S(2)}) %collective-permute-start.26) | collective-permute-done | bytes 524320 | tf_op jit(solution)/shard_map/ppermute | solution.py:227
  202.4 8.7 %collective-permute-done.20.refs_1_ = bf16[256,1024]{1,0:T(8,128)(2,1)S(1)} collective-permute-done((bf16[256,1024]{1,0:T(8,128)(2,1)S(1)}, bf16[256,1024]{1,0:T(8,128)(2,1)S(1)}, u32[]{:S(2)}, u32[]{:S(2)}) %collective-permute-start.20) | collective-permute-done | bytes 524320 | tf_op jit(solution)/shard_map/ppermute | solution.py:227
  211.1 2.5 %collective-permute-start.29 = (bf16[256,1024]{1,0:T(8,128)(2,1)S(1)}, bf16[256,1024]{1,0:T(8,128)(2,1)S(1)}, u32[]{:S(2)}, u32[]{:S(2)}) collective-permute-start(bf16[256,1024]{1,0:T(8,128)(2,1)S(1)} %add_convert_fusion.1), channel_id=1, source_target_pairs={{0,4},{2,6},{4,0},{6,2},{8,12},{10,14},{12,8},{14,10},{1,5},{3,7},... | collective-permute-start | bytes 1572872 | tf_op jit(solution)/shard_map/ppermute | solution.py:216
  213.6 2.8 %pieces.17 = f32[256,1024]{1,0:T(8,128)S(1)} custom-call(s32[9]{0:T(128)S(1)} %pad_add_fusion.place_ref, bf16[256,1024]{1,0:T(8,128)(2,1)S(1)} %get-tuple-element.82.gated_ref, bf16[1024,8192]{1,0:T(8,128)(2,1)} %w_ref.19, bf16[256,1024]{1,0:T(8,128)(2,1)S(1)} %collective-permute-done.15.refs_0_), custom_call_target="tpu_custom_call" | custom-call | flops 1000000 | bytes 100000 | tf_op jit(solution)/shard_map/pieces/pallas_call | solution.py:164
  216.4 2.9 %pieces.13 = f32[256,1024]{1,0:T(8,128)S(1)} custom-call(s32[9]{0:T(128)S(1)} %pad_add_fusion.place_ref, bf16[256,1024]{1,0:T(8,128)(2,1)S(1)} %get-tuple-element.80.gated_ref, bf16[1024,8192]{1,0:T(8,128)(2,1)} %w_ref.19, bf16[256,1024]{1,0:T(8,128)(2,1)S(1)} %collective-permute-done.15.refs_0_), custom_call_target="tpu_custom_call" | custom-call | flops 1000000 | bytes 100000 | tf_op jit(solution)/shard_map/pieces/pallas_call | solution.py:164
  (88 shorter events, 45.6 us)
Async XLA Ops:
  0.0 26.4 %collective-permute-start = (bf16[512,1024]{1,0:T(8,128)(2,1)}, bf16[512,1024]{1,0:T(8,128)(2,1)S(1)}, u32[]{:S(2)}, u32[]{:S(2)}) collective-permute-start(bf16[512,1024]{1,0:T(8,128)(2,1)} %refs_0_.1), channel_id=1, source_target_pairs={{0,4},{2,6},{4,0},{6,2},{8,12},{10,14},{12,8},{14,10},{1,5},{3,7},... | collective-permute-start | bytes 3145736 | tf_op jit(solution)/shard_map/ppermute | solution.py:216
  3.0 25.0 %collective-permute-start.3 = (bf16[512,1024]{1,0:T(8,128)(2,1)}, bf16[512,1024]{1,0:T(8,128)(2,1)S(1)}, u32[]{:S(2)}, u32[]{:S(2)}) collective-permute-start(bf16[512,1024]{1,0:T(8,128)(2,1)} %refs_0_.1), channel_id=1, source_target_pairs={{4,8},{6,10},{8,4},{10,6},{5,9},{7,11},{9,5},{11,7},{20,24},{22,26... | collective-permute-start | bytes 3145736 | tf_op jit(solution)/shard_map/ppermute | solution.py:216
  3.7 25.6 %collective-permute-start.1 = (bf16[512,1024]{1,0:T(8,128)(2,1)}, bf16[512,1024]{1,0:T(8,128)(2,1)S(1)}, u32[]{:S(2)}, u32[]{:S(2)}) collective-permute-start(bf16[512,1024]{1,0:T(8,128)(2,1)} %refs_0_.1), channel_id=1, source_target_pairs={{0,2},{2,0},{4,6},{6,4},{8,10},{10,8},{12,14},{14,12},{1,3},{3,1},... | collective-permute-start | bytes 3145736 | tf_op jit(solution)/shard_map/ppermute | solution.py:227
  26.4 21.1 %collective-permute-start.5 = (bf16[512,1024]{1,0:T(8,128)(2,1)S(1)}, bf16[512,1024]{1,0:T(8,128)(2,1)}, u32[]{:S(2)}, u32[]{:S(2)}) collective-permute-start(bf16[512,1024]{1,0:T(8,128)(2,1)S(1)} %collective-permute-done.refs_1_), channel_id=1, source_target_pairs={{4,8},{6,10},{8,4},{10,6},{5,9},{7,11},{9,5},{11,7},{20,24},{22,26... | collective-permute-start | bytes 3145736 | tf_op jit(solution)/shard_map/ppermute | solution.py:216
  28.0 27.3 %collective-permute-start.4 = (bf16[512,1024]{1,0:T(8,128)(2,1)S(1)}, bf16[512,1024]{1,0:T(8,128)(2,1)}, u32[]{:S(2)}, u32[]{:S(2)}) collective-permute-start(bf16[512,1024]{1,0:T(8,128)(2,1)S(1)} %collective-permute-done.3.refs_2_), channel_id=1, source_target_pairs={{4,0},{6,2},{8,12},{10,14},{5,1},{7,3},{9,13},{11,15},{20,16},{22,... | collective-permute-start | bytes 3145736 | tf_op jit(solution)/shard_map/ppermute | solution.py:216
  29.3 27.4 %collective-permute-start.2 = (bf16[512,1024]{1,0:T(8,128)(2,1)S(1)}, bf16[512,1024]{1,0:T(8,128)(2,1)}, u32[]{:S(2)}, u32[]{:S(2)}) collective-permute-start(bf16[512,1024]{1,0:T(8,128)(2,1)S(1)} %collective-permute-done.refs_1_), channel_id=1, source_target_pairs={{0,2},{2,0},{4,6},{6,4},{8,10},{10,8},{12,14},{14,12},{1,3},{3,1},... | collective-permute-start | bytes 3145736 | tf_op jit(solution)/shard_map/ppermute | solution.py:227
  47.5 29.9 %collective-permute-start.7 = (bf16[512,1024]{1,0:T(8,128)(2,1)}, bf16[512,1024]{1,0:T(8,128)(2,1)S(1)}, u32[]{:S(2)}, u32[]{:S(2)}) collective-permute-start(bf16[512,1024]{1,0:T(8,128)(2,1)} %collective-permute-done.5), channel_id=1, source_target_pairs={{4,0},{6,2},{8,12},{10,14},{5,1},{7,3},{9,13},{11,15},{20,16},{22,... | collective-permute-start | bytes 3145736 | tf_op jit(solution)/shard_map/ppermute | solution.py:216
  56.7 22.8 %collective-permute-start.6 = (bf16[512,1024]{1,0:T(8,128)(2,1)S(1)}, bf16[512,1024]{1,0:T(8,128)(2,1)S(1)}, u32[]{:S(2)}, u32[]{:S(2)}) collective-permute-start(bf16[512,1024]{1,0:T(8,128)(2,1)S(1)} %broadcast_select_fusion.refs_1_), channel_id=1, source_target_pairs={{0,2},{2,0},{4,6},{6,4},{8,10},{10,8},{12,14},{14,12},{1,3},{3,1},... | collective-permute-start | bytes 3145736 | tf_op jit(solution)/shard_map/ppermute | solution.py:227
  58.3 37.2 %collective-permute-start.10 = (bf16[512,512]{1,0:T(8,128)(2,1)S(1)}, bf16[512,512]{1,0:T(8,128)(2,1)S(1)}, u32[]{:S(2)}, u32[]{:S(2)}) collective-permute-start(bf16[512,512]{1,0:T(8,128)(2,1)S(1)} %slice.27), channel_id=1, source_target_pairs={{4,8},{6,10},{8,4},{10,6},{5,9},{7,11},{9,5},{11,7},{20,24},{22,26... | collective-permute-start | bytes 1572872 | tf_op jit(solution)/shard_map/ppermute | solution.py:216
  79.6 16.0 %collective-permute-start.9 = (bf16[512,512]{1,0:T(8,128)(2,1)S(1)}, bf16[512,512]{1,0:T(8,128)(2,1)S(1)}, u32[]{:S(2)}, u32[]{:S(2)}) collective-permute-start(bf16[512,512]{1,0:T(8,128)(2,1)S(1)} %slice.26), channel_id=1, source_target_pairs={{4,0},{6,2},{8,12},{10,14},{5,1},{7,3},{9,13},{11,15},{20,16},{22,... | collective-permute-start | bytes 1572872 | tf_op jit(solution)/shard_map/ppermute | solution.py:216
  80.9 14.7 %collective-permute-start.8 = (bf16[512,512]{1,0:T(8,128)(2,1)S(1)}, bf16[512,512]{1,0:T(8,128)(2,1)S(1)}, u32[]{:S(2)}, u32[]{:S(2)}) collective-permute-start(bf16[512,512]{1,0:T(8,128)(2,1)S(1)} %slice_select_fusion), channel_id=1, source_target_pairs={{0,2},{2,0},{4,6},{6,4},{8,10},{10,8},{12,14},{14,12},{1,3},{3,1},... | collective-permute-start | bytes 1572872 | tf_op jit(solution)/shard_map/ppermute | solution.py:227
  105.0 2.2 collective-permute-start.11
  118.9 3.2 %collective-permute-start.12 = (f32[16,8,128]{2,1,0:T(8,128)S(1)}, f32[16,8,128]{2,1,0:T(8,128)S(1)}, u32[]{:S(2)}, u32[]{:S(2)}) collective-permute-start(f32[16,8,128]{2,1,0:T(8,128)S(1)} %get-tuple-element.77), channel_id=1, source_target_pairs={{0,1},{2,3},{4,5},{6,7},{8,9},{10,11},{12,13},{14,15},{16,17},{18,... | collective-permute-start | bytes 196616 | tf_op jit(solution)/shard_map/ppermute | solution.py:19
  127.7 15.1 %collective-permute-start.13 = (bf16[256,1024]{1,0:T(8,128)(2,1)S(1)}, bf16[256,1024]{1,0:T(8,128)(2,1)S(1)}, u32[]{:S(2)}, u32[]{:S(2)}) collective-permute-start(bf16[256,1024]{1,0:T(8,128)(2,1)S(1)} %pieces.10.refs_0_), channel_id=1, source_target_pairs={{0,2},{2,0},{4,6},{6,4},{8,10},{10,8},{12,14},{14,12},{1,3},{3,1},... | collective-permute-start | bytes 1572872 | tf_op jit(solution)/shard_map/ppermute | solution.py:227
  134.4 16.9 %collective-permute-start.14 = (bf16[256,1024]{1,0:T(8,128)(2,1)S(1)}, bf16[256,1024]{1,0:T(8,128)(2,1)S(1)}, u32[]{:S(2)}, u32[]{:S(2)}) collective-permute-start(bf16[256,1024]{1,0:T(8,128)(2,1)S(1)} %pieces.12.refs_0_), channel_id=1, source_target_pairs={{0,4},{2,6},{12,8},{14,10},{1,5},{3,7},{13,9},{15,11},{16,20},{18,... | collective-permute-start | bytes 1572872 | tf_op jit(solution)/shard_map/ppermute | solution.py:216
  143.0 19.6 %collective-permute-start.17 = (bf16[256,1024]{1,0:T(8,128)(2,1)S(1)}, bf16[256,1024]{1,0:T(8,128)(2,1)S(1)}, u32[]{:S(2)}, u32[]{:S(2)}) collective-permute-start(bf16[256,1024]{1,0:T(8,128)(2,1)S(1)} %add_convert_fusion.7), channel_id=1, source_target_pairs={{0,4},{2,6},{12,8},{14,10},{1,5},{3,7},{13,9},{15,11},{16,20},{18,... | collective-permute-start | bytes 1572872 | tf_op jit(solution)/shard_map/ppermute | solution.py:216
  146.7 15.8 %collective-permute-start.16 = (bf16[256,1024]{1,0:T(8,128)(2,1)S(1)}, bf16[256,1024]{1,0:T(8,128)(2,1)S(1)}, u32[]{:S(2)}, u32[]{:S(2)}) collective-permute-start(bf16[256,1024]{1,0:T(8,128)(2,1)S(1)} %get-tuple-element.88), channel_id=1, source_target_pairs={{0,2},{2,0},{4,6},{6,4},{8,10},{10,8},{12,14},{14,12},{1,3},{3,1},... | collective-permute-start | bytes 1572872 | tf_op jit(solution)/shard_map/ppermute | solution.py:227
  151.5 23.2 %collective-permute-start.15 = (bf16[256,1024]{1,0:T(8,128)(2,1)S(1)}, bf16[256,1024]{1,0:T(8,128)(2,1)S(1)}, u32[]{:S(2)}, u32[]{:S(2)}) collective-permute-start(bf16[256,1024]{1,0:T(8,128)(2,1)S(1)} %add_convert_fusion.8), channel_id=1, source_target_pairs={{0,2},{2,0},{4,6},{6,4},{8,10},{10,8},{12,14},{14,12},{1,3},{3,1},... | collective-permute-start | bytes 1572872 | tf_op jit(solution)/shard_map/ppermute | solution.py:227
  153.1 23.2 %collective-permute-start.24 = (bf16[256,1024]{1,0:T(8,128)(2,1)S(1)}, bf16[256,1024]{1,0:T(8,128)(2,1)S(1)}, u32[]{:S(2)}, u32[]{:S(2)}) collective-permute-start(bf16[256,1024]{1,0:T(8,128)(2,1)S(1)} %get-tuple-element.85.refs_0_), channel_id=1, source_target_pairs={{0,4},{2,6},{12,8},{14,10},{1,5},{3,7},{13,9},{15,11},{16,20},{18,... | collective-permute-start | bytes 1572872 | tf_op jit(solution)/shard_map/ppermute | solution.py:216
  157.5 24.7 %collective-permute-start.25 = (bf16[256,1024]{1,0:T(8,128)(2,1)S(1)}, bf16[256,1024]{1,0:T(8,128)(2,1)S(1)}, u32[]{:S(2)}, u32[]{:S(2)}) collective-permute-start(bf16[256,1024]{1,0:T(8,128)(2,1)S(1)} %pieces.12.refs_0_), channel_id=1, source_target_pairs={{4,8},{6,10},{8,4},{10,6},{5,9},{7,11},{9,5},{11,7},{20,24},{22,26... | collective-permute-start | bytes 1572872 | tf_op jit(solution)/shard_map/ppermute | solution.py:216
  162.8 28.0 %collective-permute-start.21 = (bf16[256,1024]{1,0:T(8,128)(2,1)S(1)}, bf16[256,1024]{1,0:T(8,128)(2,1)S(1)}, u32[]{:S(2)}, u32[]{:S(2)}) collective-permute-start(bf16[256,1024]{1,0:T(8,128)(2,1)S(1)} %add_convert_fusion.6), channel_id=1, source_target_pairs={{4,8},{6,10},{8,4},{10,6},{5,9},{7,11},{9,5},{11,7},{20,24},{22,26... | collective-permute-start | bytes 1572872 | tf_op jit(solution)/shard_map/ppermute | solution.py:216
  163.5 21.5 %collective-permute-start.18 = (bf16[256,1024]{1,0:T(8,128)(2,1)S(1)}, bf16[256,1024]{1,0:T(8,128)(2,1)S(1)}, u32[]{:S(2)}, u32[]{:S(2)}) collective-permute-start(bf16[256,1024]{1,0:T(8,128)(2,1)S(1)} %add_convert_fusion.6), channel_id=1, source_target_pairs={{0,4},{2,6},{12,8},{14,10},{1,5},{3,7},{13,9},{15,11},{16,20},{18,... | collective-permute-start | bytes 1572872 | tf_op jit(solution)/shard_map/ppermute | solution.py:216
  174.7 15.5 %collective-permute-start.19 = (bf16[256,1024]{1,0:T(8,128)(2,1)S(1)}, bf16[256,1024]{1,0:T(8,128)(2,1)S(1)}, u32[]{:S(2)}, u32[]{:S(2)}) collective-permute-start(bf16[256,1024]{1,0:T(8,128)(2,1)S(1)} %get-tuple-element.92), channel_id=1, source_target_pairs={{0,2},{2,0},{4,6},{6,4},{8,10},{10,8},{12,14},{14,12},{1,3},{3,1},... | collective-permute-start | bytes 1572872 | tf_op jit(solution)/shard_map/ppermute | solution.py:227
  176.6 19.7 %collective-permute-start.30 = (bf16[256,1024]{1,0:T(8,128)(2,1)S(1)}, bf16[256,1024]{1,0:T(8,128)(2,1)S(1)}, u32[]{:S(2)}, u32[]{:S(2)}) collective-permute-start(bf16[256,1024]{1,0:T(8,128)(2,1)S(1)} %add_convert_fusion.3.refs_0_), channel_id=1, source_target_pairs={{0,4},{2,6},{12,8},{14,10},{1,5},{3,7},{13,9},{15,11},{16,20},{18,... | collective-permute-start | bytes 1572872 | tf_op jit(solution)/shard_map/ppermute | solution.py:216
  182.2 18.4 %collective-permute-start.28 = (bf16[256,1024]{1,0:T(8,128)(2,1)S(1)}, bf16[256,1024]{1,0:T(8,128)(2,1)S(1)}, u32[]{:S(2)}, u32[]{:S(2)}) collective-permute-start(bf16[256,1024]{1,0:T(8,128)(2,1)S(1)} %add_convert_fusion.3.refs_0_), channel_id=1, source_target_pairs={{4,8},{6,10},{8,4},{10,6},{5,9},{7,11},{9,5},{11,7},{20,24},{22,26... | collective-permute-start | bytes 1572872 | tf_op jit(solution)/shard_map/ppermute | solution.py:216
  185.0 14.9 %collective-permute-start.26 = (bf16[256,1024]{1,0:T(8,128)(2,1)S(1)}, bf16[256,1024]{1,0:T(8,128)(2,1)S(1)}, u32[]{:S(2)}, u32[]{:S(2)}) collective-permute-start(bf16[256,1024]{1,0:T(8,128)(2,1)S(1)} %get-tuple-element.98), channel_id=1, source_target_pairs={{0,2},{2,0},{4,6},{6,4},{8,10},{10,8},{12,14},{14,12},{1,3},{3,1},... | collective-permute-start | bytes 1572872 | tf_op jit(solution)/shard_map/ppermute | solution.py:227
  190.2 20.9 %collective-permute-start.20 = (bf16[256,1024]{1,0:T(8,128)(2,1)S(1)}, bf16[256,1024]{1,0:T(8,128)(2,1)S(1)}, u32[]{:S(2)}, u32[]{:S(2)}) collective-permute-start(bf16[256,1024]{1,0:T(8,128)(2,1)S(1)} %get-tuple-element.93), channel_id=1, source_target_pairs={{0,2},{2,0},{4,6},{6,4},{8,10},{10,8},{12,14},{14,12},{1,3},{3,1},... | collective-permute-start | bytes 1572872 | tf_op jit(solution)/shard_map/ppermute | solution.py:227
  191.1 28.7 %collective-permute-start.22 = (bf16[256,1024]{1,0:T(8,128)(2,1)S(1)}, bf16[256,1024]{1,0:T(8,128)(2,1)S(1)}, u32[]{:S(2)}, u32[]{:S(2)}) collective-permute-start(bf16[256,1024]{1,0:T(8,128)(2,1)S(1)} %add_convert_fusion.5), channel_id=1, source_target_pairs={{0,4},{2,6},{4,0},{6,2},{8,12},{10,14},{12,8},{14,10},{1,5},{3,7},... | collective-permute-start | bytes 1572872 | tf_op jit(solution)/shard_map/ppermute | solution.py:216
  196.2 23.5 %collective-permute-start.23 = (bf16[256,1024]{1,0:T(8,128)(2,1)S(1)}, bf16[256,1024]{1,0:T(8,128)(2,1)S(1)}, u32[]{:S(2)}, u32[]{:S(2)}) collective-permute-start(bf16[256,1024]{1,0:T(8,128)(2,1)S(1)} %add_convert_fusion.4), channel_id=1, source_target_pairs={{4,8},{6,10},{8,4},{10,6},{5,9},{7,11},{9,5},{11,7},{20,24},{22,26... | collective-permute-start | bytes 1572872 | tf_op jit(solution)/shard_map/ppermute | solution.py:216
  199.9 19.9 %collective-permute-start.31 = (bf16[256,1024]{1,0:T(8,128)(2,1)S(1)}, bf16[256,1024]{1,0:T(8,128)(2,1)S(1)}, u32[]{:S(2)}, u32[]{:S(2)}) collective-permute-start(bf16[256,1024]{1,0:T(8,128)(2,1)S(1)} %add_convert_fusion), channel_id=1, source_target_pairs={{4,8},{6,10},{8,4},{10,6},{5,9},{7,11},{9,5},{11,7},{20,24},{22,26... | collective-permute-start | bytes 1572872 | tf_op jit(solution)/shard_map/ppermute | solution.py:216
  200.6 19.6 %collective-permute-start.27 = (bf16[256,1024]{1,0:T(8,128)(2,1)S(1)}, bf16[256,1024]{1,0:T(8,128)(2,1)S(1)}, u32[]{:S(2)}, u32[]{:S(2)}) collective-permute-start(bf16[256,1024]{1,0:T(8,128)(2,1)S(1)} %add_convert_fusion.2), channel_id=1, source_target_pairs={{0,2},{2,0},{4,6},{6,4},{8,10},{10,8},{12,14},{14,12},{1,3},{3,1},... | collective-permute-start | bytes 1572872 | tf_op jit(solution)/shard_map/ppermute | solution.py:227
  211.1 9.6 %collective-permute-start.29 = (bf16[256,1024]{1,0:T(8,128)(2,1)S(1)}, bf16[256,1024]{1,0:T(8,128)(2,1)S(1)}, u32[]{:S(2)}, u32[]{:S(2)}) collective-permute-start(bf16[256,1024]{1,0:T(8,128)(2,1)S(1)} %add_convert_fusion.1), channel_id=1, source_target_pairs={{0,4},{2,6},{4,0},{6,2},{8,12},{10,14},{12,8},{14,10},{1,5},{3,7},... | collective-permute-start | bytes 1572872 | tf_op jit(solution)/shard_map/ppermute | solution.py:216
  (9 other events, 119.4 us)

commit v4 on v3

--- a/solution.py
+++ b/solution.py
@@ -151,16 +151,9 @@
             outs[j][...] = total.astype(outs[j].dtype)
 
 
-def pieces(table, out_weight, gated, wanted, *earlier):
+def pieces(out_weight, gated, wanted, *earlier):
     rows, chans = gated.shape
     count = len(wanted)
-
-    def place(t, p):
-        shard = p[wanted[0][0]]
-        for j in range(1, count):
-            shard = jnp.where(t == j, p[wanted[j][0]], shard)
-        return shard
-
     out = pl.pallas_call(
         functools.partial(pieces_kernel, count),
         grid_spec=pltpu.PrefetchScalarGridSpec(
@@ -168,16 +161,16 @@
             grid=(count,),
             in_specs=[
                 pl.BlockSpec((rows, chans), lambda t, p: (0, 0)),
-                pl.BlockSpec((chans, chans), lambda t, p: (0, place(t, p))),
+                pl.BlockSpec((chans, chans), lambda t, p: (0, p[t])),
             ]
             + [pl.BlockSpec(memory_space=pl.ANY)] * len(earlier),
             out_specs=[pl.BlockSpec((rows, chans), lambda t, p: (0, 0))] * count,
         ),
-        out_shape=[jax.ShapeDtypeStruct((rows, chans), dtype) for k, dtype in wanted],
+        out_shape=[jax.ShapeDtypeStruct((rows, chans), dtype) for place, dtype in wanted],
         compiler_params=pltpu.CompilerParams(vmem_limit_bytes=VMEM_LIMIT),
         cost_estimate=pl.CostEstimate(flops=count * 1000000, bytes_accessed=count * 100000, transcendentals=0),
         name="pieces",
-    )(table, gated, out_weight, *earlier)
+    )(jnp.stack([place.astype(jnp.int32) for place, dtype in wanted]), gated, out_weight, *earlier)
     return list(out)
 
 
@@ -270,12 +263,13 @@
     return [acc, more, rest], inv_rms, rim, params
 
 
-def project_and_reduce(table, upper, lower, out_weight, tokens):
+def project_and_reduce(upper, lower, out_weight, tokens):
     half = tokens.shape[0] // 2
-    send = lambda k: (2 * k + 1, jnp.bfloat16)
-    keep = lambda k: (2 * k, jnp.float32)
+    me = lax.axis_index("chan")
+    send = lambda k: (me ^ (2 * k + 1), jnp.bfloat16)
+    keep = lambda k: (me ^ (2 * k), jnp.float32)
     narrow = lambda a: a.astype(jnp.bfloat16)
-    make = functools.partial(pieces, table, out_weight)
+    make = functools.partial(pieces, out_weight)
     both = (0, 1)
 
     third_send_0 = make(upper, [send(3)])[0]
@@ -515,7 +509,7 @@
         half = rows // 2
         upper, state = respond(query, product, state, *filt, 0, half)
         lower = lambda *earlier: respond(query, product, state, *filt, half, half, *earlier)[0]
-        return project_and_reduce(table, upper, lower, out_weight, tokens)
+        return project_and_reduce(upper, lower, out_weight, tokens)
     gated = respond(query, product, state, *filt, 0, rows)[0]
     partial = jnp.dot(gated, out_weight, preferred_element_type=jnp.float32)
     branch = lax.psum_scatter(partial.astype(jnp.bfloat16), "chan", scatter_dimension=1, tiled=True)

time: 224 us -> 242 us (1.080)
  other arithmetic: 3.83 us -> 10.9 us
  waiting for transfers between devices: 41.1 us -> 47.3 us
  local copies, waits for them, and re-layouts: 4.28 us -> 8.9 us
    ppermute x11, waiting for transfers between devices: 13.9 us -> 24.3 us  [across(): return lax.ppermute(block, 'chan', [(c, c ^ 1) for c in range(count)])]
    convert_element_type x9, other arithmetic: 1.9 us -> 8.77 us  [project_and_reduce(): narrow = lambda a: a.astype(jnp.bfloat16)]
    unnamed x20 -> x22, local copies, waits for them, and re-layouts: 2.66 us -> 7.29 us
    ppermute x19, waiting for transfers between devices: 25.4 us -> 21.2 us  [along_line(): lax.ppermute(block, 'chan', [(2 * a + y, 2 * b + y) for a, b in pairs for...]
  transfers between devices with their start and end apart: 32 -> 32, of which waited for: 14 -> 12; matrix products, arithmetic and copies ran while one was open for 3% -> 6% of each run, Pallas kernels for 38% -> 35%
where the time goes in v4:
time: 242 us; the launch traced here: 241 us
  Pallas kernels  113 us (47%)
  starting transfers between devices  60 us (25%)
  waiting for transfers between devices  47.3 us (20%)
  other arithmetic  10.9 us (5%)
  local copies, waits for them, and re-layouts  8.9 us (4%)
    pallas_call x5, Pallas kernels, accumulate(): pl.pallas_call(functools.partial(accumulate_kernel, depths, pairs, width,...  60.9 us
    ppermute x19, starting transfers between devices, along_line(): lax.ppermute(block, 'chan', [(2 * a + y, 2 * b + y) for a, b in pairs for...  42.9 us
    pallas_call x10, Pallas kernels, pieces(): pl.pallas_call(functools.partial(pieces_kernel, count), grid_spec=pltpu.P...  33.1 us
    ppermute x11, waiting for transfers between devices, across(): return lax.ppermute(block, 'chan', [(c, c ^ 1) for c in range(count)])  24.3 us
    ppermute x19, waiting for transfers between devices, along_line(): lax.ppermute(block, 'chan', [(2 * a + y, 2 * b + y) for a, b in pairs for...  21.2 us
    ppermute x11, starting transfers between devices, across(): return lax.ppermute(block, 'chan', [(c, c ^ 1) for c in range(count)])  13.5 us
    pallas_call x1, Pallas kernels, convolve(): pl.pallas_call(functools.partial(convolve_kernel, len(parts)), grid=(rows...  11.3 us
    convert_element_type x9, other arithmetic, project_and_reduce(): narrow = lambda a: a.astype(jnp.bfloat16)  8.77 us
  transfers between devices with their start and end apart: 32, of which 12 were waited for; matrix products, arithmetic and copies ran while one was open for 6% of the time, Pallas kernels for 35%

profile of v4, /device:TPU:0, one launch (start us, length us, event | category | flops | bytes accessed | tf_op | source)
XLA Modules:
  0.0 240.7 jit_solution(6010741341763359918)
XLA Ops:
  0.0 3.0 %collective-permute-start = (bf16[512,1024]{1,0:T(8,128)(2,1)}, bf16[512,1024]{1,0:T(8,128)(2,1)S(1)}, u32[]{:S(2)}, u32[]{:S(2)}) collective-permute-start(bf16[512,1024]{1,0:T(8,128)(2,1)} %refs_0_.1), channel_id=1, source_target_pairs={{0,4},{2,6},{4,0},{6,2},{8,12},{10,14},{12,8},{14,10},{1,5},{3,7},... | collective-permute-start | bytes 3145736 | tf_op jit(solution)/shard_map/ppermute | solution.py:209
  7.4 9.4 %accumulate.5 = (f32[3,512,1024]{2,1,0:T(8,128)}, f32[512,128]{1,0:T(8,128)S(1)}) custom-call(s32[9]{0:T(128)S(1)} %pad_add_fusion.place_ref, bf16[512,1024]{1,0:T(8,128)(2,1)S(1)} %copy-done.3, f32[8,1,1024]{2,1,0:T(1,128)S(1)} %bitcast.16, bf16[3,8192,1024]{2,1,0:T(8,128)(2,1)} %refs_6_.3), custom_call_target="tpu_custom_call" | custom-call | flops 536870912 | bytes 6291456 | tf_op jit(solution)/shard_map/accumulate/pallas_call | solution.py:115
  16.8 9.6 %collective-permute-done.refs_1_ = bf16[512,1024]{1,0:T(8,128)(2,1)S(1)} collective-permute-done((bf16[512,1024]{1,0:T(8,128)(2,1)}, bf16[512,1024]{1,0:T(8,128)(2,1)S(1)}, u32[]{:S(2)}, u32[]{:S(2)}) %collective-permute-start) | collective-permute-done | bytes 1048608 | tf_op jit(solution)/shard_map/ppermute | solution.py:209
  35.0 14.2 %accumulate.6 = (f32[3,512,1024]{2,1,0:T(8,128)}, f32[512,128]{1,0:T(8,128)S(1)}) custom-call(s32[9]{0:T(128)S(1)} %pad_add_fusion.place_ref, bf16[512,1024]{1,0:T(8,128)(2,1)S(1)} %collective-permute-done.1.refs_0_, bf16[512,1024]{1,0:T(8,128)(2,1)S(1)} %collective-permute-done.refs_1_, ...), custom_call_target="tpu_custom_call", output_to_operand_aliasing={{0}: (7, {}), {1}: (8, {})} | custom-call | flops 1073741824 | bytes 12582912 | tf_op jit(solution)/shard_map/accumulate/pallas_call | solution.py:115
  50.4 4.9 %collective-permute-done.4 = bf16[512,1024]{1,0:T(8,128)(2,1)} collective-permute-done((bf16[512,1024]{1,0:T(8,128)(2,1)S(1)}, bf16[512,1024]{1,0:T(8,128)(2,1)}, u32[]{:S(2)}, u32[]{:S(2)}) %collective-permute-start.4) | collective-permute-done | bytes 1048608 | tf_op jit(solution)/shard_map/ppermute | solution.py:209
  59.0 14.8 %accumulate.7 = (f32[3,512,1024]{2,1,0:T(8,128)}, f32[512,128]{1,0:T(8,128)S(1)}) custom-call(s32[9]{0:T(128)S(1)} %pad_add_fusion.place_ref, bf16[512,1024]{1,0:T(8,128)(2,1)} %collective-permute-done.2.refs_0_, bf16[512,1024]{1,0:T(8,128)(2,1)S(1)} %broadcast_select_fusion.refs_1_, ...), custom_call_target="tpu_custom_call", output_to_operand_aliasing={{0}: (7, {}), {1}: (8, {})} | custom-call | flops 1073741824 | bytes 12582912 | tf_op jit(solution)/shard_map/accumulate/pallas_call | solution.py:115
  73.8 3.5 %collective-permute-done.7.refs_1_ = bf16[512,1024]{1,0:T(8,128)(2,1)S(1)} collective-permute-done((bf16[512,1024]{1,0:T(8,128)(2,1)}, bf16[512,1024]{1,0:T(8,128)(2,1)S(1)}, u32[]{:S(2)}, u32[]{:S(2)}) %collective-permute-start.7) | collective-permute-done | bytes 1048608 | tf_op jit(solution)/shard_map/ppermute | solution.py:209
  77.5 2.5 %collective-permute-done.6.refs_0_ = bf16[512,1024]{1,0:T(8,128)(2,1)S(1)} collective-permute-done((bf16[512,1024]{1,0:T(8,128)(2,1)S(1)}, bf16[512,1024]{1,0:T(8,128)(2,1)S(1)}, u32[]{:S(2)}, u32[]{:S(2)}) %collective-permute-start.6) | collective-permute-done | bytes 1048608 | tf_op jit(solution)/shard_map/ppermute | solution.py:220
  82.9 13.1 %accumulate.8 = (f32[3,512,1024]{2,1,0:T(8,128)}, f32[512,128]{1,0:T(8,128)S(1)}) custom-call(s32[9]{0:T(128)S(1)} %pad_add_fusion.place_ref, bf16[512,1024]{1,0:T(8,128)(2,1)S(1)} %collective-permute-done.6.refs_0_, bf16[512,1024]{1,0:T(8,128)(2,1)S(1)} %collective-permute-done.7.refs_1_, ...), custom_call_target="tpu_custom_call", output_to_operand_aliasing={{1}: (8, {})} | custom-call | flops 1073741824 | bytes 12582912 | tf_op jit(solution)/shard_map/accumulate/pallas_call | solution.py:115
  96.0 9.4 %accumulate.9 = (f32[3,512,1024]{2,1,0:T(8,128)}, f32[512,128]{1,0:T(8,128)S(1)}, f32[3,8,1024]{2,1,0:T(8,128)S(1)}) custom-call(s32[9]{0:T(128)S(1)} %pad_add_fusion.place_ref, bf16[512,512]{1,0:T(8,128)(2,1)S(1)} %collective-permute-done.8.refs_0_, bf16[512,512]{1,0:T(8,128)(2,1)S(1)} %collective-permute-done.9.refs_1_, ...), custom_call_target="tpu_custom_call", output_to_operand_aliasing={{1}: (8, {})} | custom-call | flops 536870912 | bytes 6291456 | tf_op jit(solution)/shard_map/accumulate/pallas_call | solution.py:115
  107.7 11.3 %convolve.1 = (f32[512,8,128]{2,1,0:T(8,128)S(1)}, f32[512,8,128]{2,1,0:T(8,128)S(1)}, f32[16,8,128]{2,1,0:T(8,128)S(1)}) custom-call(f32[3,512,1024]{2,1,0:T(8,128)} %get-tuple-element.61.refs_8_.refs_0_, f32[3,512,1024]{2,1,0:T(8,128)} %get-tuple-element.65.refs_9_.refs_1_, f32[3,512,1024]{2,1,0:T(8,128)} %get-tuple-element.70.refs_2_, ...), custom_call_target="tpu_custom_call" | custom-call | flops 57671680 | bytes 10485760 | tf_op jit(solution)/shard_map/convolve/pallas_call | solution.py:376
  125.1 2.7 %respond.2 = (bf16[256,1024]{1,0:T(8,128)(2,1)S(1)}, f32[16,8,128]{2,1,0:T(8,128)S(1)}) custom-call(f32[512,8,128]{2,1,0:T(8,128)S(1)} %get-tuple-element.75.q_ref, f32[512,8,128]{2,1,0:T(8,128)S(1)} %copy-done.1, f32[16,8,128]{2,1,0:T(8,128)S(1)} %collective-permute-done.12.enter_ref, f32[16,8,128]{2,1,0:T(8,128)S(1)} %bitcast.26, ...), custom_call_target="tpu_custom_call" | custom-call | flops 18350080 | bytes 20971520 | tf_op jit(solution)/shard_map/respond/pallas_call | solution.py:449
  127.9 3.2 %pieces.10.refs_0_ = bf16[256,1024]{1,0:T(8,128)(2,1)} custom-call(s32[1]{0:T(128)} %bitcast.7.place_ref, bf16[256,1024]{1,0:T(8,128)(2,1)S(1)} %get-tuple-element.80.gated_ref, bf16[1024,8192]{1,0:T(8,128)(2,1)} %w_ref.19), custom_call_target="tpu_custom_call" | custom-call | flops 1000000 | bytes 100000 | tf_op jit(solution)/shard_map/pieces/pallas_call | solution.py:157
  131.6 3.3 %respond.3 = (bf16[256,1024]{1,0:T(8,128)(2,1)S(1)}, f32[16,8,128]{2,1,0:T(8,128)}) custom-call(f32[512,8,128]{2,1,0:T(8,128)S(1)} %get-tuple-element.75.q_ref, f32[512,8,128]{2,1,0:T(8,128)S(1)} %copy-done.2, f32[16,8,128]{2,1,0:T(8,128)S(1)} %get-tuple-element.81.enter_ref, f32[16,8,128]{2,1,0:T(8,128)S(1)} %bitcast.27, f32[16,8,128]{2,1,0:T(8,128)S(1)} %bitcast.29, ...), custom_call_target="tpu_custom_call" | custom-call | flops 18350080 | bytes 20971520 | tf_op jit(solution)/shard_map/respond/pallas_call | solution.py:449
  134.9 2.3 pieces.12.refs_0_
  137.2 5.4 %collective-permute-start.14 = (bf16[256,1024]{1,0:T(8,128)(2,1)S(1)}, bf16[256,1024]{1,0:T(8,128)(2,1)}, u32[]{:S(2)}, u32[]{:S(2)}) collective-permute-start(bf16[256,1024]{1,0:T(8,128)(2,1)S(1)} %pieces.12.refs_0_), channel_id=1, source_target_pairs={{0,4},{2,6},{12,8},{14,10},{1,5},{3,7},{13,9},{15,11},{16,20},{18,... | collective-permute-start | bytes 1572872 | tf_op jit(solution)/shard_map/ppermute | solution.py:209
  142.6 4.5 %pieces.15 = (bf16[256,1024]{1,0:T(8,128)(2,1)}, f32[256,1024]{1,0:T(8,128)S(1)}) custom-call(s32[2]{0:T(128)S(1)} %pad_add_fusion.1.place_ref, bf16[256,1024]{1,0:T(8,128)(2,1)S(1)} %get-tuple-element.80.gated_ref, bf16[1024,8192]{1,0:T(8,128)(2,1)} %w_ref.19, bf16[256,1024]{1,0:T(8,128)(2,1)S(1)} %pieces.12.refs_0_), custom_call_target="tpu_custom_call" | custom-call | flops 2000000 | bytes 200000 | tf_op jit(solution)/shard_map/pieces/pallas_call | solution.py:157
  149.1 3.1 %collective-permute-start.17 = (bf16[256,1024]{1,0:T(8,128)(2,1)}, bf16[256,1024]{1,0:T(8,128)(2,1)S(1)}, u32[]{:S(2)}, u32[]{:S(2)}) collective-permute-start(bf16[256,1024]{1,0:T(8,128)(2,1)} %add_convert_fusion.7), channel_id=1, source_target_pairs={{0,4},{2,6},{12,8},{14,10},{1,5},{3,7},{13,9},{15,11},{16,20},{18,... | collective-permute-start | bytes 1572872 | tf_op jit(solution)/shard_map/ppermute | solution.py:209
  152.2 3.7 %pieces.11 = (bf16[256,1024]{1,0:T(8,128)(2,1)S(1)}, bf16[256,1024]{1,0:T(8,128)(2,1)S(1)}) custom-call(s32[2]{0:T(128)S(1)} %pad_add_fusion.1.place_ref, bf16[256,1024]{1,0:T(8,128)(2,1)S(1)} %get-tuple-element.82.gated_ref, bf16[1024,8192]{1,0:T(8,128)(2,1)} %w_ref.19, bf16[256,1024]{1,0:T(8,128)(2,1)} %collective-permute-done.13.refs_0_), custom_call_target="tpu_custom_call" | custom-call | flops 2000000 | bytes 200000 | tf_op jit(solution)/shard_map/pieces/pallas_call | solution.py:157
  158.5 4.4 %collective-permute-start.24 = (bf16[256,1024]{1,0:T(8,128)(2,1)S(1)}, bf16[256,1024]{1,0:T(8,128)(2,1)}, u32[]{:S(2)}, u32[]{:S(2)}) collective-permute-start(bf16[256,1024]{1,0:T(8,128)(2,1)S(1)} %get-tuple-element.85.refs_0_), channel_id=1, source_target_pairs={{0,4},{2,6},{12,8},{14,10},{1,5},{3,7},{13,9},{15,11},{16,20},{18,... | collective-permute-start | bytes 1572872 | tf_op jit(solution)/shard_map/ppermute | solution.py:209
  164.4 3.7 %pieces.14 = (f32[256,1024]{1,0:T(8,128)S(1)}, bf16[256,1024]{1,0:T(8,128)(2,1)S(1)}) custom-call(s32[2]{0:T(128)S(1)} %pad_add_fusion.3.place_ref, bf16[256,1024]{1,0:T(8,128)(2,1)S(1)} %get-tuple-element.80.gated_ref, bf16[1024,8192]{1,0:T(8,128)(2,1)} %w_ref.19, bf16[256,1024]{1,0:T(8,128)(2,1)S(1)} %get-tuple-element.85.refs_0_), custom_call_target="tpu_custom_call" | custom-call | flops 2000000 | bytes 200000 | tf_op jit(solution)/shard_map/pieces/pallas_call | solution.py:157
  168.1 3.7 %pieces.18 = (f32[256,1024]{1,0:T(8,128)S(1)}, bf16[256,1024]{1,0:T(8,128)(2,1)S(1)}) custom-call(s32[2]{0:T(128)S(1)} %pad_add_fusion.3.place_ref, bf16[256,1024]{1,0:T(8,128)(2,1)S(1)} %get-tuple-element.82.gated_ref, bf16[1024,8192]{1,0:T(8,128)(2,1)} %w_ref.19, bf16[256,1024]{1,0:T(8,128)(2,1)S(1)} %collective-permute-done.17.refs_0_), custom_call_target="tpu_custom_call" | custom-call | flops 2000000 | bytes 200000 | tf_op jit(solution)/shard_map/pieces/pallas_call | solution.py:157
  173.0 2.6 %collective-permute-done.24 = bf16[256,1024]{1,0:T(8,128)(2,1)} collective-permute-done((bf16[256,1024]{1,0:T(8,128)(2,1)S(1)}, bf16[256,1024]{1,0:T(8,128)(2,1)}, u32[]{:S(2)}, u32[]{:S(2)}) %collective-permute-start.24) | collective-permute-done | bytes 524320 | tf_op jit(solution)/shard_map/ppermute | solution.py:209
  176.9 4.5 %collective-permute-start.30 = (bf16[256,1024]{1,0:T(8,128)(2,1)S(1)}, bf16[256,1024]{1,0:T(8,128)(2,1)S(1)}, u32[]{:S(2)}, u32[]{:S(2)}) collective-permute-start(bf16[256,1024]{1,0:T(8,128)(2,1)S(1)} %add_convert_fusion.3.refs_0_), channel_id=1, source_target_pairs={{0,4},{2,6},{12,8},{14,10},{1,5},{3,7},{13,9},{15,11},{16,20},{18,... | collective-permute-start | bytes 1572872 | tf_op jit(solution)/shard_map/ppermute | solution.py:209
  183.9 4.3 %collective-permute-start.18 = (bf16[256,1024]{1,0:T(8,128)(2,1)S(1)}, bf16[256,1024]{1,0:T(8,128)(2,1)S(1)}, u32[]{:S(2)}, u32[]{:S(2)}) collective-permute-start(bf16[256,1024]{1,0:T(8,128)(2,1)S(1)} %add_convert_fusion.6), channel_id=1, source_target_pairs={{0,4},{2,6},{12,8},{14,10},{1,5},{3,7},{13,9},{15,11},{16,20},{18,... | collective-permute-start | bytes 1572872 | tf_op jit(solution)/shard_map/ppermute | solution.py:209
  188.9 3.7 %pieces.19 = (f32[256,1024]{1,0:T(8,128)S(1)}, bf16[256,1024]{1,0:T(8,128)(2,1)S(1)}) custom-call(s32[2]{0:T(128)S(1)} %pad_add_fusion.2.place_ref, bf16[256,1024]{1,0:T(8,128)(2,1)S(1)} %get-tuple-element.82.gated_ref, bf16[1024,8192]{1,0:T(8,128)(2,1)} %w_ref.19, bf16[256,1024]{1,0:T(8,128)(2,1)S(1)} %add_convert_fusion.3.refs_0_), custom_call_target="tpu_custom_call" | custom-call | flops 2000000 | bytes 200000 | tf_op jit(solution)/shard_map/pieces/pallas_call | solution.py:157
  195.5 12.0 %collective-permute-done.26 = bf16[256,1024]{1,0:T(8,128)(2,1)S(1)} collective-permute-done((bf16[256,1024]{1,0:T(8,128)(2,1)S(1)}, bf16[256,1024]{1,0:T(8,128)(2,1)S(1)}, u32[]{:S(2)}, u32[]{:S(2)}) %collective-permute-start.26) | collective-permute-done | bytes 524320 | tf_op jit(solution)/shard_map/ppermute | solution.py:220
  208.5 3.9 %collective-permute-start.29 = (bf16[256,1024]{1,0:T(8,128)(2,1)S(1)}, bf16[256,1024]{1,0:T(8,128)(2,1)S(1)}, u32[]{:S(2)}, u32[]{:S(2)}) collective-permute-start(bf16[256,1024]{1,0:T(8,128)(2,1)S(1)} %add_convert_fusion.1), channel_id=1, source_target_pairs={{0,4},{2,6},{4,0},{6,2},{8,12},{10,14},{12,8},{14,10},{1,5},{3,7},... | collective-permute-start | bytes 1572872 | tf_op jit(solution)/shard_map/ppermute | solution.py:209
  213.9 3.7 %pieces.16 = (f32[256,1024]{1,0:T(8,128)S(1)}, bf16[256,1024]{1,0:T(8,128)(2,1)S(1)}) custom-call(s32[2]{0:T(128)S(1)} %pad_add_fusion.2.place_ref, bf16[256,1024]{1,0:T(8,128)(2,1)S(1)} %get-tuple-element.80.gated_ref, bf16[1024,8192]{1,0:T(8,128)(2,1)} %w_ref.19, bf16[256,1024]{1,0:T(8,128)(2,1)S(1)} %collective-permute-done.18.refs_0_), custom_call_target="tpu_custom_call" | custom-call | flops 2000000 | bytes 200000 | tf_op jit(solution)/shard_map/pieces/pallas_call | solution.py:157
  219.8 3.8 %collective-permute-start.22 = (bf16[256,1024]{1,0:T(8,128)(2,1)S(1)}, bf16[256,1024]{1,0:T(8,128)(2,1)S(1)}, u32[]{:S(2)}, u32[]{:S(2)}) collective-permute-start(bf16[256,1024]{1,0:T(8,128)(2,1)S(1)} %add_convert_fusion.5), channel_id=1, source_target_pairs={{0,4},{2,6},{4,0},{6,2},{8,12},{10,14},{12,8},{14,10},{1,5},{3,7},... | collective-permute-start | bytes 1572872 | tf_op jit(solution)/shard_map/ppermute | solution.py:209
  227.5 2.4 pieces.17
  230.8 8.1 %collective-permute-done.20.refs_1_ = bf16[256,1024]{1,0:T(8,128)(2,1)S(1)} collective-permute-done((bf16[256,1024]{1,0:T(8,128)(2,1)S(1)}, bf16[256,1024]{1,0:T(8,128)(2,1)S(1)}, u32[]{:S(2)}, u32[]{:S(2)}) %collective-permute-start.20) | collective-permute-done | bytes 524320 | tf_op jit(solution)/shard_map/ppermute | solution.py:220
  (93 shorter events, 55.5 us)
Async XLA Ops:
  0.0 26.4 %collective-permute-start = (bf16[512,1024]{1,0:T(8,128)(2,1)}, bf16[512,1024]{1,0:T(8,128)(2,1)S(1)}, u32[]{:S(2)}, u32[]{:S(2)}) collective-permute-start(bf16[512,1024]{1,0:T(8,128)(2,1)} %refs_0_.1), channel_id=1, source_target_pairs={{0,4},{2,6},{4,0},{6,2},{8,12},{10,14},{12,8},{14,10},{1,5},{3,7},... | collective-permute-start | bytes 3145736 | tf_op jit(solution)/shard_map/ppermute | solution.py:209
  3.0 25.0 %collective-permute-start.3 = (bf16[512,1024]{1,0:T(8,128)(2,1)}, bf16[512,1024]{1,0:T(8,128)(2,1)S(1)}, u32[]{:S(2)}, u32[]{:S(2)}) collective-permute-start(bf16[512,1024]{1,0:T(8,128)(2,1)} %refs_0_.1), channel_id=1, source_target_pairs={{4,8},{6,10},{8,4},{10,6},{5,9},{7,11},{9,5},{11,7},{20,24},{22,26... | collective-permute-start | bytes 3145736 | tf_op jit(solution)/shard_map/ppermute | solution.py:209
  3.7 25.6 %collective-permute-start.1 = (bf16[512,1024]{1,0:T(8,128)(2,1)}, bf16[512,1024]{1,0:T(8,128)(2,1)S(1)}, u32[]{:S(2)}, u32[]{:S(2)}) collective-permute-start(bf16[512,1024]{1,0:T(8,128)(2,1)} %refs_0_.1), channel_id=1, source_target_pairs={{0,2},{2,0},{4,6},{6,4},{8,10},{10,8},{12,14},{14,12},{1,3},{3,1},... | collective-permute-start | bytes 3145736 | tf_op jit(solution)/shard_map/ppermute | solution.py:220
  26.4 22.7 %collective-permute-start.5 = (bf16[512,1024]{1,0:T(8,128)(2,1)S(1)}, bf16[512,1024]{1,0:T(8,128)(2,1)}, u32[]{:S(2)}, u32[]{:S(2)}) collective-permute-start(bf16[512,1024]{1,0:T(8,128)(2,1)S(1)} %collective-permute-done.refs_1_), channel_id=1, source_target_pairs={{4,8},{6,10},{8,4},{10,6},{5,9},{7,11},{9,5},{11,7},{20,24},{22,26... | collective-permute-start | bytes 3145736 | tf_op jit(solution)/shard_map/ppermute | solution.py:209
  28.0 27.3 %collective-permute-start.4 = (bf16[512,1024]{1,0:T(8,128)(2,1)S(1)}, bf16[512,1024]{1,0:T(8,128)(2,1)}, u32[]{:S(2)}, u32[]{:S(2)}) collective-permute-start(bf16[512,1024]{1,0:T(8,128)(2,1)S(1)} %collective-permute-done.3.refs_2_), channel_id=1, source_target_pairs={{4,0},{6,2},{8,12},{10,14},{5,1},{7,3},{9,13},{11,15},{20,16},{22,... | collective-permute-start | bytes 3145736 | tf_op jit(solution)/shard_map/ppermute | solution.py:209
  29.3 27.4 %collective-permute-start.2 = (bf16[512,1024]{1,0:T(8,128)(2,1)S(1)}, bf16[512,1024]{1,0:T(8,128)(2,1)}, u32[]{:S(2)}, u32[]{:S(2)}) collective-permute-start(bf16[512,1024]{1,0:T(8,128)(2,1)S(1)} %collective-permute-done.refs_1_), channel_id=1, source_target_pairs={{0,2},{2,0},{4,6},{6,4},{8,10},{10,8},{12,14},{14,12},{1,3},{3,1},... | collective-permute-start | bytes 3145736 | tf_op jit(solution)/shard_map/ppermute | solution.py:220
  49.1 28.2 %collective-permute-start.7 = (bf16[512,1024]{1,0:T(8,128)(2,1)}, bf16[512,1024]{1,0:T(8,128)(2,1)S(1)}, u32[]{:S(2)}, u32[]{:S(2)}) collective-permute-start(bf16[512,1024]{1,0:T(8,128)(2,1)} %collective-permute-done.5), channel_id=1, source_target_pairs={{4,0},{6,2},{8,12},{10,14},{5,1},{7,3},{9,13},{11,15},{20,16},{22,... | collective-permute-start | bytes 3145736 | tf_op jit(solution)/shard_map/ppermute | solution.py:209
  56.7 23.3 %collective-permute-start.6 = (bf16[512,1024]{1,0:T(8,128)(2,1)S(1)}, bf16[512,1024]{1,0:T(8,128)(2,1)S(1)}, u32[]{:S(2)}, u32[]{:S(2)}) collective-permute-start(bf16[512,1024]{1,0:T(8,128)(2,1)S(1)} %broadcast_select_fusion.refs_1_), channel_id=1, source_target_pairs={{0,2},{2,0},{4,6},{6,4},{8,10},{10,8},{12,14},{14,12},{1,3},{3,1},... | collective-permute-start | bytes 3145736 | tf_op jit(solution)/shard_map/ppermute | solution.py:220
  58.3 37.7 %collective-permute-start.10 = (bf16[512,512]{1,0:T(8,128)(2,1)S(1)}, bf16[512,512]{1,0:T(8,128)(2,1)S(1)}, u32[]{:S(2)}, u32[]{:S(2)}) collective-permute-start(bf16[512,512]{1,0:T(8,128)(2,1)S(1)} %slice.27), channel_id=1, source_target_pairs={{4,8},{6,10},{8,4},{10,6},{5,9},{7,11},{9,5},{11,7},{20,24},{22,26... | collective-permute-start | bytes 1572872 | tf_op jit(solution)/shard_map/ppermute | solution.py:209
  80.0 16.0 %collective-permute-start.8 = (bf16[512,512]{1,0:T(8,128)(2,1)S(1)}, bf16[512,512]{1,0:T(8,128)(2,1)S(1)}, u32[]{:S(2)}, u32[]{:S(2)}) collective-permute-start(bf16[512,512]{1,0:T(8,128)(2,1)S(1)} %slice_select_fusion), channel_id=1, source_target_pairs={{0,2},{2,0},{4,6},{6,4},{8,10},{10,8},{12,14},{14,12},{1,3},{3,1},... | collective-permute-start | bytes 1572872 | tf_op jit(solution)/shard_map/ppermute | solution.py:220
  81.6 14.4 %collective-permute-start.9 = (bf16[512,512]{1,0:T(8,128)(2,1)S(1)}, bf16[512,512]{1,0:T(8,128)(2,1)S(1)}, u32[]{:S(2)}, u32[]{:S(2)}) collective-permute-start(bf16[512,512]{1,0:T(8,128)(2,1)S(1)} %slice.26), channel_id=1, source_target_pairs={{4,0},{6,2},{8,12},{10,14},{5,1},{7,3},{9,13},{11,15},{20,16},{22,... | collective-permute-start | bytes 1572872 | tf_op jit(solution)/shard_map/ppermute | solution.py:209
  105.5 2.2 collective-permute-start.11
  120.4 3.1 %collective-permute-start.12 = (f32[16,8,128]{2,1,0:T(8,128)S(1)}, f32[16,8,128]{2,1,0:T(8,128)S(1)}, u32[]{:S(2)}, u32[]{:S(2)}) collective-permute-start(f32[16,8,128]{2,1,0:T(8,128)S(1)} %get-tuple-element.77), channel_id=1, source_target_pairs={{0,1},{2,3},{4,5},{6,7},{8,9},{10,11},{12,13},{14,15},{16,17},{18,... | collective-permute-start | bytes 196616 | tf_op jit(solution)/shard_map/ppermute | solution.py:19
  131.1 16.0 %collective-permute-start.13 = (bf16[256,1024]{1,0:T(8,128)(2,1)}, bf16[256,1024]{1,0:T(8,128)(2,1)}, u32[]{:S(2)}, u32[]{:S(2)}) collective-permute-start(bf16[256,1024]{1,0:T(8,128)(2,1)} %pieces.10.refs_0_), channel_id=1, source_target_pairs={{0,2},{2,0},{4,6},{6,4},{8,10},{10,8},{12,14},{14,12},{1,3},{3,1},... | collective-permute-start | bytes 1572872 | tf_op jit(solution)/shard_map/ppermute | solution.py:220
  137.2 18.7 %collective-permute-start.14 = (bf16[256,1024]{1,0:T(8,128)(2,1)S(1)}, bf16[256,1024]{1,0:T(8,128)(2,1)}, u32[]{:S(2)}, u32[]{:S(2)}) collective-permute-start(bf16[256,1024]{1,0:T(8,128)(2,1)S(1)} %pieces.12.refs_0_), channel_id=1, source_target_pairs={{0,4},{2,6},{12,8},{14,10},{1,5},{3,7},{13,9},{15,11},{16,20},{18,... | collective-permute-start | bytes 1572872 | tf_op jit(solution)/shard_map/ppermute | solution.py:209
  149.1 19.0 %collective-permute-start.17 = (bf16[256,1024]{1,0:T(8,128)(2,1)}, bf16[256,1024]{1,0:T(8,128)(2,1)S(1)}, u32[]{:S(2)}, u32[]{:S(2)}) collective-permute-start(bf16[256,1024]{1,0:T(8,128)(2,1)} %add_convert_fusion.7), channel_id=1, source_target_pairs={{0,4},{2,6},{12,8},{14,10},{1,5},{3,7},{13,9},{15,11},{16,20},{18,... | collective-permute-start | bytes 1572872 | tf_op jit(solution)/shard_map/ppermute | solution.py:209
  157.9 15.1 %collective-permute-start.15 = (bf16[256,1024]{1,0:T(8,128)(2,1)}, bf16[256,1024]{1,0:T(8,128)(2,1)S(1)}, u32[]{:S(2)}, u32[]{:S(2)}) collective-permute-start(bf16[256,1024]{1,0:T(8,128)(2,1)} %add_convert_fusion.8), channel_id=1, source_target_pairs={{0,2},{2,0},{4,6},{6,4},{8,10},{10,8},{12,14},{14,12},{1,3},{3,1},... | collective-permute-start | bytes 1572872 | tf_op jit(solution)/shard_map/ppermute | solution.py:220
  158.5 17.2 %collective-permute-start.24 = (bf16[256,1024]{1,0:T(8,128)(2,1)S(1)}, bf16[256,1024]{1,0:T(8,128)(2,1)}, u32[]{:S(2)}, u32[]{:S(2)}) collective-permute-start(bf16[256,1024]{1,0:T(8,128)(2,1)S(1)} %get-tuple-element.85.refs_0_), channel_id=1, source_target_pairs={{0,4},{2,6},{12,8},{14,10},{1,5},{3,7},{13,9},{15,11},{16,20},{18,... | collective-permute-start | bytes 1572872 | tf_op jit(solution)/shard_map/ppermute | solution.py:209
  162.9 19.7 %collective-permute-start.16 = (bf16[256,1024]{1,0:T(8,128)(2,1)}, bf16[256,1024]{1,0:T(8,128)(2,1)}, u32[]{:S(2)}, u32[]{:S(2)}) collective-permute-start(bf16[256,1024]{1,0:T(8,128)(2,1)} %get-tuple-element.88), channel_id=1, source_target_pairs={{0,2},{2,0},{4,6},{6,4},{8,10},{10,8},{12,14},{14,12},{1,3},{3,1},... | collective-permute-start | bytes 1572872 | tf_op jit(solution)/shard_map/ppermute | solution.py:220
  163.5 29.1 %collective-permute-start.25 = (bf16[256,1024]{1,0:T(8,128)(2,1)S(1)}, bf16[256,1024]{1,0:T(8,128)(2,1)S(1)}, u32[]{:S(2)}, u32[]{:S(2)}) collective-permute-start(bf16[256,1024]{1,0:T(8,128)(2,1)S(1)} %pieces.12.refs_0_), channel_id=1, source_target_pairs={{4,8},{6,10},{8,4},{10,6},{5,9},{7,11},{9,5},{11,7},{20,24},{22,26... | collective-permute-start | bytes 1572872 | tf_op jit(solution)/shard_map/ppermute | solution.py:209
  176.9 17.5 %collective-permute-start.30 = (bf16[256,1024]{1,0:T(8,128)(2,1)S(1)}, bf16[256,1024]{1,0:T(8,128)(2,1)S(1)}, u32[]{:S(2)}, u32[]{:S(2)}) collective-permute-start(bf16[256,1024]{1,0:T(8,128)(2,1)S(1)} %add_convert_fusion.3.refs_0_), channel_id=1, source_target_pairs={{0,4},{2,6},{12,8},{14,10},{1,5},{3,7},{13,9},{15,11},{16,20},{18,... | collective-permute-start | bytes 1572872 | tf_op jit(solution)/shard_map/ppermute | solution.py:209
  181.5 26.8 %collective-permute-start.28 = (bf16[256,1024]{1,0:T(8,128)(2,1)S(1)}, bf16[256,1024]{1,0:T(8,128)(2,1)S(1)}, u32[]{:S(2)}, u32[]{:S(2)}) collective-permute-start(bf16[256,1024]{1,0:T(8,128)(2,1)S(1)} %add_convert_fusion.3.refs_0_), channel_id=1, source_target_pairs={{4,8},{6,10},{8,4},{10,6},{5,9},{7,11},{9,5},{11,7},{20,24},{22,26... | collective-permute-start | bytes 1572872 | tf_op jit(solution)/shard_map/ppermute | solution.py:209
  183.9 28.5 %collective-permute-start.18 = (bf16[256,1024]{1,0:T(8,128)(2,1)S(1)}, bf16[256,1024]{1,0:T(8,128)(2,1)S(1)}, u32[]{:S(2)}, u32[]{:S(2)}) collective-permute-start(bf16[256,1024]{1,0:T(8,128)(2,1)S(1)} %add_convert_fusion.6), channel_id=1, source_target_pairs={{0,4},{2,6},{12,8},{14,10},{1,5},{3,7},{13,9},{15,11},{16,20},{18,... | collective-permute-start | bytes 1572872 | tf_op jit(solution)/shard_map/ppermute | solution.py:209
  188.2 31.3 %collective-permute-start.21 = (bf16[256,1024]{1,0:T(8,128)(2,1)S(1)}, bf16[256,1024]{1,0:T(8,128)(2,1)S(1)}, u32[]{:S(2)}, u32[]{:S(2)}) collective-permute-start(bf16[256,1024]{1,0:T(8,128)(2,1)S(1)} %add_convert_fusion.6), channel_id=1, source_target_pairs={{4,8},{6,10},{8,4},{10,6},{5,9},{7,11},{9,5},{11,7},{20,24},{22,26... | collective-permute-start | bytes 1572872 | tf_op jit(solution)/shard_map/ppermute | solution.py:209
  192.6 14.9 %collective-permute-start.26 = (bf16[256,1024]{1,0:T(8,128)(2,1)S(1)}, bf16[256,1024]{1,0:T(8,128)(2,1)S(1)}, u32[]{:S(2)}, u32[]{:S(2)}) collective-permute-start(bf16[256,1024]{1,0:T(8,128)(2,1)S(1)} %get-tuple-element.98), channel_id=1, source_target_pairs={{0,2},{2,0},{4,6},{6,4},{8,10},{10,8},{12,14},{14,12},{1,3},{3,1},... | collective-permute-start | bytes 1572872 | tf_op jit(solution)/shard_map/ppermute | solution.py:220
  194.4 24.4 %collective-permute-start.19 = (bf16[256,1024]{1,0:T(8,128)(2,1)S(1)}, bf16[256,1024]{1,0:T(8,128)(2,1)S(1)}, u32[]{:S(2)}, u32[]{:S(2)}) collective-permute-start(bf16[256,1024]{1,0:T(8,128)(2,1)S(1)} %get-tuple-element.92), channel_id=1, source_target_pairs={{0,2},{2,0},{4,6},{6,4},{8,10},{10,8},{12,14},{14,12},{1,3},{3,1},... | collective-permute-start | bytes 1572872 | tf_op jit(solution)/shard_map/ppermute | solution.py:220
  207.6 16.1 %collective-permute-start.31 = (bf16[256,1024]{1,0:T(8,128)(2,1)S(1)}, bf16[256,1024]{1,0:T(8,128)(2,1)S(1)}, u32[]{:S(2)}, u32[]{:S(2)}) collective-permute-start(bf16[256,1024]{1,0:T(8,128)(2,1)S(1)} %add_convert_fusion), channel_id=1, source_target_pairs={{4,8},{6,10},{8,4},{10,6},{5,9},{7,11},{9,5},{11,7},{20,24},{22,26... | collective-permute-start | bytes 1572872 | tf_op jit(solution)/shard_map/ppermute | solution.py:209
  208.5 21.8 %collective-permute-start.29 = (bf16[256,1024]{1,0:T(8,128)(2,1)S(1)}, bf16[256,1024]{1,0:T(8,128)(2,1)S(1)}, u32[]{:S(2)}, u32[]{:S(2)}) collective-permute-start(bf16[256,1024]{1,0:T(8,128)(2,1)S(1)} %add_convert_fusion.1), channel_id=1, source_target_pairs={{0,4},{2,6},{4,0},{6,2},{8,12},{10,14},{12,8},{14,10},{1,5},{3,7},... | collective-permute-start | bytes 1572872 | tf_op jit(solution)/shard_map/ppermute | solution.py:209
  212.4 17.9 %collective-permute-start.27 = (bf16[256,1024]{1,0:T(8,128)(2,1)S(1)}, bf16[256,1024]{1,0:T(8,128)(2,1)S(1)}, u32[]{:S(2)}, u32[]{:S(2)}) collective-permute-start(bf16[256,1024]{1,0:T(8,128)(2,1)S(1)} %add_convert_fusion.2), channel_id=1, source_target_pairs={{0,2},{2,0},{4,6},{6,4},{8,10},{10,8},{12,14},{14,12},{1,3},{3,1},... | collective-permute-start | bytes 1572872 | tf_op jit(solution)/shard_map/ppermute | solution.py:220
  218.9 11.5 %collective-permute-start.23 = (bf16[256,1024]{1,0:T(8,128)(2,1)S(1)}, bf16[256,1024]{1,0:T(8,128)(2,1)S(1)}, u32[]{:S(2)}, u32[]{:S(2)}) collective-permute-start(bf16[256,1024]{1,0:T(8,128)(2,1)S(1)} %add_convert_fusion.4), channel_id=1, source_target_pairs={{4,8},{6,10},{8,4},{10,6},{5,9},{7,11},{9,5},{11,7},{20,24},{22,26... | collective-permute-start | bytes 1572872 | tf_op jit(solution)/shard_map/ppermute | solution.py:209
  219.8 11.0 %collective-permute-start.22 = (bf16[256,1024]{1,0:T(8,128)(2,1)S(1)}, bf16[256,1024]{1,0:T(8,128)(2,1)S(1)}, u32[]{:S(2)}, u32[]{:S(2)}) collective-permute-start(bf16[256,1024]{1,0:T(8,128)(2,1)S(1)} %add_convert_fusion.5), channel_id=1, source_target_pairs={{0,4},{2,6},{4,0},{6,2},{8,12},{10,14},{12,8},{14,10},{1,5},{3,7},... | collective-permute-start | bytes 1572872 | tf_op jit(solution)/shard_map/ppermute | solution.py:209
  223.6 15.3 %collective-permute-start.20 = (bf16[256,1024]{1,0:T(8,128)(2,1)S(1)}, bf16[256,1024]{1,0:T(8,128)(2,1)S(1)}, u32[]{:S(2)}, u32[]{:S(2)}) collective-permute-start(bf16[256,1024]{1,0:T(8,128)(2,1)S(1)} %get-tuple-element.93), channel_id=1, source_target_pairs={{0,2},{2,0},{4,6},{6,4},{8,10},{10,8},{12,14},{14,12},{1,3},{3,1},... | collective-permute-start | bytes 1572872 | tf_op jit(solution)/shard_map/ppermute | solution.py:220
  (10 other events, 82.0 us)

commit v5 on v2

--- a/solution.py
+++ b/solution.py
@@ -392,7 +392,7 @@
     groups = chans // LANES
     tap_count, poles = taps.shape[1], log_decay.shape[0]
     count = len(parts)
-    blk = min(128, rows // 2)
+    blk = min(64, rows // 2)
     whole = lambda *shape: pl.BlockSpec(shape, lambda t: (0,) * len(shape))
     start = 1 if rim is None else 0
     row_spec = pl.BlockSpec((blk, groups, LANES), lambda t: (t + start, 0, 0))

time: 225 us -> 224 us (level)
  transfers between devices with their start and end apart: 32 -> 32, of which waited for: 13 -> 13; matrix products, arithmetic and copies ran while one was open for 3% -> 3% of each run, Pallas kernels for 42% -> 43%
where the time goes in v5:
time: 224 us; the launch traced here: 223 us
  Pallas kernels  116 us (52%)
  starting transfers between devices  57.9 us (26%)
  waiting for transfers between devices  40.3 us (18%)
  local copies, waits for them, and re-layouts  4.29 us (2%)
  other arithmetic  3.79 us (2%)
    pallas_call x5, Pallas kernels, accumulate(): pl.pallas_call(functools.partial(accumulate_kernel, depths, pairs, width,...  60.9 us
    ppermute x19, starting transfers between devices, along_line(): lax.ppermute(block, 'chan', [(2 * a + y, 2 * b + y) for a, b in pairs for...  40.8 us
    pallas_call x10, Pallas kernels, pieces(): pl.pallas_call(functools.partial(pieces_kernel, count), grid_spec=pltpu.P...  33.5 us
    ppermute x19, waiting for transfers between devices, along_line(): lax.ppermute(block, 'chan', [(2 * a + y, 2 * b + y) for a, b in pairs for...  25.5 us
    ppermute x11, starting transfers between devices, across(): return lax.ppermute(block, 'chan', [(c, c ^ 1) for c in range(count)])  14.5 us
    ppermute x11, waiting for transfers between devices, across(): return lax.ppermute(block, 'chan', [(c, c ^ 1) for c in range(count)])  13.9 us
    pallas_call x2, Pallas kernels, convolve(): pl.pallas_call(functools.partial(convolve_kernel, count, None if rim is N...  13.6 us
    pallas_call x2, Pallas kernels, respond(): pl.pallas_call(respond_kernel, grid=(rows // blk,), in_specs=[row_spec, r...  5.99 us
  transfers between devices with their start and end apart: 32, of which 13 were waited for; matrix products, arithmetic and copies ran while one was open for 3% of the time, Pallas kernels for 43%

profile of v5, /device:TPU:0, one launch (start us, length us, event | category | flops | bytes accessed | tf_op | source)
XLA Modules:
  0.0 222.5 jit_solution(10096805779676553525)
XLA Ops:
  0.0 3.0 %collective-permute-start = (bf16[512,1024]{1,0:T(8,128)(2,1)}, bf16[512,1024]{1,0:T(8,128)(2,1)S(1)}, u32[]{:S(2)}, u32[]{:S(2)}) collective-permute-start(bf16[512,1024]{1,0:T(8,128)(2,1)} %refs_0_.1), channel_id=1, source_target_pairs={{0,4},{2,6},{4,0},{6,2},{8,12},{10,14},{12,8},{14,10},{1,5},{3,7},... | collective-permute-start | bytes 3145736 | tf_op jit(solution)/shard_map/ppermute | solution.py:216
  7.4 9.4 %accumulate.5 = (f32[3,512,1024]{2,1,0:T(8,128)}, f32[512,128]{1,0:T(8,128)S(1)}) custom-call(s32[9]{0:T(128)S(1)} %pad_add_fusion.place_ref, bf16[512,1024]{1,0:T(8,128)(2,1)S(1)} %copy-done, f32[8,1,1024]{2,1,0:T(1,128)S(1)} %bitcast.8, bf16[3,8192,1024]{2,1,0:T(8,128)(2,1)} %refs_6_.3), custom_call_target="tpu_custom_call" | custom-call | flops 536870912 | bytes 6291456 | tf_op jit(solution)/shard_map/accumulate/pallas_call | solution.py:115
  16.8 9.6 %collective-permute-done.refs_1_ = bf16[512,1024]{1,0:T(8,128)(2,1)S(1)} collective-permute-done((bf16[512,1024]{1,0:T(8,128)(2,1)}, bf16[512,1024]{1,0:T(8,128)(2,1)S(1)}, u32[]{:S(2)}, u32[]{:S(2)}) %collective-permute-start) | collective-permute-done | bytes 1048608 | tf_op jit(solution)/shard_map/ppermute | solution.py:216
  33.3 14.2 %accumulate.6 = (f32[3,512,1024]{2,1,0:T(8,128)}, f32[512,128]{1,0:T(8,128)S(1)}) custom-call(s32[9]{0:T(128)S(1)} %pad_add_fusion.place_ref, bf16[512,1024]{1,0:T(8,128)(2,1)S(1)} %collective-permute-done.1.refs_0_, bf16[512,1024]{1,0:T(8,128)(2,1)S(1)} %collective-permute-done.refs_1_, ...), custom_call_target="tpu_custom_call", output_to_operand_aliasing={{0}: (7, {}), {1}: (8, {})} | custom-call | flops 1073741824 | bytes 12582912 | tf_op jit(solution)/shard_map/accumulate/pallas_call | solution.py:115
  48.8 6.6 %collective-permute-done.4 = bf16[512,1024]{1,0:T(8,128)(2,1)} collective-permute-done((bf16[512,1024]{1,0:T(8,128)(2,1)S(1)}, bf16[512,1024]{1,0:T(8,128)(2,1)}, u32[]{:S(2)}, u32[]{:S(2)}) %collective-permute-start.4) | collective-permute-done | bytes 1048608 | tf_op jit(solution)/shard_map/ppermute | solution.py:216
  59.0 14.8 %accumulate.7 = (f32[3,512,1024]{2,1,0:T(8,128)}, f32[512,128]{1,0:T(8,128)S(1)}) custom-call(s32[9]{0:T(128)S(1)} %pad_add_fusion.place_ref, bf16[512,1024]{1,0:T(8,128)(2,1)} %collective-permute-done.2.refs_0_, bf16[512,1024]{1,0:T(8,128)(2,1)S(1)} %broadcast_select_fusion.refs_1_, ...), custom_call_target="tpu_custom_call", output_to_operand_aliasing={{0}: (7, {}), {1}: (8, {})} | custom-call | flops 1073741824 | bytes 12582912 | tf_op jit(solution)/shard_map/accumulate/pallas_call | solution.py:115
  73.8 3.5 %collective-permute-done.7.refs_1_ = bf16[512,1024]{1,0:T(8,128)(2,1)S(1)} collective-permute-done((bf16[512,1024]{1,0:T(8,128)(2,1)}, bf16[512,1024]{1,0:T(8,128)(2,1)S(1)}, u32[]{:S(2)}, u32[]{:S(2)}) %collective-permute-start.7) | collective-permute-done | bytes 1048608 | tf_op jit(solution)/shard_map/ppermute | solution.py:216
  82.5 13.1 %accumulate.8 = (f32[3,512,1024]{2,1,0:T(8,128)}, f32[512,128]{1,0:T(8,128)S(1)}) custom-call(s32[9]{0:T(128)S(1)} %pad_add_fusion.place_ref, bf16[512,1024]{1,0:T(8,128)(2,1)S(1)} %collective-permute-done.6.refs_0_, bf16[512,1024]{1,0:T(8,128)(2,1)S(1)} %collective-permute-done.7.refs_1_, ...), custom_call_target="tpu_custom_call", output_to_operand_aliasing={{1}: (8, {})} | custom-call | flops 1073741824 | bytes 12582912 | tf_op jit(solution)/shard_map/accumulate/pallas_call | solution.py:115
  95.6 9.4 %accumulate.9 = (f32[3,512,1024]{2,1,0:T(8,128)}, f32[512,128]{1,0:T(8,128)S(1)}, f32[3,8,1024]{2,1,0:T(8,128)S(1)}) custom-call(s32[9]{0:T(128)S(1)} %pad_add_fusion.place_ref, bf16[512,512]{1,0:T(8,128)(2,1)S(1)} %collective-permute-done.8.refs_0_, bf16[512,512]{1,0:T(8,128)(2,1)S(1)} %collective-permute-done.9.refs_1_, ...), custom_call_target="tpu_custom_call", output_to_operand_aliasing={{1}: (8, {})} | custom-call | flops 536870912 | bytes 6291456 | tf_op jit(solution)/shard_map/accumulate/pallas_call | solution.py:115
  106.4 10.9 %convolve.2 = (f32[512,8,128]{2,1,0:T(8,128)S(1)}, f32[512,8,128]{2,1,0:T(8,128)S(1)}, f32[16,8,128]{2,1,0:T(8,128)S(1)}) custom-call(f32[3,512,1024]{2,1,0:T(8,128)} %get-tuple-element.64.refs_8_.refs_0_.refs_6_, f32[3,512,1024]{2,1,0:T(8,128)} %get-tuple-element.68.refs_9_.refs_1_.refs_7_, f32[3,512,1024]{2,1,0:T(8,128)} %get-tuple-element.73.refs_2_.refs_8_, ...), custom_call_target="tpu_custom_call" | custom-call | flops 41943040 | bytes 10485760 | tf_op jit(solution)/shard_map/convolve/pallas_call | solution.py:413
  117.3 2.7 %convolve.3 = (f32[512,8,128]{2,1,0:T(8,128)S(1)}, f32[512,8,128]{2,1,0:T(8,128)S(1)}, f32[16,8,128]{2,1,0:T(8,128)S(1)}) custom-call(f32[3,512,1024]{2,1,0:T(8,128)} %get-tuple-element.64.refs_8_.refs_0_.refs_6_, f32[3,512,1024]{2,1,0:T(8,128)} %get-tuple-element.68.refs_9_.refs_1_.refs_7_, ...), custom_call_target="tpu_custom_call", output_to_operand_aliasing={{0}: (8, {}), {1}: (9, {})} | custom-call | flops 41943040 | bytes 10485760 | tf_op jit(solution)/shard_map/convolve/pallas_call | solution.py:413
  122.2 2.7 %respond.2 = (bf16[256,1024]{1,0:T(8,128)(2,1)S(1)}, f32[16,8,128]{2,1,0:T(8,128)S(1)}) custom-call(f32[512,8,128]{2,1,0:T(8,128)S(1)} %get-tuple-element.81.q_ref, f32[512,8,128]{2,1,0:T(8,128)S(1)} %get-tuple-element.82.prod_ref, f32[16,8,128]{2,1,0:T(8,128)S(1)} %collective-permute-done.12.enter_ref, f32[16,8,128]{2,1,0:T(8,128)S(1)} %bitcast.19, ...), custom_call_target="tpu_custom_call" | custom-call | flops 18350080 | bytes 20971520 | tf_op jit(solution)/shard_map/respond/pallas_call | solution.py:481
  124.9 2.8 %pieces.10.refs_0_ = bf16[256,1024]{1,0:T(8,128)(2,1)S(1)} custom-call(s32[9]{0:T(128)S(1)} %pad_add_fusion.place_ref, bf16[256,1024]{1,0:T(8,128)(2,1)S(1)} %get-tuple-element.86.gated_ref, bf16[1024,8192]{1,0:T(8,128)(2,1)} %w_ref.19), custom_call_target="tpu_custom_call" | custom-call | flops 1000000 | bytes 100000 | tf_op jit(solution)/shard_map/pieces/pallas_call | solution.py:164
  128.3 3.3 %respond.3 = (bf16[256,1024]{1,0:T(8,128)(2,1)S(1)}, f32[16,8,128]{2,1,0:T(8,128)}) custom-call(f32[512,8,128]{2,1,0:T(8,128)S(1)} %get-tuple-element.81.q_ref, f32[512,8,128]{2,1,0:T(8,128)S(1)} %get-tuple-element.82.prod_ref, f32[16,8,128]{2,1,0:T(8,128)S(1)} %get-tuple-element.87.enter_ref, f32[16,8,128]{2,1,0:T(8,128)S(1)} %bitcast.20, ...), custom_call_target="tpu_custom_call" | custom-call | flops 18350080 | bytes 20971520 | tf_op jit(solution)/shard_map/respond/pallas_call | solution.py:481
  131.6 2.8 %pieces.12.refs_0_ = bf16[256,1024]{1,0:T(8,128)(2,1)S(1)} custom-call(s32[9]{0:T(128)S(1)} %pad_add_fusion.place_ref, bf16[256,1024]{1,0:T(8,128)(2,1)S(1)} %get-tuple-element.88.gated_ref, bf16[1024,8192]{1,0:T(8,128)(2,1)} %w_ref.19), custom_call_target="tpu_custom_call" | custom-call | flops 1000000 | bytes 100000 | tf_op jit(solution)/shard_map/pieces/pallas_call | solution.py:164
  134.4 4.6 %collective-permute-start.14 = (bf16[256,1024]{1,0:T(8,128)(2,1)S(1)}, bf16[256,1024]{1,0:T(8,128)(2,1)S(1)}, u32[]{:S(2)}, u32[]{:S(2)}) collective-permute-start(bf16[256,1024]{1,0:T(8,128)(2,1)S(1)} %pieces.12.refs_0_), channel_id=1, source_target_pairs={{0,4},{2,6},{12,8},{14,10},{1,5},{3,7},{13,9},{15,11},{16,20},{18,... | collective-permute-start | bytes 1572872 | tf_op jit(solution)/shard_map/ppermute | solution.py:216
  139.1 3.7 %pieces.15 = (bf16[256,1024]{1,0:T(8,128)(2,1)S(1)}, f32[256,1024]{1,0:T(8,128)S(1)}) custom-call(s32[9]{0:T(128)S(1)} %pad_add_fusion.place_ref, bf16[256,1024]{1,0:T(8,128)(2,1)S(1)} %get-tuple-element.86.gated_ref, bf16[1024,8192]{1,0:T(8,128)(2,1)} %w_ref.19, bf16[256,1024]{1,0:T(8,128)(2,1)S(1)} %pieces.12.refs_0_), custom_call_target="tpu_custom_call" | custom-call | flops 2000000 | bytes 200000 | tf_op jit(solution)/shard_map/pieces/pallas_call | solution.py:164
  142.9 3.8 %collective-permute-start.17 = (bf16[256,1024]{1,0:T(8,128)(2,1)S(1)}, bf16[256,1024]{1,0:T(8,128)(2,1)S(1)}, u32[]{:S(2)}, u32[]{:S(2)}) collective-permute-start(bf16[256,1024]{1,0:T(8,128)(2,1)S(1)} %add_convert_fusion.7), channel_id=1, source_target_pairs={{0,4},{2,6},{12,8},{14,10},{1,5},{3,7},{13,9},{15,11},{16,20},{18,... | collective-permute-start | bytes 1572872 | tf_op jit(solution)/shard_map/ppermute | solution.py:216
  147.4 3.7 %pieces.11 = (bf16[256,1024]{1,0:T(8,128)(2,1)S(1)}, bf16[256,1024]{1,0:T(8,128)(2,1)S(1)}) custom-call(s32[9]{0:T(128)S(1)} %pad_add_fusion.place_ref, bf16[256,1024]{1,0:T(8,128)(2,1)S(1)} %get-tuple-element.88.gated_ref, bf16[1024,8192]{1,0:T(8,128)(2,1)} %w_ref.19, bf16[256,1024]{1,0:T(8,128)(2,1)S(1)} %collective-permute-done.13.refs_0_), custom_call_target="tpu_custom_call" | custom-call | flops 2000000 | bytes 200000 | tf_op jit(solution)/shard_map/pieces/pallas_call | solution.py:164
  153.1 4.6 %collective-permute-start.24 = (bf16[256,1024]{1,0:T(8,128)(2,1)S(1)}, bf16[256,1024]{1,0:T(8,128)(2,1)S(1)}, u32[]{:S(2)}, u32[]{:S(2)}) collective-permute-start(bf16[256,1024]{1,0:T(8,128)(2,1)S(1)} %get-tuple-element.91.refs_0_), channel_id=1, source_target_pairs={{0,4},{2,6},{12,8},{14,10},{1,5},{3,7},{13,9},{15,11},{16,20},{18,... | collective-permute-start | bytes 1572872 | tf_op jit(solution)/shard_map/ppermute | solution.py:216
  158.4 3.7 %pieces.14 = (f32[256,1024]{1,0:T(8,128)S(1)}, bf16[256,1024]{1,0:T(8,128)(2,1)S(1)}) custom-call(s32[9]{0:T(128)S(1)} %pad_add_fusion.place_ref, bf16[256,1024]{1,0:T(8,128)(2,1)S(1)} %get-tuple-element.86.gated_ref, bf16[1024,8192]{1,0:T(8,128)(2,1)} %w_ref.19, bf16[256,1024]{1,0:T(8,128)(2,1)S(1)} %get-tuple-element.91.refs_0_), custom_call_target="tpu_custom_call" | custom-call | flops 2000000 | bytes 200000 | tf_op jit(solution)/shard_map/pieces/pallas_call | solution.py:164
  163.5 7.5 %collective-permute-start.18 = (bf16[256,1024]{1,0:T(8,128)(2,1)S(1)}, bf16[256,1024]{1,0:T(8,128)(2,1)S(1)}, u32[]{:S(2)}, u32[]{:S(2)}) collective-permute-start(bf16[256,1024]{1,0:T(8,128)(2,1)S(1)} %add_convert_fusion.6), channel_id=1, source_target_pairs={{0,4},{2,6},{12,8},{14,10},{1,5},{3,7},{13,9},{15,11},{16,20},{18,... | collective-permute-start | bytes 1572872 | tf_op jit(solution)/shard_map/ppermute | solution.py:216
  171.0 3.7 %pieces.18 = (f32[256,1024]{1,0:T(8,128)S(1)}, bf16[256,1024]{1,0:T(8,128)(2,1)S(1)}) custom-call(s32[9]{0:T(128)S(1)} %pad_add_fusion.place_ref, bf16[256,1024]{1,0:T(8,128)(2,1)S(1)} %get-tuple-element.88.gated_ref, bf16[1024,8192]{1,0:T(8,128)(2,1)} %w_ref.19, bf16[256,1024]{1,0:T(8,128)(2,1)S(1)} %collective-permute-done.17.refs_0_), custom_call_target="tpu_custom_call" | custom-call | flops 2000000 | bytes 200000 | tf_op jit(solution)/shard_map/pieces/pallas_call | solution.py:164
  178.4 3.7 %pieces.19 = (f32[256,1024]{1,0:T(8,128)S(1)}, bf16[256,1024]{1,0:T(8,128)(2,1)S(1)}) custom-call(s32[9]{0:T(128)S(1)} %pad_add_fusion.place_ref, bf16[256,1024]{1,0:T(8,128)(2,1)S(1)} %get-tuple-element.88.gated_ref, bf16[1024,8192]{1,0:T(8,128)(2,1)} %w_ref.19, bf16[256,1024]{1,0:T(8,128)(2,1)S(1)} %add_convert_fusion.3.refs_0_), custom_call_target="tpu_custom_call" | custom-call | flops 2000000 | bytes 200000 | tf_op jit(solution)/shard_map/pieces/pallas_call | solution.py:164
  186.5 3.7 %pieces.16 = (f32[256,1024]{1,0:T(8,128)S(1)}, bf16[256,1024]{1,0:T(8,128)(2,1)S(1)}) custom-call(s32[9]{0:T(128)S(1)} %pad_add_fusion.place_ref, bf16[256,1024]{1,0:T(8,128)(2,1)S(1)} %get-tuple-element.86.gated_ref, bf16[1024,8192]{1,0:T(8,128)(2,1)} %w_ref.19, bf16[256,1024]{1,0:T(8,128)(2,1)S(1)} %collective-permute-done.18.refs_0_), custom_call_target="tpu_custom_call" | custom-call | flops 2000000 | bytes 200000 | tf_op jit(solution)/shard_map/pieces/pallas_call | solution.py:164
  191.0 2.6 %collective-permute-start.22 = (bf16[256,1024]{1,0:T(8,128)(2,1)S(1)}, bf16[256,1024]{1,0:T(8,128)(2,1)S(1)}, u32[]{:S(2)}, u32[]{:S(2)}) collective-permute-start(bf16[256,1024]{1,0:T(8,128)(2,1)S(1)} %add_convert_fusion.5), channel_id=1, source_target_pairs={{0,4},{2,6},{4,0},{6,2},{8,12},{10,14},{12,8},{14,10},{1,5},{3,7},... | collective-permute-start | bytes 1572872 | tf_op jit(solution)/shard_map/ppermute | solution.py:216
  193.8 2.4 %collective-permute-done.30 = bf16[256,1024]{1,0:T(8,128)(2,1)S(1)} collective-permute-done((bf16[256,1024]{1,0:T(8,128)(2,1)S(1)}, bf16[256,1024]{1,0:T(8,128)(2,1)S(1)}, u32[]{:S(2)}, u32[]{:S(2)}) %collective-permute-start.30) | collective-permute-done | bytes 524320 | tf_op jit(solution)/shard_map/ppermute | solution.py:216
  197.1 2.7 %collective-permute-done.26 = bf16[256,1024]{1,0:T(8,128)(2,1)S(1)} collective-permute-done((bf16[256,1024]{1,0:T(8,128)(2,1)S(1)}, bf16[256,1024]{1,0:T(8,128)(2,1)S(1)}, u32[]{:S(2)}, u32[]{:S(2)}) %collective-permute-start.26) | collective-permute-done | bytes 524320 | tf_op jit(solution)/shard_map/ppermute | solution.py:227
  202.4 8.7 %collective-permute-done.20.refs_1_ = bf16[256,1024]{1,0:T(8,128)(2,1)S(1)} collective-permute-done((bf16[256,1024]{1,0:T(8,128)(2,1)S(1)}, bf16[256,1024]{1,0:T(8,128)(2,1)S(1)}, u32[]{:S(2)}, u32[]{:S(2)}) %collective-permute-start.20) | collective-permute-done | bytes 524320 | tf_op jit(solution)/shard_map/ppermute | solution.py:227
  211.1 2.5 %collective-permute-start.29 = (bf16[256,1024]{1,0:T(8,128)(2,1)S(1)}, bf16[256,1024]{1,0:T(8,128)(2,1)S(1)}, u32[]{:S(2)}, u32[]{:S(2)}) collective-permute-start(bf16[256,1024]{1,0:T(8,128)(2,1)S(1)} %add_convert_fusion.1), channel_id=1, source_target_pairs={{0,4},{2,6},{4,0},{6,2},{8,12},{10,14},{12,8},{14,10},{1,5},{3,7},... | collective-permute-start | bytes 1572872 | tf_op jit(solution)/shard_map/ppermute | solution.py:216
  213.6 2.8 %pieces.17 = f32[256,1024]{1,0:T(8,128)S(1)} custom-call(s32[9]{0:T(128)S(1)} %pad_add_fusion.place_ref, bf16[256,1024]{1,0:T(8,128)(2,1)S(1)} %get-tuple-element.88.gated_ref, bf16[1024,8192]{1,0:T(8,128)(2,1)} %w_ref.19, bf16[256,1024]{1,0:T(8,128)(2,1)S(1)} %collective-permute-done.15.refs_0_), custom_call_target="tpu_custom_call" | custom-call | flops 1000000 | bytes 100000 | tf_op jit(solution)/shard_map/pieces/pallas_call | solution.py:164
  216.4 2.8 %pieces.13 = f32[256,1024]{1,0:T(8,128)S(1)} custom-call(s32[9]{0:T(128)S(1)} %pad_add_fusion.place_ref, bf16[256,1024]{1,0:T(8,128)(2,1)S(1)} %get-tuple-element.86.gated_ref, bf16[1024,8192]{1,0:T(8,128)(2,1)} %w_ref.19, bf16[256,1024]{1,0:T(8,128)(2,1)S(1)} %collective-permute-done.15.refs_0_), custom_call_target="tpu_custom_call" | custom-call | flops 1000000 | bytes 100000 | tf_op jit(solution)/shard_map/pieces/pallas_call | solution.py:164
  (89 shorter events, 45.8 us)
Async XLA Ops:
  0.0 26.4 %collective-permute-start = (bf16[512,1024]{1,0:T(8,128)(2,1)}, bf16[512,1024]{1,0:T(8,128)(2,1)S(1)}, u32[]{:S(2)}, u32[]{:S(2)}) collective-permute-start(bf16[512,1024]{1,0:T(8,128)(2,1)} %refs_0_.1), channel_id=1, source_target_pairs={{0,4},{2,6},{4,0},{6,2},{8,12},{10,14},{12,8},{14,10},{1,5},{3,7},... | collective-permute-start | bytes 3145736 | tf_op jit(solution)/shard_map/ppermute | solution.py:216
  3.0 25.0 %collective-permute-start.3 = (bf16[512,1024]{1,0:T(8,128)(2,1)}, bf16[512,1024]{1,0:T(8,128)(2,1)S(1)}, u32[]{:S(2)}, u32[]{:S(2)}) collective-permute-start(bf16[512,1024]{1,0:T(8,128)(2,1)} %refs_0_.1), channel_id=1, source_target_pairs={{4,8},{6,10},{8,4},{10,6},{5,9},{7,11},{9,5},{11,7},{20,24},{22,26... | collective-permute-start | bytes 3145736 | tf_op jit(solution)/shard_map/ppermute | solution.py:216
  3.7 25.6 %collective-permute-start.1 = (bf16[512,1024]{1,0:T(8,128)(2,1)}, bf16[512,1024]{1,0:T(8,128)(2,1)S(1)}, u32[]{:S(2)}, u32[]{:S(2)}) collective-permute-start(bf16[512,1024]{1,0:T(8,128)(2,1)} %refs_0_.1), channel_id=1, source_target_pairs={{0,2},{2,0},{4,6},{6,4},{8,10},{10,8},{12,14},{14,12},{1,3},{3,1},... | collective-permute-start | bytes 3145736 | tf_op jit(solution)/shard_map/ppermute | solution.py:227
  26.4 21.1 %collective-permute-start.5 = (bf16[512,1024]{1,0:T(8,128)(2,1)S(1)}, bf16[512,1024]{1,0:T(8,128)(2,1)}, u32[]{:S(2)}, u32[]{:S(2)}) collective-permute-start(bf16[512,1024]{1,0:T(8,128)(2,1)S(1)} %collective-permute-done.refs_1_), channel_id=1, source_target_pairs={{4,8},{6,10},{8,4},{10,6},{5,9},{7,11},{9,5},{11,7},{20,24},{22,26... | collective-permute-start | bytes 3145736 | tf_op jit(solution)/shard_map/ppermute | solution.py:216
  28.0 27.3 %collective-permute-start.4 = (bf16[512,1024]{1,0:T(8,128)(2,1)S(1)}, bf16[512,1024]{1,0:T(8,128)(2,1)}, u32[]{:S(2)}, u32[]{:S(2)}) collective-permute-start(bf16[512,1024]{1,0:T(8,128)(2,1)S(1)} %collective-permute-done.3.refs_2_), channel_id=1, source_target_pairs={{4,0},{6,2},{8,12},{10,14},{5,1},{7,3},{9,13},{11,15},{20,16},{22,... | collective-permute-start | bytes 3145736 | tf_op jit(solution)/shard_map/ppermute | solution.py:216
  29.3 27.4 %collective-permute-start.2 = (bf16[512,1024]{1,0:T(8,128)(2,1)S(1)}, bf16[512,1024]{1,0:T(8,128)(2,1)}, u32[]{:S(2)}, u32[]{:S(2)}) collective-permute-start(bf16[512,1024]{1,0:T(8,128)(2,1)S(1)} %collective-permute-done.refs_1_), channel_id=1, source_target_pairs={{0,2},{2,0},{4,6},{6,4},{8,10},{10,8},{12,14},{14,12},{1,3},{3,1},... | collective-permute-start | bytes 3145736 | tf_op jit(solution)/shard_map/ppermute | solution.py:227
  47.5 29.9 %collective-permute-start.7 = (bf16[512,1024]{1,0:T(8,128)(2,1)}, bf16[512,1024]{1,0:T(8,128)(2,1)S(1)}, u32[]{:S(2)}, u32[]{:S(2)}) collective-permute-start(bf16[512,1024]{1,0:T(8,128)(2,1)} %collective-permute-done.5), channel_id=1, source_target_pairs={{4,0},{6,2},{8,12},{10,14},{5,1},{7,3},{9,13},{11,15},{20,16},{22,... | collective-permute-start | bytes 3145736 | tf_op jit(solution)/shard_map/ppermute | solution.py:216
  56.7 22.8 %collective-permute-start.6 = (bf16[512,1024]{1,0:T(8,128)(2,1)S(1)}, bf16[512,1024]{1,0:T(8,128)(2,1)S(1)}, u32[]{:S(2)}, u32[]{:S(2)}) collective-permute-start(bf16[512,1024]{1,0:T(8,128)(2,1)S(1)} %broadcast_select_fusion.refs_1_), channel_id=1, source_target_pairs={{0,2},{2,0},{4,6},{6,4},{8,10},{10,8},{12,14},{14,12},{1,3},{3,1},... | collective-permute-start | bytes 3145736 | tf_op jit(solution)/shard_map/ppermute | solution.py:227
  58.3 37.3 %collective-permute-start.10 = (bf16[512,512]{1,0:T(8,128)(2,1)S(1)}, bf16[512,512]{1,0:T(8,128)(2,1)S(1)}, u32[]{:S(2)}, u32[]{:S(2)}) collective-permute-start(bf16[512,512]{1,0:T(8,128)(2,1)S(1)} %slice.27), channel_id=1, source_target_pairs={{4,8},{6,10},{8,4},{10,6},{5,9},{7,11},{9,5},{11,7},{20,24},{22,26... | collective-permute-start | bytes 1572872 | tf_op jit(solution)/shard_map/ppermute | solution.py:216
  79.6 16.0 %collective-permute-start.9 = (bf16[512,512]{1,0:T(8,128)(2,1)S(1)}, bf16[512,512]{1,0:T(8,128)(2,1)S(1)}, u32[]{:S(2)}, u32[]{:S(2)}) collective-permute-start(bf16[512,512]{1,0:T(8,128)(2,1)S(1)} %slice.26), channel_id=1, source_target_pairs={{4,0},{6,2},{8,12},{10,14},{5,1},{7,3},{9,13},{11,15},{20,16},{22,... | collective-permute-start | bytes 1572872 | tf_op jit(solution)/shard_map/ppermute | solution.py:216
  80.9 14.7 %collective-permute-start.8 = (bf16[512,512]{1,0:T(8,128)(2,1)S(1)}, bf16[512,512]{1,0:T(8,128)(2,1)S(1)}, u32[]{:S(2)}, u32[]{:S(2)}) collective-permute-start(bf16[512,512]{1,0:T(8,128)(2,1)S(1)} %slice_select_fusion), channel_id=1, source_target_pairs={{0,2},{2,0},{4,6},{6,4},{8,10},{10,8},{12,14},{14,12},{1,3},{3,1},... | collective-permute-start | bytes 1572872 | tf_op jit(solution)/shard_map/ppermute | solution.py:227
  105.1 12.2 %collective-permute-start.11 = (f32[3,8,1024]{2,1,0:T(8,128)S(1)}, f32[3,8,1024]{2,1,0:T(8,128)S(1)}, u32[]{:S(2)}, u32[]{:S(2)}) collective-permute-start(f32[3,8,1024]{2,1,0:T(8,128)S(1)} %get-tuple-element.77), channel_id=1, source_target_pairs={{0,1},{2,3},{4,5},{6,7},{8,9},{10,11},{12,13},{14,15},{16,17},{18,... | collective-permute-start | bytes 294920 | tf_op jit(solution)/shard_map/ppermute | solution.py:19
  120.0 2.2 collective-permute-start.12
  127.8 15.0 %collective-permute-start.13 = (bf16[256,1024]{1,0:T(8,128)(2,1)S(1)}, bf16[256,1024]{1,0:T(8,128)(2,1)S(1)}, u32[]{:S(2)}, u32[]{:S(2)}) collective-permute-start(bf16[256,1024]{1,0:T(8,128)(2,1)S(1)} %pieces.10.refs_0_), channel_id=1, source_target_pairs={{0,2},{2,0},{4,6},{6,4},{8,10},{10,8},{12,14},{14,12},{1,3},{3,1},... | collective-permute-start | bytes 1572872 | tf_op jit(solution)/shard_map/ppermute | solution.py:227
  134.4 16.9 %collective-permute-start.14 = (bf16[256,1024]{1,0:T(8,128)(2,1)S(1)}, bf16[256,1024]{1,0:T(8,128)(2,1)S(1)}, u32[]{:S(2)}, u32[]{:S(2)}) collective-permute-start(bf16[256,1024]{1,0:T(8,128)(2,1)S(1)} %pieces.12.refs_0_), channel_id=1, source_target_pairs={{0,4},{2,6},{12,8},{14,10},{1,5},{3,7},{13,9},{15,11},{16,20},{18,... | collective-permute-start | bytes 1572872 | tf_op jit(solution)/shard_map/ppermute | solution.py:216
  142.9 19.6 %collective-permute-start.17 = (bf16[256,1024]{1,0:T(8,128)(2,1)S(1)}, bf16[256,1024]{1,0:T(8,128)(2,1)S(1)}, u32[]{:S(2)}, u32[]{:S(2)}) collective-permute-start(bf16[256,1024]{1,0:T(8,128)(2,1)S(1)} %add_convert_fusion.7), channel_id=1, source_target_pairs={{0,4},{2,6},{12,8},{14,10},{1,5},{3,7},{13,9},{15,11},{16,20},{18,... | collective-permute-start | bytes 1572872 | tf_op jit(solution)/shard_map/ppermute | solution.py:216
  146.8 15.8 %collective-permute-start.16 = (bf16[256,1024]{1,0:T(8,128)(2,1)S(1)}, bf16[256,1024]{1,0:T(8,128)(2,1)S(1)}, u32[]{:S(2)}, u32[]{:S(2)}) collective-permute-start(bf16[256,1024]{1,0:T(8,128)(2,1)S(1)} %get-tuple-element.94), channel_id=1, source_target_pairs={{0,2},{2,0},{4,6},{6,4},{8,10},{10,8},{12,14},{14,12},{1,3},{3,1},... | collective-permute-start | bytes 1572872 | tf_op jit(solution)/shard_map/ppermute | solution.py:227
  151.5 23.2 %collective-permute-start.15 = (bf16[256,1024]{1,0:T(8,128)(2,1)S(1)}, bf16[256,1024]{1,0:T(8,128)(2,1)S(1)}, u32[]{:S(2)}, u32[]{:S(2)}) collective-permute-start(bf16[256,1024]{1,0:T(8,128)(2,1)S(1)} %add_convert_fusion.8), channel_id=1, source_target_pairs={{0,2},{2,0},{4,6},{6,4},{8,10},{10,8},{12,14},{14,12},{1,3},{3,1},... | collective-permute-start | bytes 1572872 | tf_op jit(solution)/shard_map/ppermute | solution.py:227
  153.1 23.2 %collective-permute-start.24 = (bf16[256,1024]{1,0:T(8,128)(2,1)S(1)}, bf16[256,1024]{1,0:T(8,128)(2,1)S(1)}, u32[]{:S(2)}, u32[]{:S(2)}) collective-permute-start(bf16[256,1024]{1,0:T(8,128)(2,1)S(1)} %get-tuple-element.91.refs_0_), channel_id=1, source_target_pairs={{0,4},{2,6},{12,8},{14,10},{1,5},{3,7},{13,9},{15,11},{16,20},{18,... | collective-permute-start | bytes 1572872 | tf_op jit(solution)/shard_map/ppermute | solution.py:216
  157.7 24.5 %collective-permute-start.25 = (bf16[256,1024]{1,0:T(8,128)(2,1)S(1)}, bf16[256,1024]{1,0:T(8,128)(2,1)S(1)}, u32[]{:S(2)}, u32[]{:S(2)}) collective-permute-start(bf16[256,1024]{1,0:T(8,128)(2,1)S(1)} %pieces.12.refs_0_), channel_id=1, source_target_pairs={{4,8},{6,10},{8,4},{10,6},{5,9},{7,11},{9,5},{11,7},{20,24},{22,26... | collective-permute-start | bytes 1572872 | tf_op jit(solution)/shard_map/ppermute | solution.py:216
  162.8 28.0 %collective-permute-start.21 = (bf16[256,1024]{1,0:T(8,128)(2,1)S(1)}, bf16[256,1024]{1,0:T(8,128)(2,1)S(1)}, u32[]{:S(2)}, u32[]{:S(2)}) collective-permute-start(bf16[256,1024]{1,0:T(8,128)(2,1)S(1)} %add_convert_fusion.6), channel_id=1, source_target_pairs={{4,8},{6,10},{8,4},{10,6},{5,9},{7,11},{9,5},{11,7},{20,24},{22,26... | collective-permute-start | bytes 1572872 | tf_op jit(solution)/shard_map/ppermute | solution.py:216
  163.5 21.5 %collective-permute-start.18 = (bf16[256,1024]{1,0:T(8,128)(2,1)S(1)}, bf16[256,1024]{1,0:T(8,128)(2,1)S(1)}, u32[]{:S(2)}, u32[]{:S(2)}) collective-permute-start(bf16[256,1024]{1,0:T(8,128)(2,1)S(1)} %add_convert_fusion.6), channel_id=1, source_target_pairs={{0,4},{2,6},{12,8},{14,10},{1,5},{3,7},{13,9},{15,11},{16,20},{18,... | collective-permute-start | bytes 1572872 | tf_op jit(solution)/shard_map/ppermute | solution.py:216
  174.7 15.5 %collective-permute-start.19 = (bf16[256,1024]{1,0:T(8,128)(2,1)S(1)}, bf16[256,1024]{1,0:T(8,128)(2,1)S(1)}, u32[]{:S(2)}, u32[]{:S(2)}) collective-permute-start(bf16[256,1024]{1,0:T(8,128)(2,1)S(1)} %get-tuple-element.98), channel_id=1, source_target_pairs={{0,2},{2,0},{4,6},{6,4},{8,10},{10,8},{12,14},{14,12},{1,3},{3,1},... | collective-permute-start | bytes 1572872 | tf_op jit(solution)/shard_map/ppermute | solution.py:227
  176.6 19.7 %collective-permute-start.30 = (bf16[256,1024]{1,0:T(8,128)(2,1)S(1)}, bf16[256,1024]{1,0:T(8,128)(2,1)S(1)}, u32[]{:S(2)}, u32[]{:S(2)}) collective-permute-start(bf16[256,1024]{1,0:T(8,128)(2,1)S(1)} %add_convert_fusion.3.refs_0_), channel_id=1, source_target_pairs={{0,4},{2,6},{12,8},{14,10},{1,5},{3,7},{13,9},{15,11},{16,20},{18,... | collective-permute-start | bytes 1572872 | tf_op jit(solution)/shard_map/ppermute | solution.py:216
  182.1 18.4 %collective-permute-start.28 = (bf16[256,1024]{1,0:T(8,128)(2,1)S(1)}, bf16[256,1024]{1,0:T(8,128)(2,1)S(1)}, u32[]{:S(2)}, u32[]{:S(2)}) collective-permute-start(bf16[256,1024]{1,0:T(8,128)(2,1)S(1)} %add_convert_fusion.3.refs_0_), channel_id=1, source_target_pairs={{4,8},{6,10},{8,4},{10,6},{5,9},{7,11},{9,5},{11,7},{20,24},{22,26... | collective-permute-start | bytes 1572872 | tf_op jit(solution)/shard_map/ppermute | solution.py:216
  185.0 14.9 %collective-permute-start.26 = (bf16[256,1024]{1,0:T(8,128)(2,1)S(1)}, bf16[256,1024]{1,0:T(8,128)(2,1)S(1)}, u32[]{:S(2)}, u32[]{:S(2)}) collective-permute-start(bf16[256,1024]{1,0:T(8,128)(2,1)S(1)} %get-tuple-element.104), channel_id=1, source_target_pairs={{0,2},{2,0},{4,6},{6,4},{8,10},{10,8},{12,14},{14,12},{1,3},{3,1},... | collective-permute-start | bytes 1572872 | tf_op jit(solution)/shard_map/ppermute | solution.py:227
  190.2 20.9 %collective-permute-start.20 = (bf16[256,1024]{1,0:T(8,128)(2,1)S(1)}, bf16[256,1024]{1,0:T(8,128)(2,1)S(1)}, u32[]{:S(2)}, u32[]{:S(2)}) collective-permute-start(bf16[256,1024]{1,0:T(8,128)(2,1)S(1)} %get-tuple-element.99), channel_id=1, source_target_pairs={{0,2},{2,0},{4,6},{6,4},{8,10},{10,8},{12,14},{14,12},{1,3},{3,1},... | collective-permute-start | bytes 1572872 | tf_op jit(solution)/shard_map/ppermute | solution.py:227
  191.0 28.7 %collective-permute-start.22 = (bf16[256,1024]{1,0:T(8,128)(2,1)S(1)}, bf16[256,1024]{1,0:T(8,128)(2,1)S(1)}, u32[]{:S(2)}, u32[]{:S(2)}) collective-permute-start(bf16[256,1024]{1,0:T(8,128)(2,1)S(1)} %add_convert_fusion.5), channel_id=1, source_target_pairs={{0,4},{2,6},{4,0},{6,2},{8,12},{10,14},{12,8},{14,10},{1,5},{3,7},... | collective-permute-start | bytes 1572872 | tf_op jit(solution)/shard_map/ppermute | solution.py:216
  196.2 23.5 %collective-permute-start.23 = (bf16[256,1024]{1,0:T(8,128)(2,1)S(1)}, bf16[256,1024]{1,0:T(8,128)(2,1)S(1)}, u32[]{:S(2)}, u32[]{:S(2)}) collective-permute-start(bf16[256,1024]{1,0:T(8,128)(2,1)S(1)} %add_convert_fusion.4), channel_id=1, source_target_pairs={{4,8},{6,10},{8,4},{10,6},{5,9},{7,11},{9,5},{11,7},{20,24},{22,26... | collective-permute-start | bytes 1572872 | tf_op jit(solution)/shard_map/ppermute | solution.py:216
  199.9 19.9 %collective-permute-start.31 = (bf16[256,1024]{1,0:T(8,128)(2,1)S(1)}, bf16[256,1024]{1,0:T(8,128)(2,1)S(1)}, u32[]{:S(2)}, u32[]{:S(2)}) collective-permute-start(bf16[256,1024]{1,0:T(8,128)(2,1)S(1)} %add_convert_fusion), channel_id=1, source_target_pairs={{4,8},{6,10},{8,4},{10,6},{5,9},{7,11},{9,5},{11,7},{20,24},{22,26... | collective-permute-start | bytes 1572872 | tf_op jit(solution)/shard_map/ppermute | solution.py:216
  200.6 19.5 %collective-permute-start.27 = (bf16[256,1024]{1,0:T(8,128)(2,1)S(1)}, bf16[256,1024]{1,0:T(8,128)(2,1)S(1)}, u32[]{:S(2)}, u32[]{:S(2)}) collective-permute-start(bf16[256,1024]{1,0:T(8,128)(2,1)S(1)} %add_convert_fusion.2), channel_id=1, source_target_pairs={{0,2},{2,0},{4,6},{6,4},{8,10},{10,8},{12,14},{14,12},{1,3},{3,1},... | collective-permute-start | bytes 1572872 | tf_op jit(solution)/shard_map/ppermute | solution.py:227
  211.1 9.6 %collective-permute-start.29 = (bf16[256,1024]{1,0:T(8,128)(2,1)S(1)}, bf16[256,1024]{1,0:T(8,128)(2,1)S(1)}, u32[]{:S(2)}, u32[]{:S(2)}) collective-permute-start(bf16[256,1024]{1,0:T(8,128)(2,1)S(1)} %add_convert_fusion.1), channel_id=1, source_target_pairs={{0,4},{2,6},{4,0},{6,2},{8,12},{10,14},{12,8},{14,10},{1,5},{3,7},... | collective-permute-start | bytes 1572872 | tf_op jit(solution)/shard_map/ppermute | solution.py:216
  (9 other events, 98.7 us)
